TPU v7x, 128 devices: a whole 4x4x4 slice. The times are simulated.
128 devices in a mesh: blk: 128 (over x, y, z, core).
Axes of the slice: x: 4, y: 4, z: 4, core: 2. Of those that a mesh axis runs over, the one named last changes fastest.
Arguments:
- source_points: bfloat16 [49152, 256], P('blk')
- target_points: bfloat16 [131072, 256], P('blk')
- source_mass: float32 [49152], P('blk'), may hold values from 0.25 to 4
- target_mass: float32 [131072], P('blk'), may hold values from 0.25 to 4
- target_init: float32 [131072], P('blk'), may hold values from -1.8 to 1.8
- pair_tiles: int32 [16384, 2], P('blk'), may hold values from 0 to 7, as said below
- pair_count: int32 [16384], P('blk'), may hold values from 0 to 2, as said below
Outputs:
- source_pot: float32 [49152], P('blk')
- target_pot: float32 [131072], P('blk')
Inputs may be any that keep to these rules, and one draw needn't show every extreme that they name: `pair_tiles`: the entries of a row are distinct; entries past the row's count are padding, still tile numbers below 8. Every target tile is named by a valid entry of some row, and every source device has a valid entry in some row. `pair_count`: some rows hold 2 valid entries in every draw.
All inputs are finite; a program needn't handle non-finite values.
Results may differ from a plain program's by a relative error of at most 0.0003.
Values may be sent and summed in bfloat16 or wider, within the bound.
No kernel may reach another device: no remote copies, remote signals or barrier semaphores. Data moves between devices by JAX's collectives and lax.ppermute only.
A program may use at most 192 MiB of HBM per device.

v0:
```python
import jax
import jax.numpy as jnp
from jax import lax
from jax.sharding import PartitionSpec as P

TSUB = 8
CAP = 2
ITERS = 2


EPSILON = 0.1


def combine_pairs(got_max, got_sum, asked_ids):
    picked = (asked_ids[:, :, None] == jnp.arange(TSUB, dtype=jnp.int32)[None, None, :])[..., None]
    top_col = jnp.max(jnp.where(picked, got_max[:, :, None, :], -jnp.inf), axis=(0, 1))
    col_total = jnp.sum(
        jnp.where(
            picked,
            got_sum[:, :, None, :] * jnp.exp(got_max[:, :, None, :] - top_col[None, None]),
            0.0,
        ),
        axis=(0, 1),
    )
    return (top_col, col_total)


def column_parts(col_max, col_sum, asked_ids):
    got_max, got_sum = (
        lax.all_to_all(col_max, "blk", split_axis=0, concat_axis=0, tiled=True),
        lax.all_to_all(col_sum, "blk", split_axis=0, concat_axis=0, tiled=True),
    )
    return combine_pairs(got_max, got_sum, asked_ids)


def body(
    source_points, target_points, source_mass, target_mass, target_init, pair_tiles, pair_count
):
    peer_count = lax.axis_size("blk")
    src_rows, feat_width = source_points.shape
    tile_rows = target_points.shape[0] // TSUB
    tiles_here = target_points.reshape(TSUB, tile_rows, feat_width)
    asked_ids, asked_count = (
        lax.all_to_all(pair_tiles, "blk", split_axis=0, concat_axis=0, tiled=True),
        lax.all_to_all(pair_count, "blk", split_axis=0, concat_axis=0, tiled=True),
    )
    slot_valid = jnp.arange(CAP, dtype=jnp.int32)[None, :] < pair_count[:, None]
    log_source = jnp.log(source_mass)
    log_target = jnp.log(target_mass).reshape(TSUB, tile_rows)
    target_pot = target_init.reshape(TSUB, tile_rows)
    source_pot = jnp.zeros((src_rows,), jnp.float32)
    source_norm = jnp.sum(jnp.square(source_points.astype(jnp.float32)), axis=-1)
    outgoing = tiles_here[asked_ids].reshape(peer_count, CAP * tile_rows, feat_width)
    piece_rows = lax.all_to_all(outgoing, "blk", split_axis=0, concat_axis=0, tiled=True)
    tile_norm = jnp.sum(jnp.square(piece_rows.astype(jnp.float32)), axis=-1)
    cross_term = jnp.einsum(
        "sd,nkd->snk", source_points, piece_rows, preferred_element_type=jnp.float32
    )
    cost_tile = (source_norm[:, None, None] + tile_norm[None] - 2.0 * cross_term) / feat_width
    cost_tile = cost_tile.reshape(src_rows, peer_count * CAP, tile_rows)
    flat_valid = slot_valid.reshape(-1)
    for iteration in range(ITERS):
        g_slots = lax.all_to_all(
            target_pot[asked_ids], "blk", split_axis=0, concat_axis=0, tiled=True
        )
        g_slots = g_slots.reshape(peer_count * CAP, tile_rows)
        scores = jnp.where(
            flat_valid[None, :, None], (g_slots[None] - cost_tile) / EPSILON, -jnp.inf
        )
        row_max = jnp.max(scores, axis=(1, 2))
        row_sum = jnp.sum(jnp.exp(scores - row_max[:, None, None]), axis=(1, 2))
        source_pot = EPSILON * log_source - EPSILON * (row_max + jnp.log(row_sum))
        col_score = (source_pot[:, None, None] - cost_tile) / EPSILON
        col_max = jnp.max(col_score, axis=0)
        col_sum = jnp.sum(jnp.exp(col_score - col_max[None]), axis=0)
        col_max = jnp.where(flat_valid[:, None], col_max, -jnp.inf)
        col_sum = jnp.where(flat_valid[:, None], col_sum, 0.0)
        top_col, col_total = column_parts(
            col_max.reshape(peer_count, CAP, tile_rows),
            col_sum.reshape(peer_count, CAP, tile_rows),
            asked_ids,
        )
        target_pot = EPSILON * log_target - EPSILON * (top_col + jnp.log(col_total))
    return (source_pot, target_pot.reshape(-1))


def solution(mesh):
    placed = (
        P("blk", None),
        P("blk", None),
        P("blk"),
        P("blk"),
        P("blk"),
        P("blk", None),
        P("blk"),
    )
    return jax.shard_map(
        body, mesh=mesh, in_specs=placed, out_specs=(P("blk"), P("blk")), check_vma=False
    )
```

profile of v0, /device:TPU:1, one launch (start us, length us, event | category | flops | bytes accessed | tf_op | source)
XLA Modules:
  0.0 528.3 jit_solution(13646776008927532983)
XLA Ops:
  0.7 0.9 copy.30
  1.5 20.7 %all_to_all.47 = s32[128,1,2]{2,1,0:T(1,128)S(1)} all-to-all(s32[128,1,2]{2,1,0:T(1,128)S(1)} %bitcast.53), channel_id=1, replica_groups=mesh['blk'=128] {'blk'}, dimensions={0} | all-to-all | bytes 2048 | tf_op jit(solution)/shard_map/all_to_all | solution.py:44
  22.3 2.0 gather_fusion
  24.4 4.8 all-to-all-start.1
  29.1 9.7 %gather_fusion.1 = bf16[256,128,256]{2,1,0:T(8,128)(2,1)} fusion(bf16[8,128,256]{2,1,0:T(8,128)(2,1)S(1)} %bitcast.37, s32[1024]{0:T(1024)S(1)} %pad_clamp_fusion), kind=kCustom, calls=%fused_computation.1 | custom fusion | bytes 33555456 | tf_op jit(solution)/shard_map/gather | solution.py:53
  38.9 10.1 %all-to-all-start.2 = ((bf16[128,256,256]{2,1,0:T(8,128)(2,1)}), bf16[128,256,256]{2,1,0:T(8,128)(2,1)}, u32[]{:S(2)}, u32[]{:S(2)}) async-start(bf16[128,256,256]{2,1,0:T(8,128)(2,1)} %bitcast.39), calls=%async_computation.2 | async-start | bytes 33554432 | tf_op jit(solution)/shard_map/all_to_all | solution.py:54
  49.4 226.5 %all-to-all-done.2 = bf16[128,256,256]{2,1,0:T(8,128)(2,1)} async-done(((bf16[128,256,256]{2,1,0:T(8,128)(2,1)}), bf16[128,256,256]{2,1,0:T(8,128)(2,1)}, u32[]{:S(2)}, u32[]{:S(2)}) %all-to-all-start.2) | async-done | bytes 16777248 | tf_op jit(solution)/shard_map/all_to_all | solution.py:54
  275.9 7.6 %multiply_reduce_fusion = f32[128,256]{1,0:T(8,128)S(1)} fusion(bf16[128,256,256]{2,1,0:T(8,128)(2,1)} %all-to-all-done.2), kind=kLoop, calls=%fused_computation.17 | loop fusion | flops 25133056 | bytes 16908288 | tf_op jit(solution)/shard_map/reduce_sum | solution.py:55
  283.5 23.1 %fusion.3 = (f32[384]{0:T(512)S(1)}, f32[384,128,256]{0,2,1:T(8,128)}) fusion(f32[128,256]{1,0:T(8,128)S(1)} %bitcast.44, pred[128,256]{1,0:T(8,128)(4,1)S(1)} %copy.29, bf16[128,256,256]{2,1,0:T(8,128)(2,1)} %all-to-all-done.2, bf16[384,256]{1,0:T(8,128)(2,1)S(1)} %copy-done.2, f32[128,256]{1,0:T(8,128)S(1)} %multiply_reduce_fusion, ...), kind=kOutput, calls=%fused_computation.15 | convolution fusion | flops 6543113728 | bytes 67603456 | tf_op jit(solution)/shard_map/sd,nkd->snk/dot_general | solution.py:56
  306.6 17.2 %exponential_reduce_fusion.3 = f32[384]{0:T(512)S(1)} fusion(f32[384,128,256]{0,2,1:T(8,128)} %get-tuple-element.7, f32[384]{0:T(512)S(1)} %get-tuple-element.6, f32[128,256]{1,0:T(8,128)S(1)} %bitcast.45, pred[128,256]{1,0:T(8,128)(4,1)S(1)} %copy.29), kind=kLoop, calls=%fused_computation.11 | loop fusion | flops 62914176 | bytes 50498560 | tf_op jit(solution)/shard_map/reduce_sum | solution.py:71
  323.8 22.4 %fusion.1 = f32[128,256]{1,0:T(8,128)S(1)} fusion(f32[384,128,256]{0,2,1:T(8,128)} %get-tuple-element.7, f32[384]{0:T(512)S(1)} %multiply_subtract_fusion.1), kind=kLoop, calls=%fused_computation.13 | loop fusion | flops 37715968 | bytes 50464256 | tf_op jit(solution)/shard_map/reduce_max | solution.py:74
  346.2 16.9 %exponential_reduce_fusion.2 = f32[128,256]{1,0:T(8,128)S(1)} fusion(f32[384,128,256]{0,2,1:T(8,128)} %get-tuple-element.7, f32[128,256]{1,0:T(8,128)S(1)} %fusion.1, f32[384]{0:T(512)S(1)} %multiply_subtract_fusion.1), kind=kLoop, calls=%fused_computation.9 | loop fusion | flops 50298880 | bytes 50595328 | tf_op jit(solution)/shard_map/reduce_sum | solution.py:75
  363.3 0.7 copy.32
  364.1 21.5 %all-to-all-start.3 = ((f32[128,2,128]{2,1,0:T(2,128)}), f32[128,2,128]{2,1,0:T(2,128)S(1)}, u32[]{:S(2)}, u32[]{:S(2)}) async-start(f32[128,2,128]{2,1,0:T(2,128)} %copy.32), calls=%async_computation.3 | async-start | bytes 262144 | tf_op jit(solution)/shard_map/all_to_all | solution.py:30
  385.8 0.7 copy.34
  386.5 8.8 %all-to-all-done.3 = f32[128,2,128]{2,1,0:T(2,128)S(1)} async-done(((f32[128,2,128]{2,1,0:T(2,128)}), f32[128,2,128]{2,1,0:T(2,128)S(1)}, u32[]{:S(2)}, u32[]{:S(2)}) %all-to-all-start.3) | async-done | bytes 131104 | tf_op jit(solution)/shard_map/all_to_all | solution.py:30
  395.3 4.5 all-to-all-start.4
  400.1 9.4 %all-to-all-done.4 = f32[128,2,128]{2,1,0:T(2,128)S(1)} async-done(((f32[128,2,128]{2,1,0:T(2,128)}), f32[128,2,128]{2,1,0:T(2,128)S(1)}, u32[]{:S(2)}, u32[]{:S(2)}) %all-to-all-start.4) | async-done | bytes 131104 | tf_op jit(solution)/shard_map/all_to_all | solution.py:31
  409.5 0.4 select_reduce_fusion.2
  410.0 0.7 gather_fusion.2
  410.7 14.3 %all_to_all.48 = f32[128,2,128]{2,1,0:T(2,128)S(1)} all-to-all(f32[128,2,128]{2,1,0:T(2,128)S(1)} %bitcast.50), channel_id=1, replica_groups=mesh['blk'=128] {'blk'}, dimensions={0} | all-to-all | bytes 262144 | tf_op jit(solution)/shard_map/all_to_all | solution.py:63
  425.0 16.3 %fusion.4 = f32[384]{0:T(512)S(1)} fusion(f32[384,128,256]{0,2,1:T(8,128)} %get-tuple-element.7, f32[128,256]{1,0:T(8,128)S(1)} %bitcast.40, pred[128,256]{1,0:T(8,128)(4,1)S(1)} %copy.29), kind=kLoop, calls=%fused_computation.16 | loop fusion | flops 50331264 | bytes 50497024 | tf_op jit(solution)/shard_map/reduce_max | solution.py:70
  441.2 17.2 %exponential_reduce_fusion.1 = f32[384]{0:T(512)S(1)} fusion(f32[384,128,256]{0,2,1:T(8,128)} %get-tuple-element.7, f32[384]{0:T(512)S(1)} %fusion.4, f32[128,256]{1,0:T(8,128)S(1)} %bitcast.41, pred[128,256]{1,0:T(8,128)(4,1)S(1)} %copy.29), kind=kLoop, calls=%fused_computation.7 | loop fusion | flops 62914176 | bytes 50498560 | tf_op jit(solution)/shard_map/reduce_sum | solution.py:71
  458.4 22.4 %fusion.2 = f32[128,256]{1,0:T(8,128)S(1)} fusion(f32[384,128,256]{0,2,1:T(8,128)} %get-tuple-element.7, f32[384]{0:T(512)S(1)} %multiply_subtract_fusion), kind=kLoop, calls=%fused_computation.14 | loop fusion | flops 37715968 | bytes 50464256 | tf_op jit(solution)/shard_map/reduce_max | solution.py:74
  480.9 16.9 %exponential_reduce_fusion = f32[128,256]{1,0:T(8,128)S(1)} fusion(f32[384,128,256]{0,2,1:T(8,128)} %get-tuple-element.7, f32[128,256]{1,0:T(8,128)S(1)} %fusion.2, f32[384]{0:T(512)S(1)} %multiply_subtract_fusion), kind=kLoop, calls=%fused_computation.5 | loop fusion | flops 50298880 | bytes 50595328 | tf_op jit(solution)/shard_map/reduce_sum | solution.py:75
  498.0 0.7 copy.36
  498.8 4.5 all-to-all-start.6
  503.3 0.8 copy.38
  504.0 9.0 %all-to-all-done.6 = f32[128,2,128]{2,1,0:T(2,128)S(1)} async-done(((f32[128,2,128]{2,1,0:T(2,128)}), f32[128,2,128]{2,1,0:T(2,128)S(1)}, u32[]{:S(2)}, u32[]{:S(2)}) %all-to-all-start.6) | async-done | bytes 131104 | tf_op jit(solution)/shard_map/all_to_all | solution.py:30
  513.1 4.5 all-to-all-start.7
  517.9 9.4 %all-to-all-done.7 = f32[128,2,128]{2,1,0:T(2,128)S(1)} async-done(((f32[128,2,128]{2,1,0:T(2,128)}), f32[128,2,128]{2,1,0:T(2,128)S(1)}, u32[]{:S(2)}, u32[]{:S(2)}) %all-to-all-start.7) | async-done | bytes 131104 | tf_op jit(solution)/shard_map/all_to_all | solution.py:31
  527.7 0.6 bitcast_subtract_fusion.1
  (37 shorter events, 2.3 us)
Async XLA Ops:
  0.6 28.5 %copy-start = (bf16[1024,256]{1,0:T(8,128)(2,1)S(1)}, bf16[1024,256]{1,0:T(8,128)(2,1)}, u32[]{:S(2)}) copy-start(bf16[1024,256]{1,0:T(8,128)(2,1)} %param.8) | copy-start | bytes 1572868
  0.6 48.4 %copy-start.6 = (s32[128]{0:T(128)S(1)}, s32[128]{0:T(128)}, u32[]{:S(2)}) copy-start(s32[128]{0:T(128)} %param.13) | copy-start | bytes 1540
  0.7 48.5 %copy-start.2 = (bf16[384,256]{1,0:T(8,128)(2,1)S(1)}, bf16[384,256]{1,0:T(8,128)(2,1)}, u32[]{:S(2)}) copy-start(bf16[384,256]{1,0:T(8,128)(2,1)} %param.7) | copy-start | bytes 589828
  24.4 14.5 %all-to-all-start.1 = ((f32[128,2,128]{2,1,0:T(2,128)}), f32[128,2,128]{2,1,0:T(2,128)S(1)}, u32[]{:S(2)}, u32[]{:S(2)}) async-start(f32[128,2,128]{2,1,0:T(2,128)} %bitcast.6), calls=%async_computation.1 | async-start | bytes 262144 | tf_op jit(solution)/shard_map/all_to_all | solution.py:63
  38.9 237.0 %all-to-all-start.2 = ((bf16[128,256,256]{2,1,0:T(8,128)(2,1)}), bf16[128,256,256]{2,1,0:T(8,128)(2,1)}, u32[]{:S(2)}, u32[]{:S(2)}) async-start(bf16[128,256,256]{2,1,0:T(8,128)(2,1)} %bitcast.39), calls=%async_computation.2 | async-start | bytes 33554432 | tf_op jit(solution)/shard_map/all_to_all | solution.py:54
  306.6 17.2 %copy-start.5 = (f32[384]{0:T(512)S(1)}, f32[384]{0:T(512)}, u32[]{:S(2)}) copy-start(f32[384]{0:T(512)} %param.9) | copy-start | bytes 4612
  323.8 86.2 %copy-start.4 = (f32[1024]{0:T(1024)S(1)}, f32[1024]{0:T(1024)}, u32[]{:S(2)}) copy-start(f32[1024]{0:T(1024)} %param.10) | copy-start | bytes 12292
  364.1 31.2 %all-to-all-start.3 = ((f32[128,2,128]{2,1,0:T(2,128)}), f32[128,2,128]{2,1,0:T(2,128)S(1)}, u32[]{:S(2)}, u32[]{:S(2)}) async-start(f32[128,2,128]{2,1,0:T(2,128)} %copy.32), calls=%async_computation.3 | async-start | bytes 262144 | tf_op jit(solution)/shard_map/all_to_all | solution.py:30
  395.3 14.2 %all-to-all-start.4 = ((f32[128,2,128]{2,1,0:T(2,128)}), f32[128,2,128]{2,1,0:T(2,128)S(1)}, u32[]{:S(2)}, u32[]{:S(2)}) async-start(f32[128,2,128]{2,1,0:T(2,128)} %copy.34), calls=%async_computation.4 | async-start | bytes 262144 | tf_op jit(solution)/shard_map/all_to_all | solution.py:31
  458.4 69.9 %copy-start.1 = (bf16[1024,256]{1,0:T(8,128)(2,1)S(1)}, bf16[1024,256]{1,0:T(8,128)(2,1)}, u32[]{:S(2)}) copy-start(bf16[1024,256]{1,0:T(8,128)(2,1)} %param.8) | copy-start | bytes 1572868
  458.4 39.4 %copy-start.3 = (f32[384]{0:T(512)}, f32[384]{0:T(512)S(1)}, u32[]{:S(2)}) copy-start(f32[384]{0:T(512)S(1)} %multiply_subtract_fusion) | copy-start | bytes 4612
  498.8 14.3 %all-to-all-start.6 = ((f32[128,2,128]{2,1,0:T(2,128)}), f32[128,2,128]{2,1,0:T(2,128)S(1)}, u32[]{:S(2)}, u32[]{:S(2)}) async-start(f32[128,2,128]{2,1,0:T(2,128)} %copy.36), calls=%async_computation.6 | async-start | bytes 262144 | tf_op jit(solution)/shard_map/all_to_all | solution.py:30
  513.1 14.2 %all-to-all-start.7 = ((f32[128,2,128]{2,1,0:T(2,128)}), f32[128,2,128]{2,1,0:T(2,128)S(1)}, u32[]{:S(2)}, u32[]{:S(2)}) async-start(f32[128,2,128]{2,1,0:T(2,128)} %copy.38), calls=%async_computation.7 | async-start | bytes 262144 | tf_op jit(solution)/shard_map/all_to_all | solution.py:31
where the time goes:
time: 529 us; the launch traced here: 528 us
  waiting for transfers between devices  263 us (50%)
  other arithmetic  139 us (26%)
  starting transfers between devices  49.8 us (9%)
  blocking collectives  34.9 us (7%)
  matrix products  23.1 us (4%)
  local copies, waits for them, and re-layouts  17 us (3%)
    all_to_all x1, waiting for transfers between devices, body(): lax.all_to_all(outgoing, 'blk', split_axis=0, concat_axis=0, tiled=True)  227 us
    reduce_max x2, other arithmetic, body(): col_max = jnp.max(col_score, axis=0)  44.8 us
    reduce_sum x2, other arithmetic, body(): row_sum = jnp.sum(jnp.exp(scores - row_max[:, None, None]), axis=(1, 2))  34.4 us
    reduce_sum x2, other arithmetic, body(): col_sum = jnp.sum(jnp.exp(col_score - col_max[None]), axis=0)  33.8 us
    all_to_all x2, starting transfers between devices, column_parts(): lax.all_to_all(col_max, 'blk', split_axis=0, concat_axis=0, tiled=True)  26 us
    dot_general x1, matrix products, body(): jnp.einsum('sd,nkd->snk', source_points, piece_rows, preferred_element_ty...  23.1 us
    all_to_all x1, blocking collectives, body(): lax.all_to_all(pair_tiles, 'blk', split_axis=0, concat_axis=0, tiled=True)  20.7 us
    all_to_all x2, waiting for transfers between devices, column_parts(): lax.all_to_all(col_sum, 'blk', split_axis=0, concat_axis=0, tiled=True)  18.8 us
  transfers between devices with their start and end apart: 6, of which 6 were waited for; matrix products, arithmetic and copies ran while one was open for 2% of the time, Pallas kernels for 0%

commit v1 on v0

v1 whole, which is shorter than its diff:
```python
import functools

import jax
import jax.numpy as jnp
from jax import lax
from jax.experimental import pallas as pl
from jax.experimental.pallas import tpu as pltpu
from jax.sharding import Mesh
from jax.sharding import PartitionSpec as P

TSUB = 8
CAP = 2
ITERS = 2
EPSILON = 0.1

DIMS = (4, 4, 4, 2)
NAMES = ("x", "y", "z", "core")
ROWS = ("y", "z")
COLS = ("x", "core")
N_ROWS = 16
N_COLS = 8
SRC = 384
TILE = 128
SUBS = SRC // TILE
FEAT = 256
TILES = N_COLS * TSUB
ITEMS = N_ROWS * N_COLS
UNROLL = 2
HALF = SRC // 2
RING = 4
GAIN = 2.0 / (FEAT * EPSILON)
SPAN = 70.0


def lse_over_first(parts):
    top = jnp.max(parts, axis=0)
    base = jnp.where(top == -jnp.inf, 0.0, top)
    return top + jnp.log(jnp.sum(jnp.exp(parts - base[None]), axis=0))


def spread(values, norm_ref):
    high, low = jnp.max(values), jnp.min(values)
    reach = GAIN * jnp.sqrt(jnp.max(norm_ref[0:8]) * jnp.max(norm_ref[8:16]))
    return 0.5 * high + 0.5 * low, 0.5 * high - 0.5 * low + reach <= SPAN


def diagonal():
    return lax.broadcasted_iota(jnp.int32, (TILE, TILE), 0) == lax.broadcasted_iota(
        jnp.int32, (TILE, TILE), 1
    )


def products(x, y):
    return GAIN * jnp.dot(x, y, preferred_element_type=jnp.float32)


def item_at(item_ref, w):
    return tuple(item_ref[8 + 8 * w + k] for k in range(7))


def exps(xa_ref, xb_ref, y_ref, ia, ib, r0, r1):
    x = jnp.concatenate([xa_ref[ia], xb_ref[ib]], axis=0)
    return jnp.exp(products(x, jnp.concatenate([y_ref[r0], y_ref[r1]], axis=1)))


def rescale(old, new):
    return jnp.where(old == new, 1.0, jnp.exp(old - new))


def row_kernel(
    combine, item_ref, xa_ref, xb_ref, y_ref, norm_ref, a_ref, lb_ref, out_ref, a_buf, u_buf, acc, top
):
    if combine:
        a = lb_ref[...] - lse_over_first(a_ref[...])
    else:
        a = a_ref[...]
    mid, fast = spread(a, norm_ref)
    n_items = item_ref[0]
    eye = diagonal()

    acc[...] = jnp.zeros_like(acc)

    @pl.when(fast)
    def _():
        u_buf[0:TILES] = jnp.exp(a - mid)
        u_buf[TILES:] = jnp.zeros((8, TILE), jnp.float32)

        def step(w, _):
            for h in range(UNROLL):
                s, ia, ib, t0, t1, r0, r1 = item_at(item_ref, UNROLL * w + h)
                e = exps(xa_ref, xb_ref, y_ref, ia, ib, r0, r1)
                acc[s] += (
                    e[:, :TILE] * u_buf[pl.ds(t0, 1), :] + e[:, TILE:] * u_buf[pl.ds(t1, 1), :]
                )
            return 0

        lax.fori_loop(0, lax.div(n_items + UNROLL - 1, UNROLL), step, 0)
        for k in range(N_ROWS * SUBS):
            s, b = k // SUBS, k % SUBS
            col = jnp.sum(acc[s, b * TILE : (b + 1) * TILE, :], axis=1, keepdims=True)
            done = mid + jnp.log(jnp.sum(jnp.where(eye, col, 0.0), axis=0, keepdims=True))
            out_ref[:, k : k + 1, :] = jnp.broadcast_to(done[None], (N_ROWS, 1, TILE))

    @pl.when(jnp.logical_not(fast))
    def _():
        a_buf[0:TILES] = a
        a_buf[TILES:] = jnp.zeros((8, TILE), jnp.float32)
        top[...] = jnp.full_like(top, -jnp.inf)

        def step(w, _):
            s, ia, ib, t0, t1, r0, r1 = item_at(item_ref, w)
            for t, r in ((t0, r0), (t1, r1)):

                @pl.when(t < TILES)
                def _(t=t, r=r):
                    x = jnp.concatenate([xa_ref[ia], xb_ref[ib]], axis=0)
                    score = products(x, y_ref[r]) + a_buf[pl.ds(t, 1), :]
                    old = top[s]
                    new = jnp.maximum(old, score)
                    acc[s] = acc[s] * rescale(old, new) + jnp.exp(score - new)
                    top[s] = new

            return 0

        lax.fori_loop(0, n_items, step, 0)

        def finish(k, _):
            s, b = lax.div(k, SUBS), lax.rem(k, SUBS)
            rows = pl.ds(pl.multiple_of(b * TILE, TILE), TILE)
            block = top[s, rows, :]
            high = jnp.max(block, axis=1, keepdims=True)
            base = jnp.where(high == -jnp.inf, 0.0, high)
            total = jnp.sum(acc[s, rows, :] * jnp.exp(block - base), axis=1, keepdims=True)
            high_row = jnp.max(jnp.where(eye, high, -jnp.inf), axis=0, keepdims=True)
            total_row = jnp.sum(jnp.where(eye, total, 0.0), axis=0, keepdims=True)
            done = high_row + jnp.log(total_row)
            out_ref[:, pl.ds(k, 1), :] = jnp.broadcast_to(done[None], (N_ROWS, 1, TILE))
            return 0

        lax.fori_loop(0, N_ROWS * SUBS, finish, 0)


def col_kernel(
    item_ref, xa_ref, xb_ref, y_ref, norm_ref, parts_ref, la_ref, out_ref, b_ref, spread_buf, acc, top
):
    b = la_ref[...] - lse_over_first(parts_ref[...])
    b_ref[...] = b
    mid, fast = spread(b, norm_ref)
    n_items = item_ref[0]
    eye = diagonal()

    def lay_out(values):
        for k in range(N_ROWS * SUBS):
            s, part = k // SUBS, k % SUBS
            row = values[k : k + 1, :]
            col = jnp.sum(jnp.where(eye, row, 0.0), axis=1, keepdims=True)
            spread_buf[s, part * TILE : (part + 1) * TILE, :] = jnp.broadcast_to(col, (TILE, TILE))

    acc[...] = jnp.zeros_like(acc)

    @pl.when(fast)
    def _():
        lay_out(jnp.exp(b - mid))

        def step(w, _):
            for h in range(UNROLL):
                s, ia, ib, t0, t1, r0, r1 = item_at(item_ref, UNROLL * w + h)
                e = exps(xa_ref, xb_ref, y_ref, ia, ib, r0, r1)
                v = spread_buf[s]
                acc[t0] += jnp.sum((e[:, :TILE] * v).reshape(SRC // 8, 8, TILE), axis=0)
                acc[t1] += jnp.sum((e[:, TILE:] * v).reshape(SRC // 8, 8, TILE), axis=0)
            return 0

        lax.fori_loop(0, lax.div(n_items + UNROLL - 1, UNROLL), step, 0)
        done = mid + jnp.log(jnp.sum(acc[0:TILES], axis=1))
        out_ref[...] = jnp.broadcast_to(done[None], out_ref.shape)

    @pl.when(jnp.logical_not(fast))
    def _():
        lay_out(b)
        top[...] = jnp.full_like(top, -jnp.inf)

        def step(w, _):
            s, ia, ib, t0, t1, r0, r1 = item_at(item_ref, w)
            for t, r in ((t0, r0), (t1, r1)):

                @pl.when(t < TILES)
                def _(t=t, r=r):
                    x = jnp.concatenate([xa_ref[ia], xb_ref[ib]], axis=0)
                    score = products(x, y_ref[r]) + spread_buf[s]
                    score = score.reshape(SRC // 8, 8, TILE)
                    old = top[t]
                    new = jnp.maximum(old, jnp.max(score, axis=0))
                    acc[t] = acc[t] * rescale(old, new) + jnp.sum(
                        jnp.exp(score - new[None]), axis=0
                    )
                    top[t] = new

            return 0

        lax.fori_loop(0, n_items, step, 0)
        high = jnp.max(top[0:TILES], axis=1)
        base = jnp.where(high == -jnp.inf, 0.0, high)
        total = jnp.sum(acc[0:TILES] * jnp.exp(top[0:TILES] - base[:, None, :]), axis=1)
        out_ref[...] = jnp.broadcast_to((high + jnp.log(total))[None], out_ref.shape)


VMEM = pl.BlockSpec(memory_space=pltpu.VMEM)
SMEM = pl.BlockSpec(memory_space=pltpu.SMEM)
LIMIT = pltpu.CompilerParams(vmem_limit_bytes=40 * 1024 * 1024)


def row_pass(items, xa, xb, ys, norms, a, lb, combine):
    return pl.pallas_call(
        functools.partial(row_kernel, combine),
        out_shape=jax.ShapeDtypeStruct((N_ROWS, N_ROWS * SUBS, TILE), jnp.float32),
        in_specs=[SMEM] + [VMEM] * 6,
        out_specs=VMEM,
        scratch_shapes=[
            pltpu.VMEM((TILES + 8, TILE), jnp.float32),
            pltpu.VMEM((TILES + 8, TILE), jnp.float32),
            pltpu.VMEM((N_ROWS, SRC, TILE), jnp.float32),
            pltpu.VMEM((N_ROWS, SRC, TILE), jnp.float32),
        ],
        compiler_params=LIMIT,
        name="row_pass",
    )(items, xa, xb, ys, norms, a, lb)


def col_pass(items, xa, xb, ys, norms, parts, la, copies):
    return pl.pallas_call(
        col_kernel,
        out_shape=(
            jax.ShapeDtypeStruct((copies, TILES, TILE), jnp.float32),
            jax.ShapeDtypeStruct((N_ROWS * SUBS, TILE), jnp.float32),
        ),
        in_specs=[SMEM] + [VMEM] * 6,
        out_specs=(VMEM, VMEM),
        scratch_shapes=[
            pltpu.VMEM((N_ROWS, SRC, TILE), jnp.float32),
            pltpu.VMEM((TILES + 1, 8, TILE), jnp.float32),
            pltpu.VMEM((TILES + 1, 8, TILE), jnp.float32),
        ],
        compiler_params=LIMIT,
        name="col_pass",
    )(items, xa, xb, ys, norms, parts, la)


def swap(blocks, axes):
    return lax.all_to_all(blocks, axes, split_axis=0, concat_axis=0, tiled=True)


def fetch(block, axis, ahead):
    size = 2 if axis == "core" else RING
    return lax.ppermute(block, axis, [((k + ahead) % size, k) for k in range(size)])


def gather_ring(block, axis):
    return [block] + [fetch(block, axis, ahead) for ahead in range(1, RING)]


def gather_sources(points):
    first, second = points[:HALF], points[HALF:]
    first = jnp.concatenate(gather_ring(first, "y"))
    second = jnp.concatenate(gather_ring(second, "z"))
    first = jnp.concatenate(gather_ring(first, "z")).reshape(N_ROWS, HALF, FEAT)
    second = jnp.concatenate(gather_ring(second, "y")).reshape(N_ROWS, HALF, FEAT)
    return first, second


def gather_targets(points):
    near = gather_ring(points, "x")
    far = [fetch(block, "core", 1) for block in near]
    return jnp.concatenate(near + far)


def work_items(ids, counts):
    slot = jnp.arange(CAP, dtype=jnp.int32)
    valid = (slot[None, None, :] < counts[:, :, None]).reshape(N_ROWS, N_COLS * CAP)
    tile = (ids + TSUB * jnp.arange(N_COLS, dtype=jnp.int32)[None, :, None]).reshape(
        N_ROWS, N_COLS * CAP
    )
    place = jnp.cumsum(valid.astype(jnp.int32), axis=1) - 1
    filled = jnp.sum(valid.astype(jnp.int32), axis=1)
    width = (filled + 1) // 2
    start = jnp.cumsum(width) - width
    total = jnp.sum(width)
    position = 2 * start[:, None] + place
    room = ITEMS + 8
    want = jnp.arange(2 * room, dtype=jnp.int32)
    hit = valid[None] & (position[None] == want[:, None, None])
    tiles = TILES + jnp.sum(jnp.where(hit, tile[None] - TILES, 0), axis=(1, 2))
    order = jnp.arange(room, dtype=jnp.int32)
    block = jnp.sum((order[:, None] >= (start + width)[None, :]).astype(jnp.int32), axis=1)
    block = jnp.minimum(block, N_ROWS - 1)
    along = {name: lax.axis_index(name) for name in NAMES}
    ky, kz = (block // RING - along["y"]) % RING, (block % RING - along["z"]) % RING
    owner, sub = tiles % TILES // TSUB, tiles % TSUB
    kx, kc = (owner // 2 - along["x"]) % RING, (owner % 2 - along["core"]) % 2
    held = ((kc * RING + kx) * TSUB + sub).reshape(room, 2)
    tiles = tiles.reshape(room, 2)
    listed = jnp.concatenate(
        [jnp.stack([block, kz * RING + ky, ky * RING + kz], axis=1), tiles, held, held[:, :1]],
        axis=1,
    ).reshape(-1)
    return jnp.concatenate([jnp.full((8,), total, jnp.int32), listed.astype(jnp.int32)])


def body(
    source_points, target_points, source_mass, target_mass, target_init, pair_tiles, pair_count
):
    unit = 1.0 / (FEAT * EPSILON)
    source_norm = jnp.sum(jnp.square(source_points.astype(jnp.float32)), axis=-1)
    target_norm = jnp.sum(jnp.square(target_points.astype(jnp.float32)), axis=-1)
    log_source = jnp.log(source_mass)
    log_target = jnp.log(target_mass)

    asked = jnp.concatenate([pair_tiles, pair_count[:, None]], axis=1).reshape(*DIMS, CAP + 1)
    asked = asked.transpose(1, 2, 0, 3, 4).reshape(N_ROWS, N_COLS * (CAP + 1))
    own = jnp.concatenate([log_source, jnp.full((8,), jnp.max(source_norm))])
    sent = jnp.concatenate(
        [asked.astype(jnp.float32), jnp.broadcast_to(own[None], (N_ROWS, SRC + 8))], axis=1
    )
    got = swap(sent, ROWS)
    wide = N_COLS * (CAP + 1)
    pairs = got[:, :wide].astype(jnp.int32).reshape(N_ROWS, N_COLS, CAP + 1)
    la = got[:, wide : wide + SRC].reshape(N_ROWS * SUBS, TILE)
    items = work_items(pairs[:, :, :CAP], pairs[:, :, CAP])

    first = jnp.concatenate(
        [
            target_init / EPSILON - target_norm * unit,
            log_target,
            jnp.full((TILE,), jnp.max(target_norm)),
        ]
    )
    firsts = swap(jnp.broadcast_to(first[None], (N_COLS,) + first.shape), COLS)
    n_targets = TSUB * TILE
    a0 = firsts[:, :n_targets].reshape(TILES, TILE)
    lb = firsts[:, n_targets : 2 * n_targets].reshape(TILES, TILE)
    norms = jnp.concatenate(
        [
            jnp.full((8, TILE), jnp.max(got[:, wide + SRC :])),
            jnp.full((8, TILE), jnp.max(firsts[:, 2 * n_targets :])),
        ]
    )

    ys = gather_targets(target_points.reshape(TSUB, TILE, FEAT).transpose(0, 2, 1))
    xa, xb = gather_sources(source_points)
    held = (items, xa, xb, ys, norms)

    row_parts = row_pass(*held, a0, lb, False)
    for iteration in range(ITERS):
        final = iteration == ITERS - 1
        col_parts, b = col_pass(*held, swap(row_parts, ROWS), la, 1 if final else N_COLS)
        if not final:
            row_parts = row_pass(*held, swap(col_parts, COLS), lb, True)
    here = lax.axis_index(ROWS)
    b_here = lax.dynamic_slice_in_dim(b, here * SUBS, SUBS).reshape(SRC)
    source_pot = EPSILON * (b_here + source_norm * unit)
    last = swap(col_parts.reshape(N_COLS, n_targets), COLS)
    target_pot = EPSILON * (log_target - lse_over_first(last) + target_norm * unit)
    return (source_pot, target_pot)


def solution(mesh):
    grid = Mesh(mesh.devices.reshape(DIMS), NAMES)
    placed = (
        P(NAMES, None),
        P(NAMES, None),
        P(NAMES),
        P(NAMES),
        P(NAMES),
        P(NAMES, None),
        P(NAMES),
    )
    return jax.shard_map(
        body, mesh=grid, in_specs=placed, out_specs=(P(NAMES), P(NAMES)), check_vma=False
    )
```

time: 529 us -> 344 us (0.65)
  waiting for transfers between devices: 263 us -> 39.1 us
  Pallas kernels: 0 us -> 170 us
  other arithmetic: 139 us -> 12.9 us
  matrix products: 23.1 us -> 0 us
  blocking collectives: 34.9 us -> 12.3 us
  local copies, waits for them, and re-layouts: 17 us -> 36.8 us
  starting transfers between devices: 49.8 us -> 66.2 us
    all_to_all x6 -> x5, waiting for transfers between devices: 263 us -> 16.8 us  [swap(): return lax.all_to_all(blocks, axes, split_axis=0, concat_axis=0, tiled=True)]
    pallas_call x0 -> x4, Pallas kernels: none -> 170 us  [the longest x2 90.4 us: row_pass(): pl.pallas_call(functools.partial(row_kernel, combine), out_shape=jax.Shap...]
    reduce_sum x7 -> x6, other arithmetic: 76.6 us -> 2.3 us  [the longest x1 1.25 us: body(): jnp.sum(jnp.square(target_points.astype(jnp.float32)), axis=-1)]
    reduce_max x5 -> x4, other arithmetic: 61.7 us -> 2.73 us  [the longest x1 1.43 us: body(): jnp.max(got[:, wide + SRC:])]
    ppermute x0 -> x19, starting transfers between devices: none -> 29.6 us  [fetch(): lax.ppermute(block, axis, [((k + ahead) % size, k) for k in range(size)])]
    dot_general x1 -> x0, matrix products: 23.1 us -> none  [body(): jnp.einsum('sd,nkd->snk', source_points, piece_rows, preferred_element_ty...]
    all_to_all x2 -> x1, blocking collectives: 34.9 us -> 12.3 us  [swap(): return lax.all_to_all(blocks, axes, split_axis=0, concat_axis=0, tiled=True)]
    ppermute x0 -> x19, waiting for transfers between devices: none -> 22.3 us  [fetch(): lax.ppermute(block, axis, [((k + ahead) % size, k) for k in range(size)])]
  transfers between devices with their start and end apart: 6 -> 24, of which waited for: 6 -> 8; matrix products, arithmetic and copies ran while one was open for 2% -> 10% of each run, Pallas kernels for 0% -> 0%
where the time goes in v1:
time: 344 us; the launch traced here: 339 us
  Pallas kernels  170 us (49%)
  starting transfers between devices  66.2 us (19%)
  waiting for transfers between devices  39.1 us (11%)
  local copies, waits for them, and re-layouts  36.8 us (11%)
  other arithmetic  12.9 us (4%)
  blocking collectives  12.3 us (4%)
    pallas_call x2, Pallas kernels, row_pass(): pl.pallas_call(functools.partial(row_kernel, combine), out_shape=jax.Shap...  90.4 us
    pallas_call x2, Pallas kernels, col_pass(): pl.pallas_call(col_kernel, out_shape=(jax.ShapeDtypeStruct((copies, TILES...  79.9 us
    all_to_all x5, starting transfers between devices, swap(): return lax.all_to_all(blocks, axes, split_axis=0, concat_axis=0, tiled=True)  36.7 us
    ppermute x19, starting transfers between devices, fetch(): lax.ppermute(block, axis, [((k + ahead) % size, k) for k in range(size)])  29.6 us
    ppermute x19, waiting for transfers between devices, fetch(): lax.ppermute(block, axis, [((k + ahead) % size, k) for k in range(size)])  22.3 us
    unnamed x55, local copies, waits for them, and re-layouts  18.9 us
    all_to_all x5, waiting for transfers between devices, swap(): return lax.all_to_all(blocks, axes, split_axis=0, concat_axis=0, tiled=True)  16.8 us
    all_to_all x1, blocking collectives, swap(): return lax.all_to_all(blocks, axes, split_axis=0, concat_axis=0, tiled=True)  12.3 us
  transfers between devices with their start and end apart: 24, of which 8 were waited for; matrix products, arithmetic and copies ran while one was open for 10% of the time, Pallas kernels for 0%

profile of v1, /device:TPU:1, one launch (start us, length us, event | category | flops | bytes accessed | tf_op | source)
XLA Modules:
  0.0 338.9 jit_solution(2961745947364110521)
XLA Ops:
  1.6 4.7 %collective-permute-start.6 = (bf16[192,256]{1,0:T(8,128)(2,1)S(1)}, bf16[192,256]{1,0:T(8,128)(2,1)}, u32[]{:S(2)}, u32[]{:S(2)}) collective-permute-start(bf16[192,256]{1,0:T(8,128)(2,1)S(1)} %get-tuple-element.15), channel_id=1, source_target_pairs={{2,0},{4,2},{6,4},{0,6},{3,1},{5,3},{7,5},{1,7},{10,8},{12,10},{14... | collective-permute-start | bytes 294920 | tf_op jit(solution)/shard_map/ppermute | solution.py:255
  7.0 2.7 collective-permute-start
  16.1 6.0 %all-to-all-start = ((f32[16,1,416]{2,1,0:T(1,128)}), f32[16,1,416]{2,1,0:T(1,128)S(1)}, u32[]{:S(2)}, u32[]{:S(2)}) async-start(f32[16,1,416]{2,1,0:T(1,128)} %all_to_all.31), calls=%async_computation | async-start | bytes 65536 | tf_op jit(solution)/shard_map/all_to_all | solution.py:250
  23.4 2.1 copy.45
  25.5 1.9 constant_dynamic-update-slice_fusion.21
  29.5 7.3 %all-to-all-start.1 = ((f32[8,1,2176]{2,1,0:T(1,128)}), f32[8,1,2176]{2,1,0:T(1,128)}, u32[]{:S(2)}, u32[]{:S(2)}) async-start(f32[8,1,2176]{2,1,0:T(1,128)} %broadcast_in_dim.28), calls=%async_computation.1 | async-start | bytes 139264 | tf_op jit(solution)/shard_map/all_to_all | solution.py:250
  41.5 1.7 concatenate.50
  44.9 1.4 slice_reduce_fusion
  50.0 2.6 collective-permute-start.12
  53.6 2.0 collective-permute-start.9
  57.9 2.5 collective-permute-start.3
  67.2 9.4 %collective-permute-done.11 = bf16[768,256]{1,0:T(8,128)(2,1)S(1)} collective-permute-done((bf16[768,256]{1,0:T(8,128)(2,1)S(1)}, bf16[768,256]{1,0:T(8,128)(2,1)S(1)}, u32[]{:S(2)}, u32[]{:S(2)}) %collective-permute-start.11) | collective-permute-done | bytes 393248 | tf_op jit(solution)/shard_map/ppermute | solution.py:255
  77.6 6.7 %collective-permute-start.15 = (bf16[8,256,128]{2,1,0:T(8,128)(2,1)S(1)}, bf16[8,256,128]{2,1,0:T(8,128)(2,1)S(1)}, u32[]{:S(2)}, u32[]{:S(2)}) collective-permute-start(bf16[8,256,128]{2,1,0:T(8,128)(2,1)S(1)} %bitcast.54), channel_id=1, source_target_pairs={{1,0},{0,1},{3,2},{2,3},{5,4},{4,5},{7,6},{6,7},{9,8},{8,9},{11,10... | collective-permute-start | bytes 1572872 | tf_op jit(solution)/shard_map/ppermute | solution.py:255
  84.3 6.2 %collective-permute-done.5 = bf16[768,256]{1,0:T(8,128)(2,1)S(1)} collective-permute-done((bf16[768,256]{1,0:T(8,128)(2,1)S(1)}, bf16[768,256]{1,0:T(8,128)(2,1)S(1)}, u32[]{:S(2)}, u32[]{:S(2)}) %collective-permute-start.5) | collective-permute-done | bytes 393248 | tf_op jit(solution)/shard_map/ppermute | solution.py:255
  90.6 1.6 collective-permute-start.17
  92.3 5.0 %collective-permute-done.14 = bf16[8,256,128]{2,1,0:T(8,128)(2,1)S(1)} collective-permute-done((bf16[8,256,128]{2,1,0:T(8,128)(2,1)S(1)}, bf16[8,256,128]{2,1,0:T(8,128)(2,1)S(1)}, u32[]{:S(2)}, u32[]{:S(2)}) %collective-permute-start.14) | collective-permute-done | bytes 524320 | tf_op jit(solution)/shard_map/ppermute | solution.py:255
  100.0 45.3 %row_pass.2 = f32[16,48,128]{2,1,0:T(8,128)S(1)} custom-call(s32[1096]{0:T(1024)S(1)} %concatenate.51.item_ref, bf16[16,192,256]{2,1,0:T(8,128)(2,1)S(1)} %bitcast.41, bf16[16,192,256]{2,1,0:T(8,128)(2,1)S(1)} %bitcast.45, bf16[64,256,128]{2,1,0:T(8,128)(2,1)S(1)} %constant_dynamic-update-slice_fusion.14.y_ref, f32[16,128]{1,0:T(8,128)S(1)} %concatenate.59.norm_ref, ...), custom_call_target="tpu_custom_call" | custom-call | tf_op jit(solution)/shard_map/row_pass/pallas_call | solution.py:214
  145.3 1.9 copy-done.1
  148.0 8.6 %all-to-all-start.2 = ((f32[16,48,128]{2,1,0:T(8,128)}), f32[16,48,128]{2,1,0:T(8,128)S(1)}, u32[]{:S(2)}, u32[]{:S(2)}) async-start(f32[16,48,128]{2,1,0:T(8,128)} %copy-done.5), calls=%async_computation.2 | async-start | bytes 786432 | tf_op jit(solution)/shard_map/all_to_all | solution.py:250
  156.6 1.4 slice.52
  158.0 1.3 reshape.391.la_ref
  159.4 5.4 %all-to-all-done.2.parts_ref = f32[16,48,128]{2,1,0:T(8,128)S(1)} async-done(((f32[16,48,128]{2,1,0:T(8,128)}), f32[16,48,128]{2,1,0:T(8,128)S(1)}, u32[]{:S(2)}, u32[]{:S(2)}) %all-to-all-start.2) | async-done | bytes 393248 | tf_op jit(solution)/shard_map/all_to_all | solution.py:250
  164.8 2.2 copy-done.2
  167.7 40.3 %col_pass.2 = (f32[8,64,128]{2,1,0:T(8,128)S(1)}, f32[48,128]{1,0:T(8,128)}) custom-call(s32[1096]{0:T(1024)S(1)} %concatenate.51.item_ref, bf16[16,192,256]{2,1,0:T(8,128)(2,1)S(1)} %bitcast.42, bf16[16,192,256]{2,1,0:T(8,128)(2,1)S(1)} %bitcast.46, bf16[64,256,128]{2,1,0:T(8,128)(2,1)S(1)} %copy-done.2, f32[16,128]{1,0:T(8,128)S(1)} %concatenate.59.norm_ref, ...), custom_call_target="tpu_custom_call" | custom-call | tf_op jit(solution)/shard_map/col_pass/pallas_call | solution.py:231
  208.0 12.3 %all_to_all.48.a_ref = f32[8,64,128]{2,1,0:T(8,128)S(1)} all-to-all(f32[8,64,128]{2,1,0:T(8,128)S(1)} %get-tuple-element.5), channel_id=1, replica_groups=mesh['x'=4,'y'=4,'z'=4,'core'=2] {'x','core'}, dimensions={0} | all-to-all | bytes 524288 | tf_op jit(solution)/shard_map/all_to_all | solution.py:250
  220.3 45.1 %row_pass.3 = f32[16,48,128]{2,1,0:T(8,128)S(1)} custom-call(s32[1096]{0:T(1024)S(1)} %concatenate.51.item_ref, bf16[16,192,256]{2,1,0:T(8,128)(2,1)S(1)} %bitcast.43, bf16[16,192,256]{2,1,0:T(8,128)(2,1)S(1)} %bitcast.47, bf16[64,256,128]{2,1,0:T(8,128)(2,1)S(1)} %copy-done.2, f32[16,128]{1,0:T(8,128)S(1)} %concatenate.59.norm_ref, ...), custom_call_target="tpu_custom_call" | custom-call | tf_op jit(solution)/shard_map/row_pass/pallas_call | solution.py:214
  266.2 7.4 %all-to-all-start.4 = ((f32[16,48,128]{2,1,0:T(8,128)}), f32[16,48,128]{2,1,0:T(8,128)S(1)}, u32[]{:S(2)}, u32[]{:S(2)}) async-start(f32[16,48,128]{2,1,0:T(8,128)} %copy-done.4), calls=%async_computation.4 | async-start | bytes 786432 | tf_op jit(solution)/shard_map/all_to_all | solution.py:250
  273.6 8.0 %all-to-all-done.4.parts_ref = f32[16,48,128]{2,1,0:T(8,128)S(1)} async-done(((f32[16,48,128]{2,1,0:T(8,128)}), f32[16,48,128]{2,1,0:T(8,128)S(1)}, u32[]{:S(2)}, u32[]{:S(2)}) %all-to-all-start.4) | async-done | bytes 393248 | tf_op jit(solution)/shard_map/all_to_all | solution.py:250
  281.6 2.2 copy-done.3
  284.5 39.7 %col_pass.3 = (f32[1,64,128]{2,1,0:T(8,128)S(1)}, f32[48,128]{1,0:T(8,128)S(1)}) custom-call(s32[1096]{0:T(1024)S(1)} %concatenate.51.item_ref, bf16[16,192,256]{2,1,0:T(8,128)(2,1)S(1)} %bitcast.44, bf16[16,192,256]{2,1,0:T(8,128)(2,1)S(1)} %bitcast.48, bf16[64,256,128]{2,1,0:T(8,128)(2,1)S(1)} %copy-done.3, f32[16,128]{1,0:T(8,128)S(1)} %concatenate.59.norm_ref, ...), custom_call_target="tpu_custom_call" | custom-call | tf_op jit(solution)/shard_map/col_pass/pallas_call | solution.py:231
  325.4 7.4 %all-to-all-start.5 = ((f32[8,1,1024]{2,1,0:T(1,128)}), f32[8,1,1024]{2,1,0:T(1,128)S(1)}, u32[]{:S(2)}, u32[]{:S(2)}) async-start(f32[8,1,1024]{2,1,0:T(1,128)} %bitcast.49), calls=%async_computation.5 | async-start | bytes 65536 | tf_op jit(solution)/shard_map/all_to_all | solution.py:250
  334.1 3.4 %all-to-all-done.5 = f32[8,1,1024]{2,1,0:T(1,128)S(1)} async-done(((f32[8,1,1024]{2,1,0:T(1,128)}), f32[8,1,1024]{2,1,0:T(1,128)S(1)}, u32[]{:S(2)}, u32[]{:S(2)}) %all-to-all-start.5) | async-done | bytes 32800 | tf_op jit(solution)/shard_map/all_to_all | solution.py:250
  (151 shorter events, 42.1 us)
Async XLA Ops:
  1.6 47.6 %collective-permute-start.6 = (bf16[192,256]{1,0:T(8,128)(2,1)S(1)}, bf16[192,256]{1,0:T(8,128)(2,1)}, u32[]{:S(2)}, u32[]{:S(2)}) collective-permute-start(bf16[192,256]{1,0:T(8,128)(2,1)S(1)} %get-tuple-element.15), channel_id=1, source_target_pairs={{2,0},{4,2},{6,4},{0,6},{3,1},{5,3},{7,5},{1,7},{10,8},{12,10},{14... | collective-permute-start | bytes 294920 | tf_op jit(solution)/shard_map/ppermute | solution.py:255
  6.3 43.7 %collective-permute-start.7 = (bf16[192,256]{1,0:T(8,128)(2,1)S(1)}, bf16[192,256]{1,0:T(8,128)(2,1)}, u32[]{:S(2)}, u32[]{:S(2)}) collective-permute-start(bf16[192,256]{1,0:T(8,128)(2,1)S(1)} %get-tuple-element.15), channel_id=1, source_target_pairs={{4,0},{6,2},{0,4},{2,6},{5,1},{7,3},{1,5},{3,7},{12,8},{14,10},{8,... | collective-permute-start | bytes 294920 | tf_op jit(solution)/shard_map/ppermute | solution.py:255
  6.3 46.3 %collective-permute-start.8 = (bf16[192,256]{1,0:T(8,128)(2,1)S(1)}, bf16[192,256]{1,0:T(8,128)(2,1)}, u32[]{:S(2)}, u32[]{:S(2)}) collective-permute-start(bf16[192,256]{1,0:T(8,128)(2,1)S(1)} %get-tuple-element.15), channel_id=1, source_target_pairs={{6,0},{0,2},{2,4},{4,6},{7,1},{1,3},{3,5},{5,7},{14,8},{8,10},{10,... | collective-permute-start | bytes 294920 | tf_op jit(solution)/shard_map/ppermute | solution.py:255
  7.0 48.7 %collective-permute-start = (bf16[192,256]{1,0:T(8,128)(2,1)S(1)}, bf16[192,256]{1,0:T(8,128)(2,1)}, u32[]{:S(2)}, u32[]{:S(2)}) collective-permute-start(bf16[192,256]{1,0:T(8,128)(2,1)S(1)} %get-tuple-element.18), channel_id=1, source_target_pairs={{8,0},{16,8},{24,16},{0,24},{9,1},{17,9},{25,17},{1,25},{10,2},{18... | collective-permute-start | bytes 294920 | tf_op jit(solution)/shard_map/ppermute | solution.py:255
  9.7 47.0 %collective-permute-start.1 = (bf16[192,256]{1,0:T(8,128)(2,1)S(1)}, bf16[192,256]{1,0:T(8,128)(2,1)}, u32[]{:S(2)}, u32[]{:S(2)}) collective-permute-start(bf16[192,256]{1,0:T(8,128)(2,1)S(1)} %get-tuple-element.18), channel_id=1, source_target_pairs={{16,0},{24,8},{0,16},{8,24},{17,1},{25,9},{1,17},{9,25},{18,2},{26... | collective-permute-start | bytes 294920 | tf_op jit(solution)/shard_map/ppermute | solution.py:255
  11.1 16.2 %copy-start.15 = (f32[384]{0:T(512)}, f32[384]{0:T(512)S(1)}, u32[]{:S(2)}) copy-start(f32[384]{0:T(512)S(1)} %multiply_reduce_fusion.1) | copy-start | bytes 4612
  13.5 13.9 %copy-start.16 = (f32[1024]{0:T(1024)S(1)}, f32[1024]{0:T(1024)}, u32[]{:S(2)}) copy-start(f32[1024]{0:T(1024)} %param.10) | copy-start | bytes 12292
  13.5 13.8 %copy-start.17 = (f32[1024]{0:T(1024)S(1)}, f32[1024]{0:T(1024)}, u32[]{:S(2)}) copy-start(f32[1024]{0:T(1024)} %param.11) | copy-start | bytes 12292
  16.1 12.7 %all-to-all-start = ((f32[16,1,416]{2,1,0:T(1,128)}), f32[16,1,416]{2,1,0:T(1,128)S(1)}, u32[]{:S(2)}, u32[]{:S(2)}) async-start(f32[16,1,416]{2,1,0:T(1,128)} %all_to_all.31), calls=%async_computation | async-start | bytes 65536 | tf_op jit(solution)/shard_map/all_to_all | solution.py:250
  23.4 5.3 %copy-start.14 = (f32[1024]{0:T(1024)}, f32[1024]{0:T(1024)S(1)}, u32[]{:S(2)}) copy-start(f32[1024]{0:T(1024)S(1)} %multiply_reduce_fusion) | copy-start | bytes 12292
  29.5 16.8 %all-to-all-start.1 = ((f32[8,1,2176]{2,1,0:T(1,128)}), f32[8,1,2176]{2,1,0:T(1,128)}, u32[]{:S(2)}, u32[]{:S(2)}) async-start(f32[8,1,2176]{2,1,0:T(1,128)} %broadcast_in_dim.28), calls=%async_computation.1 | async-start | bytes 139264 | tf_op jit(solution)/shard_map/all_to_all | solution.py:250
  47.2 52.8 %copy-start.6 = (f32[64,128]{1,0:T(8,128)}, f32[64,128]{1,0:T(8,128)S(1)}, u32[]{:S(2)}) copy-start(f32[64,128]{1,0:T(8,128)S(1)} %reshape.390.lb_ref) | copy-start | bytes 98308
  49.2 7.8 %collective-permute-start.2 = (bf16[192,256]{1,0:T(8,128)(2,1)S(1)}, bf16[192,256]{1,0:T(8,128)(2,1)S(1)}, u32[]{:S(2)}, u32[]{:S(2)}) collective-permute-start(bf16[192,256]{1,0:T(8,128)(2,1)S(1)} %get-tuple-element.18), channel_id=1, source_target_pairs={{24,0},{0,8},{8,16},{16,24},{25,1},{1,9},{9,17},{17,25},{26,2},{2,... | collective-permute-start | bytes 294920 | tf_op jit(solution)/shard_map/ppermute | solution.py:255
  50.0 34.2 %collective-permute-start.12 = (bf16[8,256,128]{2,1,0:T(8,128)(2,1)}, bf16[8,256,128]{2,1,0:T(8,128)(2,1)S(1)}, u32[]{:S(2)}, u32[]{:S(2)}) collective-permute-start(bf16[8,256,128]{2,1,0:T(8,128)(2,1)} %bitcast.51), channel_id=1, source_target_pairs={{32,0},{64,32},{96,64},{0,96},{33,1},{65,33},{97,65},{1,97},{34,2}... | collective-permute-start | bytes 1572872 | tf_op jit(solution)/shard_map/ppermute | solution.py:255
  53.6 13.0 %copy-start.12 = (bf16[8,128,256]{1,2,0:T(8,128)(2,1)S(1)}, bf16[8,128,256]{1,2,0:T(8,128)(2,1)}, u32[]{:S(2)}) copy-start(bf16[8,128,256]{1,2,0:T(8,128)(2,1)} %copy.45) | copy-start | bytes 1572868
  53.6 11.3 %collective-permute-start.9 = (bf16[768,256]{1,0:T(8,128)(2,1)S(1)}, bf16[768,256]{1,0:T(8,128)(2,1)S(1)}, u32[]{:S(2)}, u32[]{:S(2)}) collective-permute-start(bf16[768,256]{1,0:T(8,128)(2,1)S(1)} %pad_maximum_fusion.1), channel_id=1, source_target_pairs={{8,0},{16,8},{24,16},{0,24},{9,1},{17,9},{25,17},{1,25},{10,2},{18... | collective-permute-start | bytes 1179656 | tf_op jit(solution)/shard_map/ppermute | solution.py:255
  55.7 11.0 %collective-permute-start.10 = (bf16[768,256]{1,0:T(8,128)(2,1)S(1)}, bf16[768,256]{1,0:T(8,128)(2,1)S(1)}, u32[]{:S(2)}, u32[]{:S(2)}) collective-permute-start(bf16[768,256]{1,0:T(8,128)(2,1)S(1)} %pad_maximum_fusion.1), channel_id=1, source_target_pairs={{16,0},{24,8},{0,16},{8,24},{17,1},{25,9},{1,17},{9,25},{18,2},{26... | collective-permute-start | bytes 1179656 | tf_op jit(solution)/shard_map/ppermute | solution.py:255
  56.7 19.9 %collective-permute-start.11 = (bf16[768,256]{1,0:T(8,128)(2,1)S(1)}, bf16[768,256]{1,0:T(8,128)(2,1)S(1)}, u32[]{:S(2)}, u32[]{:S(2)}) collective-permute-start(bf16[768,256]{1,0:T(8,128)(2,1)S(1)} %pad_maximum_fusion.1), channel_id=1, source_target_pairs={{24,0},{0,8},{8,16},{16,24},{25,1},{1,9},{9,17},{17,25},{26,2},{2,... | collective-permute-start | bytes 1179656 | tf_op jit(solution)/shard_map/ppermute | solution.py:255
  57.9 19.4 %collective-permute-start.3 = (bf16[768,256]{1,0:T(8,128)(2,1)S(1)}, bf16[768,256]{1,0:T(8,128)(2,1)S(1)}, u32[]{:S(2)}, u32[]{:S(2)}) collective-permute-start(bf16[768,256]{1,0:T(8,128)(2,1)S(1)} %pad_maximum_fusion), channel_id=1, source_target_pairs={{2,0},{4,2},{6,4},{0,6},{3,1},{5,3},{7,5},{1,7},{10,8},{12,10},{14... | collective-permute-start | bytes 1179656 | tf_op jit(solution)/shard_map/ppermute | solution.py:255
  64.9 12.6 %collective-permute-start.4 = (bf16[768,256]{1,0:T(8,128)(2,1)S(1)}, bf16[768,256]{1,0:T(8,128)(2,1)S(1)}, u32[]{:S(2)}, u32[]{:S(2)}) collective-permute-start(bf16[768,256]{1,0:T(8,128)(2,1)S(1)} %pad_maximum_fusion), channel_id=1, source_target_pairs={{4,0},{6,2},{0,4},{2,6},{5,1},{7,3},{1,5},{3,7},{12,8},{14,10},{8,... | collective-permute-start | bytes 1179656 | tf_op jit(solution)/shard_map/ppermute | solution.py:255
  66.1 26.1 %copy-start = (bf16[64,256,128]{2,1,0:T(8,128)(2,1)S(1)}, bf16[64,256,128]{2,1,0:T(8,128)(2,1)}, u32[]{:S(2)}) copy-start(bf16[64,256,128]{2,1,0:T(8,128)(2,1)} %constant_dynamic-update-slice_fusion.21) | copy-start | bytes 12582916
  66.6 23.9 %collective-permute-start.13 = (bf16[8,256,128]{2,1,0:T(8,128)(2,1)S(1)}, bf16[8,256,128]{2,1,0:T(8,128)(2,1)S(1)}, u32[]{:S(2)}, u32[]{:S(2)}) collective-permute-start(bf16[8,256,128]{2,1,0:T(8,128)(2,1)S(1)} %bitcast.52), channel_id=1, source_target_pairs={{64,0},{96,32},{0,64},{32,96},{65,1},{97,33},{1,65},{33,97},{66,2}... | collective-permute-start | bytes 1572872 | tf_op jit(solution)/shard_map/ppermute | solution.py:255
  76.6 13.9 %collective-permute-start.5 = (bf16[768,256]{1,0:T(8,128)(2,1)S(1)}, bf16[768,256]{1,0:T(8,128)(2,1)S(1)}, u32[]{:S(2)}, u32[]{:S(2)}) collective-permute-start(bf16[768,256]{1,0:T(8,128)(2,1)S(1)} %pad_maximum_fusion), channel_id=1, source_target_pairs={{6,0},{0,2},{2,4},{4,6},{7,1},{1,3},{3,5},{5,7},{14,8},{8,10},{10,... | collective-permute-start | bytes 1179656 | tf_op jit(solution)/shard_map/ppermute | solution.py:255
  77.4 19.9 %collective-permute-start.14 = (bf16[8,256,128]{2,1,0:T(8,128)(2,1)S(1)}, bf16[8,256,128]{2,1,0:T(8,128)(2,1)S(1)}, u32[]{:S(2)}, u32[]{:S(2)}) collective-permute-start(bf16[8,256,128]{2,1,0:T(8,128)(2,1)S(1)} %bitcast.53), channel_id=1, source_target_pairs={{96,0},{0,32},{32,64},{64,96},{97,1},{1,33},{33,65},{65,97},{98,2}... | collective-permute-start | bytes 1572872 | tf_op jit(solution)/shard_map/ppermute | solution.py:255
  77.6 20.9 %collective-permute-start.15 = (bf16[8,256,128]{2,1,0:T(8,128)(2,1)S(1)}, bf16[8,256,128]{2,1,0:T(8,128)(2,1)S(1)}, u32[]{:S(2)}, u32[]{:S(2)}) collective-permute-start(bf16[8,256,128]{2,1,0:T(8,128)(2,1)S(1)} %bitcast.54), channel_id=1, source_target_pairs={{1,0},{0,1},{3,2},{2,3},{5,4},{4,5},{7,6},{6,7},{9,8},{8,9},{11,10... | collective-permute-start | bytes 1572872 | tf_op jit(solution)/shard_map/ppermute | solution.py:255
  84.3 14.3 %collective-permute-start.16 = (bf16[8,256,128]{2,1,0:T(8,128)(2,1)S(1)}, bf16[8,256,128]{2,1,0:T(8,128)(2,1)S(1)}, u32[]{:S(2)}, u32[]{:S(2)}) collective-permute-start(bf16[8,256,128]{2,1,0:T(8,128)(2,1)S(1)} %collective-permute-done.12), channel_id=1, source_target_pairs={{1,0},{0,1},{3,2},{2,3},{5,4},{4,5},{7,6},{6,7},{9,8},{8,9},{11,10... | collective-permute-start | bytes 1572872 | tf_op jit(solution)/shard_map/ppermute | solution.py:255
  90.6 8.1 %collective-permute-start.17 = (bf16[8,256,128]{2,1,0:T(8,128)(2,1)S(1)}, bf16[8,256,128]{2,1,0:T(8,128)(2,1)S(1)}, u32[]{:S(2)}, u32[]{:S(2)}) collective-permute-start(bf16[8,256,128]{2,1,0:T(8,128)(2,1)S(1)} %collective-permute-done.13), channel_id=1, source_target_pairs={{1,0},{0,1},{3,2},{2,3},{5,4},{4,5},{7,6},{6,7},{9,8},{8,9},{11,10... | collective-permute-start | bytes 1572872 | tf_op jit(solution)/shard_map/ppermute | solution.py:255
  97.3 2.6 collective-permute-start.18
  148.0 16.8 %all-to-all-start.2 = ((f32[16,48,128]{2,1,0:T(8,128)}), f32[16,48,128]{2,1,0:T(8,128)S(1)}, u32[]{:S(2)}, u32[]{:S(2)}) async-start(f32[16,48,128]{2,1,0:T(8,128)} %copy-done.5), calls=%async_computation.2 | async-start | bytes 786432 | tf_op jit(solution)/shard_map/all_to_all | solution.py:250
  167.7 52.6 %copy-start.7 = (f32[64,128]{1,0:T(8,128)S(1)}, f32[64,128]{1,0:T(8,128)}, u32[]{:S(2)}) copy-start(f32[64,128]{1,0:T(8,128)} %copy-done.6) | copy-start | bytes 98308
  266.2 15.4 %all-to-all-start.4 = ((f32[16,48,128]{2,1,0:T(8,128)}), f32[16,48,128]{2,1,0:T(8,128)S(1)}, u32[]{:S(2)}, u32[]{:S(2)}) async-start(f32[16,48,128]{2,1,0:T(8,128)} %copy-done.4), calls=%async_computation.4 | async-start | bytes 786432 | tf_op jit(solution)/shard_map/all_to_all | solution.py:250
  325.4 12.1 %all-to-all-start.5 = ((f32[8,1,1024]{2,1,0:T(1,128)}), f32[8,1,1024]{2,1,0:T(1,128)S(1)}, u32[]{:S(2)}, u32[]{:S(2)}) async-start(f32[8,1,1024]{2,1,0:T(1,128)} %bitcast.49), calls=%async_computation.5 | async-start | bytes 65536 | tf_op jit(solution)/shard_map/all_to_all | solution.py:250
  (10 other events, 11.1 us)

commit v2 on v1

v2 whole, which is shorter than its diff:
```python
import functools
import math

import jax
import jax.numpy as jnp
import numpy as np
from jax import lax
from jax.experimental import pallas as pl
from jax.experimental.pallas import tpu as pltpu
from jax.sharding import Mesh
from jax.sharding import PartitionSpec as P

TSUB = 8
CAP = 2
ITERS = 2
EPSILON = 0.1

DIMS = (4, 4, 4, 2)
NAMES = ("x", "y", "z", "core")
ROWS = ("y", "z")
COLS = ("x", "core")
N_ROWS = 16
N_COLS = 8
RING = 4
SRC = 384
TILE = 128
SUBS = SRC // TILE
FEAT = 256
TILES = N_COLS * TSUB
SLOTS = N_ROWS * N_COLS * CAP
UNROLL = 4
EXTRA = 16
LISTED = 8 + SLOTS + 4 * UNROLL
NOTHING = TILES << 8
GAIN = 2.0 / (FEAT * EPSILON)
UNIT = 1.0 / (FEAT * EPSILON)
LOG2E = math.log2(math.e)
SPAN = 70.0


def lse_over_first(parts):
    top = jnp.max(parts, axis=0)
    base = jnp.where(top == -jnp.inf, 0.0, top)
    return top + jnp.log(jnp.sum(jnp.exp(parts - base[None]), axis=0))


def spread(values, norm_ref):
    high, low = jnp.max(values), jnp.min(values)
    reach = GAIN * jnp.sqrt(jnp.max(norm_ref[0:8]) * jnp.max(norm_ref[8:16]))
    return 0.5 * high + 0.5 * low, 0.5 * high - 0.5 * low + reach <= SPAN


def diagonal():
    return lax.broadcasted_iota(jnp.int32, (TILE, TILE), 0) == lax.broadcasted_iota(
        jnp.int32, (TILE, TILE), 1
    )


def as_row(eye, col):
    return jnp.sum(jnp.where(eye, col, 0.0), axis=0, keepdims=True)


def as_col(eye, row):
    return jnp.sum(jnp.where(eye, row, 0.0), axis=1, keepdims=True)


def products(x, y):
    return jnp.dot(x, y, preferred_element_type=jnp.float32)


def item_at(item_ref, w):
    one, two = item_ref[8 + 2 * w], item_ref[9 + 2 * w]
    return (
        one >> 20,
        (one >> 16) & 15,
        (one >> 8) & 255,
        (two >> 8) & 255,
        one & 255,
        two & 255,
    )


def exps(x_ref, y_ref, h, r0, r1):
    y = jnp.concatenate([y_ref[r0], y_ref[r1]], axis=1)
    return jnp.exp2((GAIN * LOG2E) * products(x_ref[h], y))


def rescale(old, new):
    return jnp.where(old == new, 1.0, jnp.exp(old - new))


def split(values):
    high = values.astype(jnp.bfloat16).astype(jnp.float32)
    rest = values - high
    middle = rest.astype(jnp.bfloat16).astype(jnp.float32)
    return [high, middle, (rest - middle).astype(jnp.bfloat16).astype(jnp.float32)]


def start_all(pairs, sems):
    copies = [pltpu.make_async_copy(src, dst, sems.at[k]) for k, (src, dst) in enumerate(pairs)]
    for copy in copies:
        copy.start()
    return copies


def prepare_kernel(*refs):
    xo_ref, yo_ref, nx_ref, ny_ref, lb_ref = refs[7:12]
    y_ref, mass_ref, goal_ref, init_ref, tile_ref, count_ref, sems = refs[12:]
    copies = start_all(
        zip(refs[:7], (xo_ref.at[0:SRC], y_ref, mass_ref, goal_ref, init_ref, tile_ref, count_ref)),
        sems,
    )
    eye = diagonal()
    for copy in copies[2:]:
        copy.wait()
    la = jnp.log(mass_ref[...])
    lb = jnp.log(goal_ref[...])
    lb_ref[...] = lb

    copies[0].wait()
    norms = []
    for b in range(SUBS):
        x = xo_ref[b * TILE : (b + 1) * TILE, :].astype(jnp.float32)
        norms.append(as_row(eye, jnp.sum(x * x, axis=1, keepdims=True)))
    nx = jnp.concatenate(norms, axis=0)
    nx_ref[...] = nx
    bound = jnp.full((1, TILE), 1.01 * jnp.max(nx))
    left = split(la) + [bound, jnp.zeros((EXTRA - 10, TILE), jnp.float32)]
    right = [
        tile_ref[...].astype(jnp.float32),
        count_ref[...].astype(jnp.float32),
        jnp.zeros((EXTRA - 3, TILE), jnp.float32),
    ]
    extra = jnp.concatenate(
        [jnp.concatenate(left, axis=0), jnp.concatenate(right, axis=0)], axis=1
    )
    xo_ref[SRC:] = extra.astype(jnp.bfloat16)

    copies[1].wait()
    norms = []
    for t in range(TSUB):
        y = y_ref[t * TILE : (t + 1) * TILE, :].astype(jnp.float32).T
        norms.append(jnp.sum(y * y, axis=0, keepdims=True))
        yo_ref[t, 0:FEAT] = y.astype(jnp.bfloat16)
    ny = jnp.concatenate(norms, axis=0)
    ny_ref[...] = ny
    a0 = init_ref[...] / EPSILON - ny * UNIT
    parts = split(a0) + split(lb)
    bound = jnp.full((1, TILE), 1.01 * jnp.max(ny))
    for t in range(TSUB):
        rows = [part[t : t + 1] for part in parts]
        rows += [bound, jnp.zeros((EXTRA - 7, TILE), jnp.float32)]
        yo_ref[t, FEAT:] = jnp.concatenate(rows, axis=0).astype(jnp.bfloat16)


def gray(k):
    return k ^ (k >> 1)


def ring_place(offset, first):
    place = gray(offset)
    other = ((place & 1) << 1) | (place >> 1)
    return jnp.where(first == 0, place, other)


def assemble_kernel(*refs):
    at_ref = refs[0]
    x_refs, y_refs = refs[1 : 1 + 2 * RING], refs[1 + 2 * RING : 1 + 4 * RING]
    item_ref, xs_ref, ys_ref, la_ref, a_ref, lb_ref, norm_ref = refs[1 + 4 * RING : 8 + 4 * RING]
    table, numbers, x_extra, y_extra, sems, sem = refs[8 + 4 * RING :]
    x, y, z, core = (at_ref[k] for k in range(4))

    small, large = [], []
    for half in range(2):
        for later in range(RING):
            piece = x_refs[RING * half + later]
            place = pl.ds(RING * later + 2 * half, 2)
            small.append((piece.at[:, SRC:, :], x_extra.at[place]))
            large.append((piece.at[:, 0:SRC, :], xs_ref.at[place]))
    for k, piece in enumerate(y_refs):
        place = pl.ds(TSUB * k, TSUB)
        small.append((piece.at[:, FEAT:, :], y_extra.at[place]))
        large.append((piece.at[:, 0:FEAT, :], ys_ref.at[place]))
    copies = start_all(small + large, sems)
    for copy in copies[: len(small)]:
        copy.wait()

    bound = None
    for later in range(RING):
        for sooner in range(RING):
            one, two = gray(sooner), gray(later)
            off_y = jnp.where(core == 0, one, two)
            off_z = jnp.where(core == 0, two, one)
            s = RING * (y ^ off_y) + (z ^ off_z)
            extra = x_extra[RING * later + sooner].astype(jnp.float32)
            la = extra[0:3, :TILE] + extra[3:6, :TILE] + extra[6:9, :TILE]
            for b in range(SUBS):
                la_ref[pl.ds(SUBS * s + b, 1), :] = la[b : b + 1]
            here = extra[9:10, :TILE]
            bound = here if bound is None else jnp.maximum(bound, here)
            table[s] = extra[0:8, TILE:].astype(jnp.int32)
    norm_ref[0:8] = jnp.broadcast_to(bound, (8, TILE))

    copy = pltpu.make_async_copy(table, numbers, sem)
    copy.start()

    bound = None
    for k in range(2 * RING):
        side = core ^ (k // RING)
        place = k % RING
        offset = jnp.where(side == 0, gray(place), (0, 3, 1, 2)[place])
        owner = 2 * (x ^ offset) + side
        extra = y_extra[TSUB * k : TSUB * (k + 1)].astype(jnp.float32)
        rows = pl.ds(pl.multiple_of(TSUB * owner, TSUB), TSUB)
        a_ref[rows, :] = extra[:, 0] + extra[:, 1] + extra[:, 2]
        lb_ref[rows, :] = extra[:, 3] + extra[:, 4] + extra[:, 5]
        here = extra[0, 6:7]
        bound = here if bound is None else jnp.maximum(bound, here)
    norm_ref[8:16] = jnp.broadcast_to(bound, (8, TILE))

    copy.wait()
    lanes, starts = [], []
    for owner in range(N_COLS):
        px, side = owner // 2, owner % 2
        lanes.append(2 * (RING * RING * px + RING * y + z) + side)
        starts.append(TSUB * (RING * (side ^ core) + ring_place(px ^ x, side)))

    def block(s, place):
        off_y, off_z = (s >> 2) ^ y, (s & 3) ^ z
        sooner = jnp.where(core == 0, off_y, off_z)
        later = jnp.where(core == 0, off_z, off_y)
        head = (s << 20) | ((RING * gray(later) + gray(sooner)) << 16)
        for owner in range(N_COLS):
            count = numbers[s, 2, lanes[owner]]
            for e in range(CAP):
                tile = numbers[s, e, lanes[owner]]
                item_ref[place] = head | ((TSUB * owner + tile) << 8) | (starts[owner] + tile)
                place = place + jnp.where(e < count, 1, 0)
        item_ref[place] = head | NOTHING
        return place + (place & 1)

    end = lax.fori_loop(0, N_ROWS, block, jnp.int32(8))
    for k in range(2 * UNROLL):
        item_ref[end + k] = jnp.int32(NOTHING)
    item_ref[0] = (end - 8) >> 1
    for copy in copies[len(small) :]:
        copy.wait()


def row_kernel(
    combine, item_ref, x_ref, y_ref, norm_ref, a_ref, lb_ref, out_ref, a_buf, u_buf, acc, top
):
    if combine:
        a = lb_ref[...] - lse_over_first(a_ref[...])
    else:
        a = a_ref[...]
    mid, fast = spread(a, norm_ref)
    n_items = item_ref[0]
    eye = diagonal()

    acc[...] = jnp.zeros_like(acc)

    @pl.when(fast)
    def _():
        u_buf[0:TILES] = jnp.exp(a - mid)
        u_buf[TILES:] = jnp.zeros((8, TILE), jnp.float32)

        def step(w, _):
            for k in range(UNROLL):
                s, h, t0, t1, r0, r1 = item_at(item_ref, UNROLL * w + k)
                e = exps(x_ref, y_ref, h, r0, r1)
                acc[s] += (
                    e[:, :TILE] * u_buf[pl.ds(t0, 1), :] + e[:, TILE:] * u_buf[pl.ds(t1, 1), :]
                )
            return 0

        lax.fori_loop(0, lax.div(n_items + UNROLL - 1, UNROLL), step, 0)
        for k in range(N_ROWS * SUBS):
            s, b = k // SUBS, k % SUBS
            col = jnp.sum(acc[s, b * TILE : (b + 1) * TILE, :], axis=1, keepdims=True)
            done = mid + jnp.log(as_row(eye, col))
            out_ref[:, k : k + 1, :] = jnp.broadcast_to(done[None], (N_ROWS, 1, TILE))

    @pl.when(jnp.logical_not(fast))
    def _():
        a_buf[0:TILES] = a
        a_buf[TILES:] = jnp.zeros((8, TILE), jnp.float32)
        top[...] = jnp.full_like(top, -jnp.inf)

        def step(w, _):
            s, h, t0, t1, r0, r1 = item_at(item_ref, w)
            for t, r in ((t0, r0), (t1, r1)):

                @pl.when(t < TILES)
                def _(t=t, r=r):
                    score = GAIN * products(x_ref[h], y_ref[r]) + a_buf[pl.ds(t, 1), :]
                    old = top[s]
                    new = jnp.maximum(old, score)
                    acc[s] = acc[s] * rescale(old, new) + jnp.exp(score - new)
                    top[s] = new

            return 0

        lax.fori_loop(0, n_items, step, 0)

        def finish(k, _):
            s, b = lax.div(k, SUBS), lax.rem(k, SUBS)
            rows = pl.ds(pl.multiple_of(b * TILE, TILE), TILE)
            block = top[s, rows, :]
            high = jnp.max(block, axis=1, keepdims=True)
            base = jnp.where(high == -jnp.inf, 0.0, high)
            total = jnp.sum(acc[s, rows, :] * jnp.exp(block - base), axis=1, keepdims=True)
            high_row = jnp.max(jnp.where(eye, high, -jnp.inf), axis=0, keepdims=True)
            done = high_row + jnp.log(as_row(eye, total))
            out_ref[:, pl.ds(k, 1), :] = jnp.broadcast_to(done[None], (N_ROWS, 1, TILE))
            return 0

        lax.fori_loop(0, N_ROWS * SUBS, finish, 0)


def col_kernel(
    item_ref, x_ref, y_ref, norm_ref, parts_ref, la_ref, out_ref, b_ref, spread_buf, acc, top
):
    b = la_ref[...] - lse_over_first(parts_ref[...])
    b_ref[...] = b
    mid, fast = spread(b, norm_ref)
    n_items = item_ref[0]
    eye = diagonal()

    def lay_out(values):
        for k in range(N_ROWS * SUBS):
            s, part = k // SUBS, k % SUBS
            col = as_col(eye, values[k : k + 1, :])
            spread_buf[s, part * TILE : (part + 1) * TILE, :] = jnp.broadcast_to(col, (TILE, TILE))

    acc[...] = jnp.zeros_like(acc)

    @pl.when(fast)
    def _():
        lay_out(jnp.exp(b - mid))

        def step(w, _):
            for k in range(UNROLL):
                s, h, t0, t1, r0, r1 = item_at(item_ref, UNROLL * w + k)
                e = exps(x_ref, y_ref, h, r0, r1)
                v = spread_buf[s]
                acc[t0] += jnp.sum((e[:, :TILE] * v).reshape(SRC // 8, 8, TILE), axis=0)
                acc[t1] += jnp.sum((e[:, TILE:] * v).reshape(SRC // 8, 8, TILE), axis=0)
            return 0

        lax.fori_loop(0, lax.div(n_items + UNROLL - 1, UNROLL), step, 0)
        done = mid + jnp.log(jnp.sum(acc[0:TILES], axis=1))
        out_ref[...] = jnp.broadcast_to(done[None], out_ref.shape)

    @pl.when(jnp.logical_not(fast))
    def _():
        lay_out(b)
        top[...] = jnp.full_like(top, -jnp.inf)

        def step(w, _):
            s, h, t0, t1, r0, r1 = item_at(item_ref, w)
            for t, r in ((t0, r0), (t1, r1)):

                @pl.when(t < TILES)
                def _(t=t, r=r):
                    score = GAIN * products(x_ref[h], y_ref[r]) + spread_buf[s]
                    score = score.reshape(SRC // 8, 8, TILE)
                    old = top[t]
                    new = jnp.maximum(old, jnp.max(score, axis=0))
                    acc[t] = acc[t] * rescale(old, new) + jnp.sum(
                        jnp.exp(score - new[None]), axis=0
                    )
                    top[t] = new

            return 0

        lax.fori_loop(0, n_items, step, 0)
        high = jnp.max(top[0:TILES], axis=1)
        base = jnp.where(high == -jnp.inf, 0.0, high)
        total = jnp.sum(acc[0:TILES] * jnp.exp(top[0:TILES] - base[:, None, :]), axis=1)
        out_ref[...] = jnp.broadcast_to((high + jnp.log(total))[None], out_ref.shape)


VMEM = pl.BlockSpec(memory_space=pltpu.VMEM)
ANY = pl.BlockSpec(memory_space=pl.ANY)
SMEM = pl.BlockSpec(memory_space=pltpu.SMEM)


def limit(mebibytes):
    return pltpu.CompilerParams(vmem_limit_bytes=mebibytes * 1024 * 1024)


def shape(dims, dtype=jnp.float32):
    return jax.ShapeDtypeStruct(dims, dtype)


def prepare(*operands):
    return pl.pallas_call(
        prepare_kernel,
        out_shape=(
            shape((SRC + EXTRA, FEAT), jnp.bfloat16),
            shape((TSUB, FEAT + EXTRA, TILE), jnp.bfloat16),
            shape((SUBS, TILE)),
            shape((TSUB, TILE)),
            shape((TSUB, TILE)),
        ),
        in_specs=[ANY] * 7,
        out_specs=(VMEM,) * 5,
        scratch_shapes=[
            pltpu.VMEM((TSUB * TILE, FEAT), jnp.bfloat16),
            pltpu.VMEM((SUBS, TILE), jnp.float32),
            pltpu.VMEM((TSUB, TILE), jnp.float32),
            pltpu.VMEM((TSUB, TILE), jnp.float32),
            pltpu.VMEM((CAP, TILE), jnp.int32),
            pltpu.VMEM((1, TILE), jnp.int32),
            pltpu.SemaphoreType.DMA((7,)),
        ],
        compiler_params=limit(60),
        name="prepare",
    )(*operands)


def assemble(at, xs, ys):
    return pl.pallas_call(
        assemble_kernel,
        out_shape=(
            shape((LISTED,), jnp.int32),
            shape((N_ROWS, SRC, FEAT), jnp.bfloat16),
            shape((TILES, FEAT, TILE), jnp.bfloat16),
            shape((N_ROWS * SUBS, TILE)),
            shape((TILES, TILE)),
            shape((TILES, TILE)),
            shape((16, TILE)),
        ),
        in_specs=[SMEM] + [ANY] * (len(xs) + len(ys)),
        out_specs=(SMEM,) + (VMEM,) * 6,
        scratch_shapes=[
            pltpu.VMEM((N_ROWS, 8, TILE), jnp.int32),
            pltpu.SMEM((N_ROWS, 8, TILE), jnp.int32),
            pltpu.VMEM((N_ROWS, EXTRA, FEAT), jnp.bfloat16),
            pltpu.VMEM((TILES, EXTRA, TILE), jnp.bfloat16),
            pltpu.SemaphoreType.DMA((8 * RING,)),
            pltpu.SemaphoreType.DMA,
        ],
        compiler_params=limit(24),
        name="assemble",
    )(at, *xs, *ys)


def row_pass(items, xs, ys, norms, a, lb, combine):
    return pl.pallas_call(
        functools.partial(row_kernel, combine),
        out_shape=shape((N_ROWS, N_ROWS * SUBS, TILE)),
        in_specs=[SMEM] + [VMEM] * 5,
        out_specs=VMEM,
        scratch_shapes=[
            pltpu.VMEM((TILES + 8, TILE), jnp.float32),
            pltpu.VMEM((TILES + 8, TILE), jnp.float32),
            pltpu.VMEM((N_ROWS, SRC, TILE), jnp.float32),
            pltpu.VMEM((N_ROWS, SRC, TILE), jnp.float32),
        ],
        compiler_params=limit(20),
        name="row_pass",
    )(items, xs, ys, norms, a, lb)


def col_pass(items, xs, ys, norms, parts, la, copies):
    return pl.pallas_call(
        col_kernel,
        out_shape=(shape((copies, TILES, TILE)), shape((N_ROWS * SUBS, TILE))),
        in_specs=[SMEM] + [VMEM] * 5,
        out_specs=(VMEM, VMEM),
        scratch_shapes=[
            pltpu.VMEM((N_ROWS, SRC, TILE), jnp.float32),
            pltpu.VMEM((TILES + 1, 8, TILE), jnp.float32),
            pltpu.VMEM((TILES + 1, 8, TILE), jnp.float32),
        ],
        compiler_params=limit(20),
        name="col_pass",
    )(items, xs, ys, norms, parts, la)


def swap(blocks, axes):
    return lax.all_to_all(blocks, axes, split_axis=0, concat_axis=0, tiled=True)


def exchange(block, partner):
    pairs = []
    for place in range(N_ROWS * N_COLS):
        at = tuple(int(k) for k in np.unravel_index(place, DIMS))
        pairs.append((place, int(np.ravel_multi_index(partner(*at), DIMS))))
    return lax.ppermute(block, NAMES, pairs)


def gather_ring(block, one, two):
    first, second = exchange(block, one), exchange(block, two)
    return [block, first, second, exchange(second, one)]


def gather_sources(block):
    one, two = source_partner(0, 1), source_partner(0, 3)
    first, second = exchange(block, one), exchange(block, two)
    opposite = exchange(second, one)
    one, two = source_partner(1, 1), source_partner(1, 3)
    pair = jnp.stack([block, first])
    pieces = gather_ring(pair, one, two)
    pair = jnp.stack([second, opposite])
    first, second = exchange(pair, one), exchange(pair, two)
    return pieces + [pair, first, second, exchange(first, two)]


def source_partner(stage, flip):
    def partner(x, y, z, core):
        return (x, y ^ flip, z, core) if stage == core else (x, y, z ^ flip, core)

    return partner


def target_partner(order):
    return lambda x, y, z, core: (x ^ (1, 3)[order ^ core], y, z, core)


def sibling(x, y, z, core):
    return (x, y, z, core ^ 1)


def body(
    source_points, target_points, source_mass, target_mass, target_init, pair_tiles, pair_count
):
    x_block, y_block, source_norm, target_norm, log_target = prepare(
        source_points,
        target_points,
        source_mass.reshape(SUBS, TILE),
        target_mass.reshape(TSUB, TILE),
        target_init.reshape(TSUB, TILE),
        pair_tiles.T,
        pair_count.reshape(1, -1),
    )
    xs = gather_sources(x_block)
    near = gather_ring(y_block, target_partner(0), target_partner(1))
    far = [exchange(block, sibling) for block in near]

    at = jnp.stack([lax.axis_index(name) for name in NAMES]).astype(jnp.int32)
    items, xs, ys, la, a0, lb, norms = assemble(at, xs, near + far)
    held = (items, xs, ys, norms)

    row_parts = row_pass(*held, a0, lb, False)
    for iteration in range(ITERS):
        final = iteration == ITERS - 1
        col_parts, b = col_pass(*held, swap(row_parts, ROWS), la, 1 if final else N_COLS)
        if not final:
            row_parts = row_pass(*held, swap(col_parts, COLS), lb, True)
    here = lax.axis_index(ROWS)
    b_here = lax.dynamic_slice_in_dim(b, here * SUBS, SUBS)
    source_pot = EPSILON * (b_here + source_norm * UNIT)
    last = swap(col_parts.reshape(N_COLS, TSUB, TILE), COLS)
    target_pot = EPSILON * (log_target - lse_over_first(last) + target_norm * UNIT)
    return (source_pot.reshape(-1), target_pot.reshape(-1))


def solution(mesh):
    grid = Mesh(mesh.devices.reshape(DIMS), NAMES)
    placed = (
        P(NAMES, None),
        P(NAMES, None),
        P(NAMES),
        P(NAMES),
        P(NAMES),
        P(NAMES, None),
        P(NAMES),
    )
    return jax.shard_map(
        body, mesh=grid, in_specs=placed, out_specs=(P(NAMES), P(NAMES)), check_vma=False
    )
```

time: 344 us -> 305 us (0.89)
  blocking collectives: 12.3 us -> 35.2 us
  waiting for transfers between devices: 39.1 us -> 22.6 us
  starting transfers between devices: 66.2 us -> 51.3 us
  local copies, waits for them, and re-layouts: 36.8 us -> 22.9 us
  other arithmetic: 12.9 us -> 3.7 us
  Pallas kernels: 170 us -> 165 us
    all_to_all x1 -> x2, blocking collectives: 12.3 us -> 35.2 us  [swap(): return lax.all_to_all(blocks, axes, split_axis=0, concat_axis=0, tiled=True)]
    ppermute x19 -> x16, waiting for transfers between devices: 22.3 us -> 11.2 us  [exchange(): return lax.ppermute(block, NAMES, pairs)]
    all_to_all x5 -> x2, starting transfers between devices: 36.7 us -> 25.9 us  [swap(): return lax.all_to_all(blocks, axes, split_axis=0, concat_axis=0, tiled=True)]
    all_to_all x5 -> x2, waiting for transfers between devices: 16.8 us -> 11.4 us  [swap(): return lax.all_to_all(blocks, axes, split_axis=0, concat_axis=0, tiled=True)]
    pallas_call x4 -> x6, Pallas kernels: 170 us -> 165 us  [the longest x2 84.1 us: row_pass(): pl.pallas_call(functools.partial(row_kernel, combine), out_shape=shape((N...]
    concatenate x9 -> x0, local copies, waits for them, and re-layouts: 4.93 us -> none  [the longest x1 1.7 us: work_items(): jnp.concatenate([jnp.stack([block, kz * RING + ky, ky * RING + kz], axis=...]
    reshape x6 -> x0, local copies, waits for them, and re-layouts: 4.41 us -> none  [the longest x1 2.05 us: body(): target_points.reshape(TSUB, TILE, FEAT).transpose(0, 2, 1)]
    ppermute x19 -> x16, starting transfers between devices: 29.6 us -> 25.4 us  [exchange(): return lax.ppermute(block, NAMES, pairs)]
  transfers between devices with their start and end apart: 24 -> 18, of which waited for: 8 -> 6; matrix products, arithmetic and copies ran while one was open for 10% -> 1% of each run, Pallas kernels for 0% -> 0%
where the time goes in v2:
time: 305 us; the launch traced here: 302 us
  Pallas kernels  165 us (54%)
  starting transfers between devices  51.3 us (17%)
  blocking collectives  35.2 us (12%)
  local copies, waits for them, and re-layouts  22.9 us (8%)
  waiting for transfers between devices  22.6 us (7%)
  other arithmetic  3.7 us (1%)
    pallas_call x2, Pallas kernels, row_pass(): pl.pallas_call(functools.partial(row_kernel, combine), out_shape=shape((N...  84.1 us
    pallas_call x2, Pallas kernels, col_pass(): pl.pallas_call(col_kernel, out_shape=(shape((copies, TILES, TILE)), shape...  73.1 us
    all_to_all x2, blocking collectives, swap(): return lax.all_to_all(blocks, axes, split_axis=0, concat_axis=0, tiled=True)  35.2 us
    all_to_all x2, starting transfers between devices, swap(): return lax.all_to_all(blocks, axes, split_axis=0, concat_axis=0, tiled=True)  25.9 us
    ppermute x16, starting transfers between devices, exchange(): return lax.ppermute(block, NAMES, pairs)  25.4 us
    unnamed x62, local copies, waits for them, and re-layouts  22.9 us
    all_to_all x2, waiting for transfers between devices, swap(): return lax.all_to_all(blocks, axes, split_axis=0, concat_axis=0, tiled=True)  11.4 us
    ppermute x16, waiting for transfers between devices, exchange(): return lax.ppermute(block, NAMES, pairs)  11.2 us
  transfers between devices with their start and end apart: 18, of which 6 were waited for; matrix products, arithmetic and copies ran while one was open for 1% of the time, Pallas kernels for 0%

profile of v2, /device:TPU:1, one launch (start us, length us, event | category | flops | bytes accessed | tf_op | source)
XLA Modules:
  0.0 301.8 jit_solution(12897674673071901994)
XLA Ops:
  0.6 2.5 prepare.1
  3.1 2.1 collective-permute-start.10
  5.2 2.2 collective-permute-start.12
  7.4 3.8 %collective-permute-start.4 = (bf16[400,256]{1,0:T(8,128)(2,1)}, bf16[400,256]{1,0:T(8,128)(2,1)S(1)}, u32[]{:S(2)}, u32[]{:S(2)}) collective-permute-start(bf16[400,256]{1,0:T(8,128)(2,1)} %get-tuple-element.17), channel_id=1, source_target_pairs={{0,24},{1,7},{2,26},{3,5},{4,28},{5,3},{6,30},{7,1},{8,16},{9,15},... | collective-permute-start | bytes 614408 | tf_op jit(solution)/shard_map/ppermute | solution.py:492
  11.4 3.4 %collective-permute-done.4 = bf16[400,256]{1,0:T(8,128)(2,1)S(1)} collective-permute-done((bf16[400,256]{1,0:T(8,128)(2,1)}, bf16[400,256]{1,0:T(8,128)(2,1)S(1)}, u32[]{:S(2)}, u32[]{:S(2)}) %collective-permute-start.4) | collective-permute-done | bytes 204832 | tf_op jit(solution)/shard_map/ppermute | solution.py:492
  14.9 1.8 collective-permute-start.11
  17.6 5.7 %collective-permute-start.2 = (bf16[2,400,256]{2,1,0:T(8,128)(2,1)S(1)}, bf16[2,400,256]{2,1,0:T(8,128)(2,1)}, u32[]{:S(2)}, u32[]{:S(2)}) collective-permute-start(bf16[2,400,256]{2,1,0:T(8,128)(2,1)S(1)} %pad_maximum_fusion.refs_1_), channel_id=1, source_target_pairs={{0,6},{1,25},{2,4},{3,27},{4,2},{5,29},{6,0},{7,31},{8,14},{9,17},... | collective-permute-start | bytes 1228808 | tf_op jit(solution)/shard_map/ppermute | solution.py:492
  24.4 1.2 collective-permute-start.6
  26.4 2.7 collective-permute-done.2.refs_3_
  29.0 3.0 %collective-permute-start.14 = (bf16[8,272,128]{2,1,0:T(8,128)(2,1)S(1)}, bf16[8,272,128]{2,1,0:T(8,128)(2,1)S(1)}, u32[]{:S(2)}, u32[]{:S(2)}) collective-permute-start(bf16[8,272,128]{2,1,0:T(8,128)(2,1)S(1)} %collective-permute-done.10.refs_11_), channel_id=1, source_target_pairs={{0,1},{1,0},{2,3},{3,2},{4,5},{5,4},{6,7},{7,6},{8,9},{9,8},{10,11... | collective-permute-start | bytes 1671176 | tf_op jit(solution)/shard_map/ppermute | solution.py:492
  32.8 1.9 collective-permute-start.13
  37.1 1.3 collective-permute-start.3
  38.4 1.9 collective-permute-start.8
  40.4 4.1 %collective-permute-done.3.refs_4_ = bf16[2,400,256]{2,1,0:T(8,128)(2,1)} collective-permute-done((bf16[2,400,256]{2,1,0:T(8,128)(2,1)}, bf16[2,400,256]{2,1,0:T(8,128)(2,1)}, u32[]{:S(2)}, u32[]{:S(2)}) %collective-permute-start.3) | collective-permute-done | bytes 409632 | tf_op jit(solution)/shard_map/ppermute | solution.py:492
  48.1 1.1 copy-done.5
  49.1 1.1 copy-done.7
  51.2 1.1 copy-done.11
  52.3 1.1 copy-done.13
  57.5 5.6 %assemble.1 = (s32[280]{0:T(512)S(1)}, bf16[16,384,256]{2,1,0:T(8,128)(2,1)S(1)}, bf16[64,256,128]{2,1,0:T(8,128)(2,1)S(1)}, f32[48,128]{1,0:T(8,128)S(1)}, f32[...) custom-call(s32[4]{0:T(128)S(1)} %pad_add_fusion.refs_0_, ...), custom_call_target="tpu_custom_call" | custom-call | tf_op jit(solution)/shard_map/assemble/pallas_call | solution.py:424
  63.1 42.0 %row_pass.2 = f32[16,48,128]{2,1,0:T(8,128)S(1)} custom-call(s32[280]{0:T(512)S(1)} %get-tuple-element.19.item_ref, bf16[16,384,256]{2,1,0:T(8,128)(2,1)S(1)} %get-tuple-element.20.x_ref, bf16[64,256,128]{2,1,0:T(8,128)(2,1)S(1)} %get-tuple-element.21.y_ref, f32[16,128]{1,0:T(8,128)S(1)} %get-tuple-element.22.norm_ref, ...), custom_call_target="tpu_custom_call" | custom-call | tf_op jit(solution)/shard_map/row_pass/pallas_call | solution.py:451
  105.1 16.0 %all_to_all.20.parts_ref = f32[16,48,128]{2,1,0:T(8,128)S(1)} all-to-all(f32[16,48,128]{2,1,0:T(8,128)S(1)} %row_pass.2), channel_id=1, replica_groups=mesh['x'=4,'y'=4,'z'=4,'core'=2] {'y','z'}, dimensions={0} | all-to-all | bytes 786432 | tf_op jit(solution)/shard_map/all_to_all | solution.py:484
  121.1 36.8 %col_pass.2 = (f32[8,64,128]{2,1,0:T(8,128)S(1)}, f32[48,128]{1,0:T(8,128)}) custom-call(s32[280]{0:T(512)S(1)} %get-tuple-element.19.item_ref, bf16[16,384,256]{2,1,0:T(8,128)(2,1)S(1)} %get-tuple-element.20.x_ref, bf16[64,256,128]{2,1,0:T(8,128)(2,1)S(1)} %get-tuple-element.21.y_ref, f32[16,128]{1,0:T(8,128)S(1)} %get-tuple-element.22.norm_ref, ...), custom_call_target="tpu_custom_call" | custom-call | tf_op jit(solution)/shard_map/col_pass/pallas_call | solution.py:468
  158.0 19.2 %all_to_all.21.a_ref = f32[8,64,128]{2,1,0:T(8,128)S(1)} all-to-all(f32[8,64,128]{2,1,0:T(8,128)S(1)} %get-tuple-element.26), channel_id=1, replica_groups=mesh['x'=4,'y'=4,'z'=4,'core'=2] {'x','core'}, dimensions={0} | all-to-all | bytes 524288 | tf_op jit(solution)/shard_map/all_to_all | solution.py:484
  177.2 42.2 %row_pass.3 = f32[16,48,128]{2,1,0:T(8,128)S(1)} custom-call(s32[280]{0:T(512)S(1)} %get-tuple-element.19.item_ref, bf16[16,384,256]{2,1,0:T(8,128)(2,1)S(1)} %get-tuple-element.20.x_ref, bf16[64,256,128]{2,1,0:T(8,128)(2,1)S(1)} %get-tuple-element.21.y_ref, f32[16,128]{1,0:T(8,128)S(1)} %get-tuple-element.22.norm_ref, f32[8,64,128]{2,1,0:T(8,128)S(1)} %all_to_all.21.a_ref, ...), custom_call_target="tpu_custom_call" | custom-call | tf_op jit(solution)/shard_map/row_pass/pallas_call | solution.py:451
  220.1 10.6 %all-to-all-start.2 = ((f32[16,48,128]{2,1,0:T(8,128)}), f32[16,48,128]{2,1,0:T(8,128)S(1)}, u32[]{:S(2)}, u32[]{:S(2)}) async-start(f32[16,48,128]{2,1,0:T(8,128)} %copy-done.4), calls=%async_computation.2 | async-start | bytes 786432 | tf_op jit(solution)/shard_map/all_to_all | solution.py:484
  230.7 8.0 %all-to-all-done.2.parts_ref = f32[16,48,128]{2,1,0:T(8,128)S(1)} async-done(((f32[16,48,128]{2,1,0:T(8,128)}), f32[16,48,128]{2,1,0:T(8,128)S(1)}, u32[]{:S(2)}, u32[]{:S(2)}) %all-to-all-start.2) | async-done | bytes 393248 | tf_op jit(solution)/shard_map/all_to_all | solution.py:484
  238.6 2.2 copy-done.1
  242.9 36.2 %col_pass.3 = (f32[1,64,128]{2,1,0:T(8,128)S(1)}, f32[48,128]{1,0:T(8,128)S(1)}) custom-call(s32[280]{0:T(512)S(1)} %copy-done.28, bf16[16,384,256]{2,1,0:T(8,128)(2,1)S(1)} %get-tuple-element.20.x_ref, bf16[64,256,128]{2,1,0:T(8,128)(2,1)S(1)} %copy-done.1, f32[16,128]{1,0:T(8,128)S(1)} %copy-done.23, f32[16,48,128]{2,1,0:T(8,128)S(1)} %all-to-all-done.2.parts_ref, ...), custom_call_target="tpu_custom_call" | custom-call | tf_op jit(solution)/shard_map/col_pass/pallas_call | solution.py:468
  280.4 15.4 %all-to-all-start.3 = ((f32[8,8,128]{2,1,0:T(8,128)}), f32[8,8,128]{2,1,0:T(8,128)S(1)}, u32[]{:S(2)}, u32[]{:S(2)}) async-start(f32[8,8,128]{2,1,0:T(8,128)} %bitcast.18), calls=%async_computation.3 | async-start | bytes 65536 | tf_op jit(solution)/shard_map/all_to_all | solution.py:484
  295.8 1.3 multiply_bitcast_fusion.1
  297.0 3.5 %all-to-all-done.3 = f32[8,8,128]{2,1,0:T(8,128)S(1)} async-done(((f32[8,8,128]{2,1,0:T(8,128)}), f32[8,8,128]{2,1,0:T(8,128)S(1)}, u32[]{:S(2)}, u32[]{:S(2)}) %all-to-all-start.3) | async-done | bytes 32800 | tf_op jit(solution)/shard_map/all_to_all | solution.py:484
  300.6 1.3 multiply_bitcast_fusion
  (82 shorter events, 19.0 us)
Async XLA Ops:
  3.1 11.8 %collective-permute-start.10 = (bf16[8,272,128]{2,1,0:T(8,128)(2,1)}, bf16[8,272,128]{2,1,0:T(8,128)(2,1)S(1)}, u32[]{:S(2)}, u32[]{:S(2)}) collective-permute-start(bf16[8,272,128]{2,1,0:T(8,128)(2,1)} %get-tuple-element.18.refs_9_), channel_id=1, source_target_pairs={{0,96},{1,33},{2,98},{3,35},{4,100},{5,37},{6,102},{7,39},{8,104},... | collective-permute-start | bytes 1671176 | tf_op jit(solution)/shard_map/ppermute | solution.py:492
  5.2 18.1 %collective-permute-start.12 = (bf16[8,272,128]{2,1,0:T(8,128)(2,1)}, bf16[8,272,128]{2,1,0:T(8,128)(2,1)S(1)}, u32[]{:S(2)}, u32[]{:S(2)}) collective-permute-start(bf16[8,272,128]{2,1,0:T(8,128)(2,1)} %get-tuple-element.18.refs_9_), channel_id=1, source_target_pairs={{0,1},{1,0},{2,3},{3,2},{4,5},{5,4},{6,7},{7,6},{8,9},{9,8},{10,11... | collective-permute-start | bytes 1671176 | tf_op jit(solution)/shard_map/ppermute | solution.py:492
  7.4 7.4 %collective-permute-start.4 = (bf16[400,256]{1,0:T(8,128)(2,1)}, bf16[400,256]{1,0:T(8,128)(2,1)S(1)}, u32[]{:S(2)}, u32[]{:S(2)}) collective-permute-start(bf16[400,256]{1,0:T(8,128)(2,1)} %get-tuple-element.17), channel_id=1, source_target_pairs={{0,24},{1,7},{2,26},{3,5},{4,28},{5,3},{6,30},{7,1},{8,16},{9,15},... | collective-permute-start | bytes 614408 | tf_op jit(solution)/shard_map/ppermute | solution.py:492
  11.2 13.2 %collective-permute-start.9 = (bf16[8,272,128]{2,1,0:T(8,128)(2,1)}, bf16[8,272,128]{2,1,0:T(8,128)(2,1)S(1)}, u32[]{:S(2)}, u32[]{:S(2)}) collective-permute-start(bf16[8,272,128]{2,1,0:T(8,128)(2,1)} %get-tuple-element.18.refs_9_), channel_id=1, source_target_pairs={{0,32},{1,97},{2,34},{3,99},{4,36},{5,101},{6,38},{7,103},{8,40},{... | collective-permute-start | bytes 1671176 | tf_op jit(solution)/shard_map/ppermute | solution.py:492
  11.4 5.2 %collective-permute-start = (bf16[400,256]{1,0:T(8,128)(2,1)}, bf16[400,256]{1,0:T(8,128)(2,1)S(1)}, u32[]{:S(2)}, u32[]{:S(2)}) collective-permute-start(bf16[400,256]{1,0:T(8,128)(2,1)} %get-tuple-element.17), channel_id=1, source_target_pairs={{0,8},{1,3},{2,10},{3,1},{4,12},{5,7},{6,14},{7,5},{8,0},{9,11},{1... | collective-permute-start | bytes 614408 | tf_op jit(solution)/shard_map/ppermute | solution.py:492
  14.8 8.5 %collective-permute-start.5 = (bf16[400,256]{1,0:T(8,128)(2,1)S(1)}, bf16[400,256]{1,0:T(8,128)(2,1)S(1)}, u32[]{:S(2)}, u32[]{:S(2)}) collective-permute-start(bf16[400,256]{1,0:T(8,128)(2,1)S(1)} %collective-permute-done.4), channel_id=1, source_target_pairs={{0,8},{1,3},{2,10},{3,1},{4,12},{5,7},{6,14},{7,5},{8,0},{9,11},{1... | collective-permute-start | bytes 614408 | tf_op jit(solution)/shard_map/ppermute | solution.py:492
  14.9 32.2 %copy-start.6 = (bf16[8,272,128]{2,1,0:T(8,128)(2,1)}, bf16[8,272,128]{2,1,0:T(8,128)(2,1)S(1)}, u32[]{:S(2)}) copy-start(bf16[8,272,128]{2,1,0:T(8,128)(2,1)S(1)} %collective-permute-done.10.refs_11_) | copy-start | bytes 1671172
  14.9 20.7 %collective-permute-start.11 = (bf16[8,272,128]{2,1,0:T(8,128)(2,1)S(1)}, bf16[8,272,128]{2,1,0:T(8,128)(2,1)S(1)}, u32[]{:S(2)}, u32[]{:S(2)}) collective-permute-start(bf16[8,272,128]{2,1,0:T(8,128)(2,1)S(1)} %collective-permute-done.10.refs_11_), channel_id=1, source_target_pairs={{0,32},{1,97},{2,34},{3,99},{4,36},{5,101},{6,38},{7,103},{8,40},{... | collective-permute-start | bytes 1671176 | tf_op jit(solution)/shard_map/ppermute | solution.py:492
  17.6 11.4 %collective-permute-start.2 = (bf16[2,400,256]{2,1,0:T(8,128)(2,1)S(1)}, bf16[2,400,256]{2,1,0:T(8,128)(2,1)}, u32[]{:S(2)}, u32[]{:S(2)}) collective-permute-start(bf16[2,400,256]{2,1,0:T(8,128)(2,1)S(1)} %pad_maximum_fusion.refs_1_), channel_id=1, source_target_pairs={{0,6},{1,25},{2,4},{3,27},{4,2},{5,29},{6,0},{7,31},{8,14},{9,17},... | collective-permute-start | bytes 1228808 | tf_op jit(solution)/shard_map/ppermute | solution.py:492
  23.3 8.8 %collective-permute-start.1 = (bf16[2,400,256]{2,1,0:T(8,128)(2,1)S(1)}, bf16[2,400,256]{2,1,0:T(8,128)(2,1)S(1)}, u32[]{:S(2)}, u32[]{:S(2)}) collective-permute-start(bf16[2,400,256]{2,1,0:T(8,128)(2,1)S(1)} %pad_maximum_fusion.refs_1_), channel_id=1, source_target_pairs={{0,2},{1,9},{2,0},{3,11},{4,6},{5,13},{6,4},{7,15},{8,10},{9,1},{1... | collective-permute-start | bytes 1228808 | tf_op jit(solution)/shard_map/ppermute | solution.py:492
  24.2 12.2 %collective-permute-start.7 = (bf16[2,400,256]{2,1,0:T(8,128)(2,1)S(1)}, bf16[2,400,256]{2,1,0:T(8,128)(2,1)S(1)}, u32[]{:S(2)}, u32[]{:S(2)}) collective-permute-start(bf16[2,400,256]{2,1,0:T(8,128)(2,1)S(1)} %pad_maximum_fusion.1.refs_5_), channel_id=1, source_target_pairs={{0,6},{1,25},{2,4},{3,27},{4,2},{5,29},{6,0},{7,31},{8,14},{9,17},... | collective-permute-start | bytes 1228808 | tf_op jit(solution)/shard_map/ppermute | solution.py:492
  24.4 14.0 %collective-permute-start.6 = (bf16[2,400,256]{2,1,0:T(8,128)(2,1)S(1)}, bf16[2,400,256]{2,1,0:T(8,128)(2,1)}, u32[]{:S(2)}, u32[]{:S(2)}) collective-permute-start(bf16[2,400,256]{2,1,0:T(8,128)(2,1)S(1)} %pad_maximum_fusion.1.refs_5_), channel_id=1, source_target_pairs={{0,2},{1,9},{2,0},{3,11},{4,6},{5,13},{6,4},{7,15},{8,10},{9,1},{1... | collective-permute-start | bytes 1228808 | tf_op jit(solution)/shard_map/ppermute | solution.py:492
  29.0 15.5 %collective-permute-start.14 = (bf16[8,272,128]{2,1,0:T(8,128)(2,1)S(1)}, bf16[8,272,128]{2,1,0:T(8,128)(2,1)S(1)}, u32[]{:S(2)}, u32[]{:S(2)}) collective-permute-start(bf16[8,272,128]{2,1,0:T(8,128)(2,1)S(1)} %collective-permute-done.10.refs_11_), channel_id=1, source_target_pairs={{0,1},{1,0},{2,3},{3,2},{4,5},{5,4},{6,7},{7,6},{8,9},{9,8},{10,11... | collective-permute-start | bytes 1671176 | tf_op jit(solution)/shard_map/ppermute | solution.py:492
  32.8 12.5 %collective-permute-start.13 = (bf16[8,272,128]{2,1,0:T(8,128)(2,1)S(1)}, bf16[8,272,128]{2,1,0:T(8,128)(2,1)S(1)}, u32[]{:S(2)}, u32[]{:S(2)}) collective-permute-start(bf16[8,272,128]{2,1,0:T(8,128)(2,1)S(1)} %collective-permute-done.9.refs_10_), channel_id=1, source_target_pairs={{0,1},{1,0},{2,3},{3,2},{4,5},{5,4},{6,7},{7,6},{8,9},{9,8},{10,11... | collective-permute-start | bytes 1671176 | tf_op jit(solution)/shard_map/ppermute | solution.py:492
  35.6 11.5 %collective-permute-start.15 = (bf16[8,272,128]{2,1,0:T(8,128)(2,1)S(1)}, bf16[8,272,128]{2,1,0:T(8,128)(2,1)}, u32[]{:S(2)}, u32[]{:S(2)}) collective-permute-start(bf16[8,272,128]{2,1,0:T(8,128)(2,1)S(1)} %collective-permute-done.11.refs_12_), channel_id=1, source_target_pairs={{0,1},{1,0},{2,3},{3,2},{4,5},{5,4},{6,7},{7,6},{8,9},{9,8},{10,11... | collective-permute-start | bytes 1671176 | tf_op jit(solution)/shard_map/ppermute | solution.py:492
  37.1 7.4 %collective-permute-start.3 = (bf16[2,400,256]{2,1,0:T(8,128)(2,1)}, bf16[2,400,256]{2,1,0:T(8,128)(2,1)}, u32[]{:S(2)}, u32[]{:S(2)}) collective-permute-start(bf16[2,400,256]{2,1,0:T(8,128)(2,1)} %collective-permute-done.2.refs_3_), channel_id=1, source_target_pairs={{0,2},{1,9},{2,0},{3,11},{4,6},{5,13},{6,4},{7,15},{8,10},{9,1},{1... | collective-permute-start | bytes 1228808 | tf_op jit(solution)/shard_map/ppermute | solution.py:492
  38.4 8.6 %collective-permute-start.8 = (bf16[2,400,256]{2,1,0:T(8,128)(2,1)}, bf16[2,400,256]{2,1,0:T(8,128)(2,1)}, u32[]{:S(2)}, u32[]{:S(2)}) collective-permute-start(bf16[2,400,256]{2,1,0:T(8,128)(2,1)} %collective-permute-done.6.refs_6_), channel_id=1, source_target_pairs={{0,6},{1,25},{2,4},{3,27},{4,2},{5,29},{6,0},{7,31},{8,14},{9,17},... | collective-permute-start | bytes 1228808 | tf_op jit(solution)/shard_map/ppermute | solution.py:492
  48.1 1.1 copy-start.5
  49.1 1.1 copy-start.7
  50.2 1.1 copy-start.9
  51.2 1.1 copy-start.11
  52.3 1.1 copy-start.13
  53.3 1.1 copy-start.15
  54.4 1.1 copy-start.17
  63.1 58.1 %copy-start.24 = (f32[48,128]{1,0:T(8,128)}, f32[48,128]{1,0:T(8,128)S(1)}, u32[]{:S(2)}) copy-start(f32[48,128]{1,0:T(8,128)S(1)} %get-tuple-element.25.la_ref) | copy-start | bytes 73732
  63.1 114.1 %copy-start = (bf16[64,256,128]{2,1,0:T(8,128)(2,1)}, bf16[64,256,128]{2,1,0:T(8,128)(2,1)S(1)}, u32[]{:S(2)}) copy-start(bf16[64,256,128]{2,1,0:T(8,128)(2,1)S(1)} %get-tuple-element.21.y_ref) | copy-start | bytes 12582916
  63.1 114.0 %copy-start.22 = (f32[16,128]{1,0:T(8,128)}, f32[16,128]{1,0:T(8,128)S(1)}, u32[]{:S(2)}) copy-start(f32[16,128]{1,0:T(8,128)S(1)} %get-tuple-element.22.norm_ref) | copy-start | bytes 24580
  63.1 114.0 %copy-start.27 = (s32[280]{0:T(512)}, s32[280]{0:T(512)S(1)}, u32[]{:S(2)}) copy-start(s32[280]{0:T(512)S(1)} %get-tuple-element.19.item_ref) | copy-start | bytes 3364
  220.1 80.5 %copy-start.30 = (f32[8,128]{1,0:T(8,128)S(1)}, f32[8,128]{1,0:T(8,128)}, u32[]{:S(2)}) copy-start(f32[8,128]{1,0:T(8,128)} %get-tuple-element.31) | copy-start | bytes 12292
  220.1 18.6 %all-to-all-start.2 = ((f32[16,48,128]{2,1,0:T(8,128)}), f32[16,48,128]{2,1,0:T(8,128)S(1)}, u32[]{:S(2)}, u32[]{:S(2)}) async-start(f32[16,48,128]{2,1,0:T(8,128)} %copy-done.4), calls=%async_computation.2 | async-start | bytes 786432 | tf_op jit(solution)/shard_map/all_to_all | solution.py:484
  238.6 2.2 copy-start.1
  280.4 20.1 %all-to-all-start.3 = ((f32[8,8,128]{2,1,0:T(8,128)}), f32[8,8,128]{2,1,0:T(8,128)S(1)}, u32[]{:S(2)}, u32[]{:S(2)}) async-start(f32[8,8,128]{2,1,0:T(8,128)} %bitcast.18), calls=%async_computation.3 | async-start | bytes 65536 | tf_op jit(solution)/shard_map/all_to_all | solution.py:484
  (17 other events, 13.4 us)

commit v3 on v2

--- a/solution.py
+++ b/solution.py
@@ -20,6 +20,7 @@
 ROWS = ("y", "z")
 COLS = ("x", "core")
 N_ROWS = 16
+N_PIECES = 15
 N_COLS = 8
 RING = 4
 SRC = 384
@@ -28,10 +29,13 @@
 FEAT = 256
 TILES = N_COLS * TSUB
 SLOTS = N_ROWS * N_COLS * CAP
-UNROLL = 4
+ROW_UNROLL = 8
+COL_UNROLL = 16
+LAST_UNROLL = 4
 EXTRA = 16
-LISTED = 8 + SLOTS + 4 * UNROLL
+LISTED = 8 + SLOTS + 4 * LAST_UNROLL
 NOTHING = TILES << 8
+NORMS = 16
 GAIN = 2.0 / (FEAT * EPSILON)
 UNIT = 1.0 / (FEAT * EPSILON)
 LOG2E = math.log2(math.e)
@@ -80,9 +84,29 @@
     )
 
 
-def exps(x_ref, y_ref, h, r0, r1):
-    y = jnp.concatenate([y_ref[r0], y_ref[r1]], axis=1)
-    return jnp.exp2((GAIN * LOG2E) * products(x_ref[h], y))
+def exps(x, y):
+    return jnp.exp2((GAIN * LOG2E) * products(x, y))
+
+
+def two_tiles(y_ref, r0, r1):
+    return jnp.concatenate([y_ref[r0], y_ref[r1]], axis=1)
+
+
+def sweep(n_items, work, many):
+    def steps(first, size):
+        def step(w, _):
+            for k in range(size):
+                work(first + size * w + k)
+            return 0
+
+        return step
+
+    whole = lax.div(n_items, many)
+    lax.fori_loop(0, whole, steps(0, many), 0)
+    left = n_items - many * whole
+    lax.fori_loop(
+        0, lax.div(left + LAST_UNROLL - 1, LAST_UNROLL), steps(many * whole, LAST_UNROLL), 0
+    )
 
 
 def rescale(old, new):
@@ -104,8 +128,8 @@
 
 
 def prepare_kernel(*refs):
-    xo_ref, yo_ref, nx_ref, ny_ref, lb_ref = refs[7:12]
-    y_ref, mass_ref, goal_ref, init_ref, tile_ref, count_ref, sems = refs[12:]
+    xo_ref, yo_ref, nx_ref, part_ref = refs[7:11]
+    y_ref, mass_ref, goal_ref, init_ref, tile_ref, count_ref, sems = refs[11:]
     copies = start_all(
         zip(refs[:7], (xo_ref.at[0:SRC], y_ref, mass_ref, goal_ref, init_ref, tile_ref, count_ref)),
         sems,
@@ -115,7 +139,6 @@
         copy.wait()
     la = jnp.log(mass_ref[...])
     lb = jnp.log(goal_ref[...])
-    lb_ref[...] = lb
 
     copies[0].wait()
     norms = []
@@ -143,7 +166,7 @@
         norms.append(jnp.sum(y * y, axis=0, keepdims=True))
         yo_ref[t, 0:FEAT] = y.astype(jnp.bfloat16)
     ny = jnp.concatenate(norms, axis=0)
-    ny_ref[...] = ny
+    part_ref[...] = EPSILON * (lb + UNIT * ny)
     a0 = init_ref[...] / EPSILON - ny * UNIT
     parts = split(a0) + split(lb)
     bound = jnp.full((1, TILE), 1.01 * jnp.max(ny))
@@ -163,27 +186,44 @@
     return jnp.where(first == 0, place, other)
 
 
-def assemble_kernel(*refs):
-    at_ref = refs[0]
-    x_refs, y_refs = refs[1 : 1 + 2 * RING], refs[1 + 2 * RING : 1 + 4 * RING]
-    item_ref, xs_ref, ys_ref, la_ref, a_ref, lb_ref, norm_ref = refs[1 + 4 * RING : 8 + 4 * RING]
-    table, numbers, x_extra, y_extra, sems, sem = refs[8 + 4 * RING :]
-    x, y, z, core = (at_ref[k] for k in range(4))
-
-    small, large = [], []
+def piece_copies(x_refs, y_refs, xs, ys, x_rows, y_rows):
+    pairs = []
     for half in range(2):
         for later in range(RING):
-            piece = x_refs[RING * half + later]
             place = pl.ds(RING * later + 2 * half, 2)
-            small.append((piece.at[:, SRC:, :], x_extra.at[place]))
-            large.append((piece.at[:, 0:SRC, :], xs_ref.at[place]))
-    for k, piece in enumerate(y_refs):
-        place = pl.ds(TSUB * k, TSUB)
-        small.append((piece.at[:, FEAT:, :], y_extra.at[place]))
-        large.append((piece.at[:, 0:FEAT, :], ys_ref.at[place]))
-    copies = start_all(small + large, sems)
-    for copy in copies[: len(small)]:
+            pairs.append((x_refs[RING * half + later].at[:, x_rows, :], xs.at[place]))
+    start = 0
+    for piece in y_refs:
+        pairs.append((piece.at[:, y_rows, :], ys.at[pl.ds(start, piece.shape[0])]))
+        start += piece.shape[0]
+    return pairs
+
+
+def first_kernel(*refs):
+    at_ref, pieces = refs[0], refs[1 : 1 + N_PIECES]
+    x_refs, y_refs = pieces[: 2 * RING], pieces[2 * RING :]
+    out_ref, item_ref, cols_ref, rows_ref, xs_out, ys_out = refs[1 + N_PIECES : 7 + N_PIECES]
+    a_buf, u_buf, acc, top, xs, ys, sems = refs[7 + N_PIECES : 14 + N_PIECES]
+    a_ref, table, numbers, x_extra, y_extra, small_sems, sem, out_sems = refs[14 + N_PIECES :]
+    la_ref, lb_ref = cols_ref.at[NORMS:], rows_ref.at[NORMS:]
+    x, y, z, core = (at_ref[k] for k in range(4))
+
+    small = start_all(
+        piece_copies(
+            x_refs, y_refs, x_extra, y_extra, slice(SRC, SRC + EXTRA), slice(FEAT, FEAT + EXTRA)
+        ),
+        small_sems,
+    )
+    large = start_all(
+        piece_copies(x_refs, y_refs, xs, ys, slice(0, SRC), slice(0, FEAT)), sems
+    )
+    for copy in small:
         copy.wait()
+
+    lane = lax.broadcasted_iota(jnp.int32, (CAP, TILE), 1)
+    px, side = lane >> 5, lane & 1
+    start = RING * (side ^ core) + ring_place(px ^ x, side)
+    entry_base = ((TSUB * (2 * px + side)) << 8) + TSUB * start
 
     bound = None
     for later in range(RING):
@@ -198,8 +238,14 @@
                 la_ref[pl.ds(SUBS * s + b, 1), :] = la[b : b + 1]
             here = extra[9:10, :TILE]
             bound = here if bound is None else jnp.maximum(bound, here)
-            table[s] = extra[0:8, TILE:].astype(jnp.int32)
-    norm_ref[0:8] = jnp.broadcast_to(bound, (8, TILE))
+            numbers_here = extra[0:3, TILE:].astype(jnp.int32)
+            head = (s << 20) | ((RING * later + sooner) << 16)
+            entry = head | (entry_base + 257 * numbers_here[0:CAP])
+            slot = lax.broadcasted_iota(jnp.int32, (CAP, TILE), 0)
+            entry = jnp.where(slot < numbers_here[CAP : CAP + 1], entry, -1)
+            table[pl.ds(s, 1)] = jnp.concatenate([entry, jnp.full((6, TILE), head)], axis=0)[None]
+    for ref in (cols_ref, rows_ref):
+        ref[0:8] = jnp.broadcast_to(bound, (8, TILE))
 
     copy = pltpu.make_async_copy(table, numbers, sem)
     copy.start()
@@ -216,44 +262,42 @@
         lb_ref[rows, :] = extra[:, 3] + extra[:, 4] + extra[:, 5]
         here = extra[0, 6:7]
         bound = here if bound is None else jnp.maximum(bound, here)
-    norm_ref[8:16] = jnp.broadcast_to(bound, (8, TILE))
+    for ref in (cols_ref, rows_ref):
+        ref[8:16] = jnp.broadcast_to(bound, (8, TILE))
 
     copy.wait()
-    lanes, starts = [], []
-    for owner in range(N_COLS):
-        px, side = owner // 2, owner % 2
-        lanes.append(2 * (RING * RING * px + RING * y + z) + side)
-        starts.append(TSUB * (RING * (side ^ core) + ring_place(px ^ x, side)))
+    lanes = [
+        2 * (RING * RING * (owner // 2) + RING * y + z) + owner % 2 for owner in range(N_COLS)
+    ]
 
     def block(s, place):
-        off_y, off_z = (s >> 2) ^ y, (s & 3) ^ z
-        sooner = jnp.where(core == 0, off_y, off_z)
-        later = jnp.where(core == 0, off_z, off_y)
-        head = (s << 20) | ((RING * gray(later) + gray(sooner)) << 16)
-        for owner in range(N_COLS):
-            count = numbers[s, 2, lanes[owner]]
+        for lane in lanes:
             for e in range(CAP):
-                tile = numbers[s, e, lanes[owner]]
-                item_ref[place] = head | ((TSUB * owner + tile) << 8) | (starts[owner] + tile)
-                place = place + jnp.where(e < count, 1, 0)
-        item_ref[place] = head | NOTHING
+                entry = numbers[s, e, lane]
+                item_ref[place] = entry
+                place = place + jnp.where(entry >= 0, 1, 0)
+        item_ref[place] = numbers[s, CAP, 0] | NOTHING
         return place + (place & 1)
 
     end = lax.fori_loop(0, N_ROWS, block, jnp.int32(8))
-    for k in range(2 * UNROLL):
+    for k in range(2 * LAST_UNROLL):
         item_ref[end + k] = jnp.int32(NOTHING)
     item_ref[0] = (end - 8) >> 1
-    for copy in copies[len(small) :]:
+    item_ref[1] = RING * y + z
+    for copy in large:
         copy.wait()
-
-
-def row_kernel(
-    combine, item_ref, x_ref, y_ref, norm_ref, a_ref, lb_ref, out_ref, a_buf, u_buf, acc, top
-):
-    if combine:
-        a = lb_ref[...] - lse_over_first(a_ref[...])
-    else:
-        a = a_ref[...]
+    outward = start_all([(xs, xs_out), (ys, ys_out)], out_sems)
+    row_core(a_ref[...], item_ref, xs, ys, cols_ref, out_ref, a_buf, u_buf, acc, top)
+    for copy in outward:
+        copy.wait()
+
+
+def row_kernel(item_ref, x_ref, y_ref, side_ref, parts_ref, out_ref, a_buf, u_buf, acc, top):
+    a = side_ref[NORMS:] - lse_over_first(parts_ref[...])
+    row_core(a, item_ref, x_ref, y_ref, side_ref, out_ref, a_buf, u_buf, acc, top)
+
+
+def row_core(a, item_ref, x_ref, y_ref, norm_ref, out_ref, a_buf, u_buf, acc, top):
     mid, fast = spread(a, norm_ref)
     n_items = item_ref[0]
     eye = diagonal()
@@ -265,16 +309,13 @@
         u_buf[0:TILES] = jnp.exp(a - mid)
         u_buf[TILES:] = jnp.zeros((8, TILE), jnp.float32)
 
-        def step(w, _):
-            for k in range(UNROLL):
-                s, h, t0, t1, r0, r1 = item_at(item_ref, UNROLL * w + k)
-                e = exps(x_ref, y_ref, h, r0, r1)
-                acc[s] += (
-                    e[:, :TILE] * u_buf[pl.ds(t0, 1), :] + e[:, TILE:] * u_buf[pl.ds(t1, 1), :]
-                )
-            return 0
-
-        lax.fori_loop(0, lax.div(n_items + UNROLL - 1, UNROLL), step, 0)
+        def work(w):
+            s, h, t0, t1, r0, r1 = item_at(item_ref, w)
+            u0, u1 = u_buf[pl.ds(t0, 1), :], u_buf[pl.ds(t1, 1), :]
+            e = exps(x_ref[h], two_tiles(y_ref, r0, r1))
+            acc[s] += e[:, :TILE] * u0 + e[:, TILE:] * u1
+
+        sweep(n_items, work, ROW_UNROLL)
         for k in range(N_ROWS * SUBS):
             s, b = k // SUBS, k % SUBS
             col = jnp.sum(acc[s, b * TILE : (b + 1) * TILE, :], axis=1, keepdims=True)
@@ -318,11 +359,23 @@
         lax.fori_loop(0, N_ROWS * SUBS, finish, 0)
 
 
-def col_kernel(
-    item_ref, x_ref, y_ref, norm_ref, parts_ref, la_ref, out_ref, b_ref, spread_buf, acc, top
+def last_col_kernel(
+    item_ref, x_ref, y_ref, side_ref, parts_ref, norm_ref, out_ref, f_ref, b_buf, *scratch
 ):
-    b = la_ref[...] - lse_over_first(parts_ref[...])
-    b_ref[...] = b
+    b = side_ref[NORMS:] - lse_over_first(parts_ref[...])
+    b_buf[...] = b
+    for k in range(SUBS):
+        here = b_buf[pl.ds(SUBS * item_ref[1] + k, 1), :]
+        f_ref[k : k + 1, :] = EPSILON * (here + UNIT * norm_ref[k : k + 1, :])
+    col_core(b, item_ref, x_ref, y_ref, side_ref, out_ref, *scratch)
+
+
+def col_kernel(item_ref, x_ref, y_ref, side_ref, parts_ref, out_ref, *scratch):
+    b = side_ref[NORMS:] - lse_over_first(parts_ref[...])
+    col_core(b, item_ref, x_ref, y_ref, side_ref, out_ref, *scratch)
+
+
+def col_core(b, item_ref, x_ref, y_ref, norm_ref, out_ref, spread_buf, acc, top):
     mid, fast = spread(b, norm_ref)
     n_items = item_ref[0]
     eye = diagonal()
@@ -339,16 +392,14 @@
     def _():
         lay_out(jnp.exp(b - mid))
 
-        def step(w, _):
-            for k in range(UNROLL):
-                s, h, t0, t1, r0, r1 = item_at(item_ref, UNROLL * w + k)
-                e = exps(x_ref, y_ref, h, r0, r1)
-                v = spread_buf[s]
-                acc[t0] += jnp.sum((e[:, :TILE] * v).reshape(SRC // 8, 8, TILE), axis=0)
-                acc[t1] += jnp.sum((e[:, TILE:] * v).reshape(SRC // 8, 8, TILE), axis=0)
-            return 0
-
-        lax.fori_loop(0, lax.div(n_items + UNROLL - 1, UNROLL), step, 0)
+        def work(w):
+            s, h, t0, t1, r0, r1 = item_at(item_ref, w)
+            e = exps(x_ref[h], two_tiles(y_ref, r0, r1))
+            v = spread_buf[s]
+            acc[t0] += jnp.sum((e[:, :TILE] * v).reshape(SRC // 8, 8, TILE), axis=0)
+            acc[t1] += jnp.sum((e[:, TILE:] * v).reshape(SRC // 8, 8, TILE), axis=0)
+
+        sweep(n_items, work, COL_UNROLL)
         done = mid + jnp.log(jnp.sum(acc[0:TILES], axis=1))
         out_ref[...] = jnp.broadcast_to(done[None], out_ref.shape)
 
@@ -402,10 +453,9 @@
             shape((TSUB, FEAT + EXTRA, TILE), jnp.bfloat16),
             shape((SUBS, TILE)),
             shape((TSUB, TILE)),
-            shape((TSUB, TILE)),
         ),
         in_specs=[ANY] * 7,
-        out_specs=(VMEM,) * 5,
+        out_specs=(VMEM,) * 4,
         scratch_shapes=[
             pltpu.VMEM((TSUB * TILE, FEAT), jnp.bfloat16),
             pltpu.VMEM((SUBS, TILE), jnp.float32),
@@ -420,64 +470,86 @@
     )(*operands)
 
 
-def assemble(at, xs, ys):
+ROW_SCRATCH = [
+    pltpu.VMEM((TILES + 8, TILE), jnp.float32),
+    pltpu.VMEM((TILES + 8, TILE), jnp.float32),
+    pltpu.VMEM((N_ROWS, SRC, TILE), jnp.float32),
+    pltpu.VMEM((N_ROWS, SRC, TILE), jnp.float32),
+]
+COL_SCRATCH = [
+    pltpu.VMEM((N_ROWS, SRC, TILE), jnp.float32),
+    pltpu.VMEM((TILES + 1, 8, TILE), jnp.float32),
+    pltpu.VMEM((TILES + 1, 8, TILE), jnp.float32),
+]
+ROW_PARTS = shape((N_ROWS, N_ROWS * SUBS, TILE))
+
+
+def first_pass(at, pieces):
     return pl.pallas_call(
-        assemble_kernel,
+        first_kernel,
         out_shape=(
+            ROW_PARTS,
             shape((LISTED,), jnp.int32),
+            shape((NORMS + N_ROWS * SUBS, TILE)),
+            shape((NORMS + TILES, TILE)),
             shape((N_ROWS, SRC, FEAT), jnp.bfloat16),
             shape((TILES, FEAT, TILE), jnp.bfloat16),
-            shape((N_ROWS * SUBS, TILE)),
-            shape((TILES, TILE)),
-            shape((TILES, TILE)),
-            shape((16, TILE)),
         ),
-        in_specs=[SMEM] + [ANY] * (len(xs) + len(ys)),
-        out_specs=(SMEM,) + (VMEM,) * 6,
-        scratch_shapes=[
+        in_specs=[SMEM] + [ANY] * N_PIECES,
+        out_specs=(VMEM, SMEM, VMEM, VMEM, ANY, ANY),
+        scratch_shapes=ROW_SCRATCH
+        + [
+            pltpu.VMEM((N_ROWS, SRC, FEAT), jnp.bfloat16),
+            pltpu.VMEM((TILES, FEAT, TILE), jnp.bfloat16),
+            pltpu.SemaphoreType.DMA((N_PIECES,)),
+            pltpu.VMEM((TILES, TILE), jnp.float32),
             pltpu.VMEM((N_ROWS, 8, TILE), jnp.int32),
             pltpu.SMEM((N_ROWS, 8, TILE), jnp.int32),
             pltpu.VMEM((N_ROWS, EXTRA, FEAT), jnp.bfloat16),
             pltpu.VMEM((TILES, EXTRA, TILE), jnp.bfloat16),
-            pltpu.SemaphoreType.DMA((8 * RING,)),
+            pltpu.SemaphoreType.DMA((N_PIECES,)),
             pltpu.SemaphoreType.DMA,
+            pltpu.SemaphoreType.DMA((2,)),
         ],
-        compiler_params=limit(24),
-        name="assemble",
-    )(at, *xs, *ys)
-
-
-def row_pass(items, xs, ys, norms, a, lb, combine):
+        compiler_params=limit(60),
+        name="first_row_pass",
+    )(at, *pieces)
+
+
+def row_pass(items, *operands):
     return pl.pallas_call(
-        functools.partial(row_kernel, combine),
-        out_shape=shape((N_ROWS, N_ROWS * SUBS, TILE)),
-        in_specs=[SMEM] + [VMEM] * 5,
+        row_kernel,
+        out_shape=ROW_PARTS,
+        in_specs=[SMEM] + [VMEM] * len(operands),
         out_specs=VMEM,
-        scratch_shapes=[
-            pltpu.VMEM((TILES + 8, TILE), jnp.float32),
-            pltpu.VMEM((TILES + 8, TILE), jnp.float32),
-            pltpu.VMEM((N_ROWS, SRC, TILE), jnp.float32),
-            pltpu.VMEM((N_ROWS, SRC, TILE), jnp.float32),
-        ],
+        scratch_shapes=ROW_SCRATCH,
         compiler_params=limit(20),
         name="row_pass",
-    )(items, xs, ys, norms, a, lb)
-
-
-def col_pass(items, xs, ys, norms, parts, la, copies):
+    )(items, *operands)
+
+
+def col_pass(items, *operands):
     return pl.pallas_call(
         col_kernel,
-        out_shape=(shape((copies, TILES, TILE)), shape((N_ROWS * SUBS, TILE))),
-        in_specs=[SMEM] + [VMEM] * 5,
-        out_specs=(VMEM, VMEM),
-        scratch_shapes=[
-            pltpu.VMEM((N_ROWS, SRC, TILE), jnp.float32),
-            pltpu.VMEM((TILES + 1, 8, TILE), jnp.float32),
-            pltpu.VMEM((TILES + 1, 8, TILE), jnp.float32),
-        ],
+        out_shape=shape((N_COLS, TILES, TILE)),
+        in_specs=[SMEM] + [VMEM] * len(operands),
+        out_specs=VMEM,
+        scratch_shapes=COL_SCRATCH,
         compiler_params=limit(20),
         name="col_pass",
-    )(items, xs, ys, norms, parts, la)
+    )(items, *operands)
+
+
+def last_col_pass(items, *operands):
+    return pl.pallas_call(
+        last_col_kernel,
+        out_shape=(shape((1, TILES, TILE)), shape((SUBS, TILE))),
+        in_specs=[SMEM] + [VMEM] * len(operands),
+        out_specs=(VMEM, VMEM),
+        scratch_shapes=[pltpu.VMEM((N_ROWS * SUBS, TILE), jnp.float32)] + COL_SCRATCH,
+        compiler_params=limit(20),
+        name="last_col_pass",
+    )(items, *operands)
 
 
 def swap(blocks, axes):
@@ -493,20 +565,19 @@
 
 
 def gather_ring(block, one, two):
-    first, second = exchange(block, one), exchange(block, two)
+    first = exchange(block, one)
+    second = exchange(block, two)
     return [block, first, second, exchange(second, one)]
 
 
 def gather_sources(block):
-    one, two = source_partner(0, 1), source_partner(0, 3)
-    first, second = exchange(block, one), exchange(block, two)
-    opposite = exchange(second, one)
+    pair = jnp.stack([block, exchange(block, source_partner(0, 1))])
+    other = exchange(pair, source_partner(0, 3))
     one, two = source_partner(1, 1), source_partner(1, 3)
-    pair = jnp.stack([block, first])
-    pieces = gather_ring(pair, one, two)
-    pair = jnp.stack([second, opposite])
     first, second = exchange(pair, one), exchange(pair, two)
-    return pieces + [pair, first, second, exchange(first, two)]
+    pieces = [pair, first, second, exchange(second, one)]
+    first, second = exchange(other, one), exchange(other, two)
+    return pieces + [other, first, second, exchange(first, two)]
 
 
 def source_partner(stage, flip):
@@ -527,7 +598,7 @@
 def body(
     source_points, target_points, source_mass, target_mass, target_init, pair_tiles, pair_count
 ):
-    x_block, y_block, source_norm, target_norm, log_target = prepare(
+    x_block, y_block, source_norm, target_part = prepare(
         source_points,
         target_points,
         source_mass.reshape(SUBS, TILE),
@@ -538,23 +609,19 @@
     )
     xs = gather_sources(x_block)
     near = gather_ring(y_block, target_partner(0), target_partner(1))
-    far = [exchange(block, sibling) for block in near]
+    far = [exchange(jnp.concatenate(near[:2]), sibling)]
+    far += [exchange(block, sibling) for block in near[2:]]
 
     at = jnp.stack([lax.axis_index(name) for name in NAMES]).astype(jnp.int32)
-    items, xs, ys, la, a0, lb, norms = assemble(at, xs, near + far)
-    held = (items, xs, ys, norms)
-
-    row_parts = row_pass(*held, a0, lb, False)
-    for iteration in range(ITERS):
-        final = iteration == ITERS - 1
-        col_parts, b = col_pass(*held, swap(row_parts, ROWS), la, 1 if final else N_COLS)
-        if not final:
-            row_parts = row_pass(*held, swap(col_parts, COLS), lb, True)
-    here = lax.axis_index(ROWS)
-    b_here = lax.dynamic_slice_in_dim(b, here * SUBS, SUBS)
-    source_pot = EPSILON * (b_here + source_norm * UNIT)
+    row_parts, items, cols, rows, xs, ys = first_pass(at, xs + near + far)
+    for iteration in range(ITERS - 1):
+        col_parts = col_pass(items, xs, ys, cols, swap(row_parts, ROWS))
+        row_parts = row_pass(items, xs, ys, rows, swap(col_parts, COLS))
+    col_parts, source_pot = last_col_pass(
+        items, xs, ys, cols, swap(row_parts, ROWS), source_norm
+    )
     last = swap(col_parts.reshape(N_COLS, TSUB, TILE), COLS)
-    target_pot = EPSILON * (log_target - lse_over_first(last) + target_norm * UNIT)
+    target_pot = target_part - EPSILON * lse_over_first(last)
     return (source_pot.reshape(-1), target_pot.reshape(-1))
 
 

time: 305 us -> 295 us (0.967)
  starting transfers between devices: 51.3 us -> 20.8 us
  Pallas kernels: 165 us -> 186 us
  blocking collectives: 35.2 us -> 52.8 us
  local copies, waits for them, and re-layouts: 22.9 us -> 7.47 us
  waiting for transfers between devices: 22.6 us -> 18.3 us
    all_to_all x2 -> x0, starting transfers between devices: 25.9 us -> none  [swap(): return lax.all_to_all(blocks, axes, split_axis=0, concat_axis=0, tiled=True)]
    pallas_call x5 -> x4, Pallas kernels: 163 us -> 184 us  [the longest x1 53.5 us: first_pass(): pl.pallas_call(first_kernel, out_shape=(ROW_PARTS, shape((LISTED,), jnp.i...]
    all_to_all x2 -> x4, blocking collectives: 35.2 us -> 52.8 us  [swap(): return lax.all_to_all(blocks, axes, split_axis=0, concat_axis=0, tiled=True)]
    unnamed x62 -> x44, local copies, waits for them, and re-layouts: 22.9 us -> 7.47 us
    all_to_all x2 -> x0, waiting for transfers between devices: 11.4 us -> none  [swap(): return lax.all_to_all(blocks, axes, split_axis=0, concat_axis=0, tiled=True)]
    ppermute x16 -> x14, waiting for transfers between devices: 11.2 us -> 18.3 us  [exchange(): return lax.ppermute(block, NAMES, pairs)]
    ppermute x16 -> x14, starting transfers between devices: 25.4 us -> 20.8 us  [exchange(): return lax.ppermute(block, NAMES, pairs)]
  transfers between devices with their start and end apart: 18 -> 14, of which waited for: 6 -> 7; matrix products, arithmetic and copies ran while one was open for 1% -> 1% of each run, Pallas kernels for 0% -> 0%
where the time goes in v3:
time: 295 us; the launch traced here: 290 us
  Pallas kernels  186 us (63%)
  blocking collectives  52.8 us (18%)
  starting transfers between devices  20.8 us (7%)
  waiting for transfers between devices  18.3 us (6%)
  local copies, waits for them, and re-layouts  7.47 us (3%)
  other arithmetic  3.4 us (1%)
    pallas_call x1, Pallas kernels, first_pass(): pl.pallas_call(first_kernel, out_shape=(ROW_PARTS, shape((LISTED,), jnp.i...  53.5 us
    all_to_all x4, blocking collectives, swap(): return lax.all_to_all(blocks, axes, split_axis=0, concat_axis=0, tiled=True)  52.8 us
    pallas_call x1, Pallas kernels, row_pass(): pl.pallas_call(row_kernel, out_shape=ROW_PARTS, in_specs=[SMEM] + [VMEM]...  46.8 us
    pallas_call x1, Pallas kernels, last_col_pass(): pl.pallas_call(last_col_kernel, out_shape=(shape((1, TILES, TILE)), shape...  42 us
    pallas_call x1, Pallas kernels, col_pass(): pl.pallas_call(col_kernel, out_shape=shape((N_COLS, TILES, TILE)), in_spe...  41.4 us
    ppermute x14, starting transfers between devices, exchange(): return lax.ppermute(block, NAMES, pairs)  20.8 us
    ppermute x14, waiting for transfers between devices, exchange(): return lax.ppermute(block, NAMES, pairs)  18.3 us
    unnamed x44, local copies, waits for them, and re-layouts  7.47 us
  transfers between devices with their start and end apart: 14, of which 7 were waited for; matrix products, arithmetic and copies ran while one was open for 1% of the time, Pallas kernels for 0%

profile of v3, /device:TPU:1, one launch (start us, length us, event | category | flops | bytes accessed | tf_op | source)
XLA Modules:
  0.0 289.9 jit_solution(16193414822111152394)
XLA Ops:
  0.6 2.5 prepare.1
  3.1 2.1 collective-permute-start.9
  5.3 1.8 collective-permute-start.8
  7.1 1.6 collective-permute-start
  8.7 3.6 %collective-permute-done = bf16[400,256]{1,0:T(8,128)(2,1)S(1)} collective-permute-done((bf16[400,256]{1,0:T(8,128)(2,1)}, bf16[400,256]{1,0:T(8,128)(2,1)S(1)}, u32[]{:S(2)}, u32[]{:S(2)}) %collective-permute-start) | collective-permute-done | bytes 204832 | tf_op jit(solution)/shard_map/ppermute | solution.py:564
  12.4 1.0 pad_maximum_fusion.1.refs_1_
  13.4 3.7 %collective-permute-start.4 = (bf16[2,400,256]{2,1,0:T(8,128)(2,1)S(1)}, bf16[2,400,256]{2,1,0:T(8,128)(2,1)S(1)}, u32[]{:S(2)}, u32[]{:S(2)}) collective-permute-start(bf16[2,400,256]{2,1,0:T(8,128)(2,1)S(1)} %pad_maximum_fusion.1.refs_1_), channel_id=1, source_target_pairs={{0,24},{1,7},{2,26},{3,5},{4,28},{5,3},{6,30},{7,1},{8,16},{9,15},... | collective-permute-start | bytes 1228808 | tf_op jit(solution)/shard_map/ppermute | solution.py:564
  17.0 2.7 collective-permute-start.2
  19.8 0.9 collective-permute-start.10
  21.2 1.2 pad_maximum_fusion
  22.4 2.5 collective-permute-start.11
  24.9 3.1 %collective-permute-start.6 = (bf16[2,400,256]{2,1,0:T(8,128)(2,1)S(1)}, bf16[2,400,256]{2,1,0:T(8,128)(2,1)S(1)}, u32[]{:S(2)}, u32[]{:S(2)}) collective-permute-start(bf16[2,400,256]{2,1,0:T(8,128)(2,1)S(1)} %collective-permute-done.4.refs_5_), channel_id=1, source_target_pairs={{0,6},{1,25},{2,4},{3,27},{4,2},{5,29},{6,0},{7,31},{8,14},{9,17},... | collective-permute-start | bytes 1228808 | tf_op jit(solution)/shard_map/ppermute | solution.py:564
  28.1 3.8 %collective-permute-done.1.refs_2_ = bf16[2,400,256]{2,1,0:T(8,128)(2,1)S(1)} collective-permute-done((bf16[2,400,256]{2,1,0:T(8,128)(2,1)S(1)}, bf16[2,400,256]{2,1,0:T(8,128)(2,1)S(1)}, u32[]{:S(2)}, u32[]{:S(2)}) %collective-permute-start.1) | collective-permute-done | bytes 409632 | tf_op jit(solution)/shard_map/ppermute | solution.py:564
  31.9 0.9 collective-permute-start.12
  33.6 2.9 collective-permute-done.5.refs_6_
  36.4 1.2 collective-permute-start.7
  38.3 2.6 collective-permute-done.3.refs_4_
  40.9 4.2 %collective-permute-done.7.refs_8_ = bf16[2,400,256]{2,1,0:T(8,128)(2,1)} collective-permute-done((bf16[2,400,256]{2,1,0:T(8,128)(2,1)}, bf16[2,400,256]{2,1,0:T(8,128)(2,1)}, u32[]{:S(2)}, u32[]{:S(2)}) %collective-permute-start.7) | collective-permute-done | bytes 409632 | tf_op jit(solution)/shard_map/ppermute | solution.py:564
  45.1 0.8 copy-done.16
  45.9 1.1 copy-done.13
  47.0 53.5 %first_row_pass.1 = (f32[16,48,128]{2,1,0:T(8,128)}, s32[280]{0:T(512)}, f32[64,128]{1,0:T(8,128)}, f32[80,128]{1,0:T(8,128)}, bf16[16,384,256]{2,1,0:T(8,128)(2,1)}, /*index=5*/bf16[64,256,128]{2,1,0:T(8,128)(2,1)}) custom-call(s32[4]{0:T(128)} %pad_add_fusion.refs_0_, bf16[2,400,256]{2,1,0:T(8,128)(2,1)} %copy-done.12, bf16[2,400,256]{2,1,0:T(8,128)(2,1)} %copy-done.18, ...), custom_call_target="tpu_custom_call" | custom-call | tf_op jit(solution)/shard_map/first_row_pass/pallas_call | solution.py:488
  100.5 12.9 %all_to_all.20.parts_ref = f32[16,48,128]{2,1,0:T(8,128)S(1)} all-to-all(f32[16,48,128]{2,1,0:T(8,128)} %get-tuple-element.21), channel_id=1, replica_groups=mesh['x'=4,'y'=4,'z'=4,'core'=2] {'y','z'}, dimensions={0} | all-to-all | bytes 786432 | tf_op jit(solution)/shard_map/all_to_all | solution.py:556
  113.4 2.2 copy-done
  115.6 1.9 copy-done.2
  117.4 0.8 copy-done.4
  118.2 0.7 copy-done.7
  118.9 41.4 %col_pass.1 = f32[8,64,128]{2,1,0:T(8,128)S(1)} custom-call(s32[280]{0:T(512)S(1)} %copy-done.7, bf16[16,384,256]{2,1,0:T(8,128)(2,1)S(1)} %copy-done.2, bf16[64,256,128]{2,1,0:T(8,128)(2,1)S(1)} %copy-done, f32[64,128]{1,0:T(8,128)S(1)} %copy-done.4, f32[16,48,128]{2,1,0:T(8,128)S(1)} %all_to_all.20.parts_ref), custom_call_target="tpu_custom_call" | custom-call | tf_op jit(solution)/shard_map/col_pass/pallas_call | solution.py:532
  160.3 15.8 %all_to_all.21.parts_ref = f32[8,64,128]{2,1,0:T(8,128)S(1)} all-to-all(f32[8,64,128]{2,1,0:T(8,128)S(1)} %col_pass.1), channel_id=1, replica_groups=mesh['x'=4,'y'=4,'z'=4,'core'=2] {'x','core'}, dimensions={0} | all-to-all | bytes 524288 | tf_op jit(solution)/shard_map/all_to_all | solution.py:556
  176.2 46.8 %row_pass.1 = f32[16,48,128]{2,1,0:T(8,128)S(1)} custom-call(s32[280]{0:T(512)S(1)} %copy-done.7, bf16[16,384,256]{2,1,0:T(8,128)(2,1)S(1)} %copy-done.3, bf16[64,256,128]{2,1,0:T(8,128)(2,1)S(1)} %copy-done.1, f32[80,128]{1,0:T(8,128)S(1)} %copy-done.6, f32[8,64,128]{2,1,0:T(8,128)S(1)} %all_to_all.21.parts_ref), custom_call_target="tpu_custom_call" | custom-call | tf_op jit(solution)/shard_map/row_pass/pallas_call | solution.py:520
  223.0 13.0 %all_to_all.22.parts_ref = f32[16,48,128]{2,1,0:T(8,128)S(1)} all-to-all(f32[16,48,128]{2,1,0:T(8,128)S(1)} %row_pass.1), channel_id=1, replica_groups=mesh['x'=4,'y'=4,'z'=4,'core'=2] {'y','z'}, dimensions={0} | all-to-all | bytes 786432 | tf_op jit(solution)/shard_map/all_to_all | solution.py:556
  236.1 42.0 %last_col_pass.1 = (f32[1,64,128]{2,1,0:T(8,128)S(1)}, f32[3,128]{1,0:T(4,128)}) custom-call(s32[280]{0:T(512)S(1)} %copy-done.8, bf16[16,384,256]{2,1,0:T(8,128)(2,1)S(1)} %copy-done.3, bf16[64,256,128]{2,1,0:T(8,128)(2,1)S(1)} %copy-done.1, f32[64,128]{1,0:T(8,128)S(1)} %copy-done.5, f32[16,48,128]{2,1,0:T(8,128)S(1)} %all_to_all.22.parts_ref, ...), custom_call_target="tpu_custom_call" | custom-call | tf_op jit(solution)/shard_map/last_col_pass/pallas_call | solution.py:544
  278.1 11.1 %all_to_all.23 = f32[8,8,128]{2,1,0:T(8,128)S(1)} all-to-all(f32[8,8,128]{2,1,0:T(8,128)S(1)} %bitcast.15), channel_id=1, replica_groups=mesh['x'=4,'y'=4,'z'=4,'core'=2] {'x','core'}, dimensions={0} | all-to-all | bytes 65536 | tf_op jit(solution)/shard_map/all_to_all | solution.py:556
  (56 shorter events, 2.7 us)
Async XLA Ops:
  3.1 18.0 %copy-start.10 = (bf16[8,272,128]{2,1,0:T(8,128)(2,1)S(1)}, bf16[8,272,128]{2,1,0:T(8,128)(2,1)}, u32[]{:S(2)}) copy-start(bf16[8,272,128]{2,1,0:T(8,128)(2,1)} %get-tuple-element.15.refs_9_) | copy-start | bytes 1671172
  3.1 16.6 %collective-permute-start.9 = (bf16[8,272,128]{2,1,0:T(8,128)(2,1)}, bf16[8,272,128]{2,1,0:T(8,128)(2,1)S(1)}, u32[]{:S(2)}, u32[]{:S(2)}) collective-permute-start(bf16[8,272,128]{2,1,0:T(8,128)(2,1)} %get-tuple-element.15.refs_9_), channel_id=1, source_target_pairs={{0,96},{1,33},{2,98},{3,35},{4,100},{5,37},{6,102},{7,39},{8,104},... | collective-permute-start | bytes 1671176 | tf_op jit(solution)/shard_map/ppermute | solution.py:564
  5.3 15.9 %collective-permute-start.8 = (bf16[8,272,128]{2,1,0:T(8,128)(2,1)}, bf16[8,272,128]{2,1,0:T(8,128)(2,1)S(1)}, u32[]{:S(2)}, u32[]{:S(2)}) collective-permute-start(bf16[8,272,128]{2,1,0:T(8,128)(2,1)} %get-tuple-element.15.refs_9_), channel_id=1, source_target_pairs={{0,32},{1,97},{2,34},{3,99},{4,36},{5,101},{6,38},{7,103},{8,40},{... | collective-permute-start | bytes 1671176 | tf_op jit(solution)/shard_map/ppermute | solution.py:564
  7.1 5.3 %collective-permute-start = (bf16[400,256]{1,0:T(8,128)(2,1)}, bf16[400,256]{1,0:T(8,128)(2,1)S(1)}, u32[]{:S(2)}, u32[]{:S(2)}) collective-permute-start(bf16[400,256]{1,0:T(8,128)(2,1)} %get-tuple-element.14), channel_id=1, source_target_pairs={{0,8},{1,3},{2,10},{3,1},{4,12},{5,7},{6,14},{7,5},{8,0},{9,11},{1... | collective-permute-start | bytes 614408 | tf_op jit(solution)/shard_map/ppermute | solution.py:564
  13.3 11.5 %copy-start.12 = (bf16[2,400,256]{2,1,0:T(8,128)(2,1)}, bf16[2,400,256]{2,1,0:T(8,128)(2,1)S(1)}, u32[]{:S(2)}) copy-start(bf16[2,400,256]{2,1,0:T(8,128)(2,1)S(1)} %pad_maximum_fusion.1.refs_1_) | copy-start | bytes 1228804
  13.4 11.5 %collective-permute-start.4 = (bf16[2,400,256]{2,1,0:T(8,128)(2,1)S(1)}, bf16[2,400,256]{2,1,0:T(8,128)(2,1)S(1)}, u32[]{:S(2)}, u32[]{:S(2)}) collective-permute-start(bf16[2,400,256]{2,1,0:T(8,128)(2,1)S(1)} %pad_maximum_fusion.1.refs_1_), channel_id=1, source_target_pairs={{0,24},{1,7},{2,26},{3,5},{4,28},{5,3},{6,30},{7,1},{8,16},{9,15},... | collective-permute-start | bytes 1228808 | tf_op jit(solution)/shard_map/ppermute | solution.py:564
  17.0 10.9 %collective-permute-start.2 = (bf16[2,400,256]{2,1,0:T(8,128)(2,1)S(1)}, bf16[2,400,256]{2,1,0:T(8,128)(2,1)}, u32[]{:S(2)}, u32[]{:S(2)}) collective-permute-start(bf16[2,400,256]{2,1,0:T(8,128)(2,1)S(1)} %pad_maximum_fusion.1.refs_1_), channel_id=1, source_target_pairs={{0,6},{1,25},{2,4},{3,27},{4,2},{5,29},{6,0},{7,31},{8,14},{9,17},... | collective-permute-start | bytes 1228808 | tf_op jit(solution)/shard_map/ppermute | solution.py:564
  19.8 12.2 %copy-start.14 = (bf16[8,272,128]{2,1,0:T(8,128)(2,1)}, bf16[8,272,128]{2,1,0:T(8,128)(2,1)S(1)}, u32[]{:S(2)}) copy-start(bf16[8,272,128]{2,1,0:T(8,128)(2,1)S(1)} %collective-permute-done.9.refs_11_) | copy-start | bytes 1671172
  19.8 13.1 %collective-permute-start.10 = (bf16[8,272,128]{2,1,0:T(8,128)(2,1)S(1)}, bf16[8,272,128]{2,1,0:T(8,128)(2,1)}, u32[]{:S(2)}, u32[]{:S(2)}) collective-permute-start(bf16[8,272,128]{2,1,0:T(8,128)(2,1)S(1)} %collective-permute-done.9.refs_11_), channel_id=1, source_target_pairs={{0,32},{1,97},{2,34},{3,99},{4,36},{5,101},{6,38},{7,103},{8,40},{... | collective-permute-start | bytes 1671176 | tf_op jit(solution)/shard_map/ppermute | solution.py:564
  21.2 1.2 copy-start.11
  22.4 22.7 %collective-permute-start.11 = (bf16[16,272,128]{2,1,0:T(8,128)(2,1)}, bf16[16,272,128]{2,1,0:T(8,128)(2,1)S(1)}, u32[]{:S(2)}, u32[]{:S(2)}) collective-permute-start(bf16[16,272,128]{2,1,0:T(8,128)(2,1)} %pad_maximum_fusion), channel_id=1, source_target_pairs={{0,1},{1,0},{2,3},{3,2},{4,5},{5,4},{6,7},{7,6},{8,9},{9,8},{10,11... | collective-permute-start | bytes 3342344 | tf_op jit(solution)/shard_map/ppermute | solution.py:564
  24.8 7.1 %collective-permute-start.1 = (bf16[2,400,256]{2,1,0:T(8,128)(2,1)S(1)}, bf16[2,400,256]{2,1,0:T(8,128)(2,1)S(1)}, u32[]{:S(2)}, u32[]{:S(2)}) collective-permute-start(bf16[2,400,256]{2,1,0:T(8,128)(2,1)S(1)} %pad_maximum_fusion.1.refs_1_), channel_id=1, source_target_pairs={{0,2},{1,9},{2,0},{3,11},{4,6},{5,13},{6,4},{7,15},{8,10},{9,1},{1... | collective-permute-start | bytes 1228808 | tf_op jit(solution)/shard_map/ppermute | solution.py:564
  24.8 8.0 %copy-start.17 = (bf16[2,400,256]{2,1,0:T(8,128)(2,1)}, bf16[2,400,256]{2,1,0:T(8,128)(2,1)S(1)}, u32[]{:S(2)}) copy-start(bf16[2,400,256]{2,1,0:T(8,128)(2,1)S(1)} %collective-permute-done.4.refs_5_) | copy-start | bytes 1228804
  24.9 8.7 %collective-permute-start.6 = (bf16[2,400,256]{2,1,0:T(8,128)(2,1)S(1)}, bf16[2,400,256]{2,1,0:T(8,128)(2,1)S(1)}, u32[]{:S(2)}, u32[]{:S(2)}) collective-permute-start(bf16[2,400,256]{2,1,0:T(8,128)(2,1)S(1)} %collective-permute-done.4.refs_5_), channel_id=1, source_target_pairs={{0,6},{1,25},{2,4},{3,27},{4,2},{5,29},{6,0},{7,31},{8,14},{9,17},... | collective-permute-start | bytes 1228808 | tf_op jit(solution)/shard_map/ppermute | solution.py:564
  27.9 8.5 %collective-permute-start.5 = (bf16[2,400,256]{2,1,0:T(8,128)(2,1)S(1)}, bf16[2,400,256]{2,1,0:T(8,128)(2,1)}, u32[]{:S(2)}, u32[]{:S(2)}) collective-permute-start(bf16[2,400,256]{2,1,0:T(8,128)(2,1)S(1)} %collective-permute-done.4.refs_5_), channel_id=1, source_target_pairs={{0,2},{1,9},{2,0},{3,11},{4,6},{5,13},{6,4},{7,15},{8,10},{9,1},{1... | collective-permute-start | bytes 1228808 | tf_op jit(solution)/shard_map/ppermute | solution.py:564
  31.9 4.5 %copy-start.18 = (bf16[2,400,256]{2,1,0:T(8,128)(2,1)}, bf16[2,400,256]{2,1,0:T(8,128)(2,1)S(1)}, u32[]{:S(2)}) copy-start(bf16[2,400,256]{2,1,0:T(8,128)(2,1)S(1)} %collective-permute-done.1.refs_2_) | copy-start | bytes 1228804
  31.9 8.9 %collective-permute-start.12 = (bf16[8,272,128]{2,1,0:T(8,128)(2,1)S(1)}, bf16[8,272,128]{2,1,0:T(8,128)(2,1)S(1)}, u32[]{:S(2)}, u32[]{:S(2)}) collective-permute-start(bf16[8,272,128]{2,1,0:T(8,128)(2,1)S(1)} %collective-permute-done.9.refs_11_), channel_id=1, source_target_pairs={{0,1},{1,0},{2,3},{3,2},{4,5},{5,4},{6,7},{7,6},{8,9},{9,8},{10,11... | collective-permute-start | bytes 1671176 | tf_op jit(solution)/shard_map/ppermute | solution.py:564
  32.9 12.2 %collective-permute-start.13 = (bf16[8,272,128]{2,1,0:T(8,128)(2,1)}, bf16[8,272,128]{2,1,0:T(8,128)(2,1)S(1)}, u32[]{:S(2)}, u32[]{:S(2)}) collective-permute-start(bf16[8,272,128]{2,1,0:T(8,128)(2,1)} %collective-permute-done.10.refs_12_), channel_id=1, source_target_pairs={{0,1},{1,0},{2,3},{3,2},{4,5},{5,4},{6,7},{7,6},{8,9},{9,8},{10,11... | collective-permute-start | bytes 1671176 | tf_op jit(solution)/shard_map/ppermute | solution.py:564
  33.6 4.1 %copy-start.19 = (bf16[2,400,256]{2,1,0:T(8,128)(2,1)}, bf16[2,400,256]{2,1,0:T(8,128)(2,1)S(1)}, u32[]{:S(2)}) copy-start(bf16[2,400,256]{2,1,0:T(8,128)(2,1)S(1)} %collective-permute-done.6.refs_7_) | copy-start | bytes 1228804
  33.6 7.3 %collective-permute-start.3 = (bf16[2,400,256]{2,1,0:T(8,128)(2,1)}, bf16[2,400,256]{2,1,0:T(8,128)(2,1)S(1)}, u32[]{:S(2)}, u32[]{:S(2)}) collective-permute-start(bf16[2,400,256]{2,1,0:T(8,128)(2,1)} %collective-permute-done.2.refs_3_), channel_id=1, source_target_pairs={{0,2},{1,9},{2,0},{3,11},{4,6},{5,13},{6,4},{7,15},{8,10},{9,1},{1... | collective-permute-start | bytes 1228808 | tf_op jit(solution)/shard_map/ppermute | solution.py:564
  36.4 8.6 %collective-permute-start.7 = (bf16[2,400,256]{2,1,0:T(8,128)(2,1)}, bf16[2,400,256]{2,1,0:T(8,128)(2,1)}, u32[]{:S(2)}, u32[]{:S(2)}) collective-permute-start(bf16[2,400,256]{2,1,0:T(8,128)(2,1)} %collective-permute-done.5.refs_6_), channel_id=1, source_target_pairs={{0,6},{1,25},{2,4},{3,27},{4,2},{5,29},{6,0},{7,31},{8,14},{9,17},... | collective-permute-start | bytes 1228808 | tf_op jit(solution)/shard_map/ppermute | solution.py:564
  40.9 4.2 %copy-start.20 = (bf16[2,400,256]{2,1,0:T(8,128)(2,1)}, bf16[2,400,256]{2,1,0:T(8,128)(2,1)S(1)}, u32[]{:S(2)}) copy-start(bf16[2,400,256]{2,1,0:T(8,128)(2,1)S(1)} %collective-permute-done.3.refs_4_) | copy-start | bytes 1228804
  40.9 4.2 %copy-start.15 = (bf16[8,272,128]{2,1,0:T(8,128)(2,1)}, bf16[8,272,128]{2,1,0:T(8,128)(2,1)S(1)}, u32[]{:S(2)}) copy-start(bf16[8,272,128]{2,1,0:T(8,128)(2,1)S(1)} %collective-permute-done.12.refs_14_) | copy-start | bytes 1671172
  113.4 2.2 copy-start
  115.6 1.9 copy-start.2
  118.9 57.3 %copy-start.1 = (bf16[64,256,128]{2,1,0:T(8,128)(2,1)S(1)}, bf16[64,256,128]{2,1,0:T(8,128)(2,1)}, u32[]{:S(2)}) copy-start(bf16[64,256,128]{2,1,0:T(8,128)(2,1)} %get-tuple-element.18.y_ref) | copy-start | bytes 12582916
  118.9 57.3 %copy-start.3 = (bf16[16,384,256]{2,1,0:T(8,128)(2,1)S(1)}, bf16[16,384,256]{2,1,0:T(8,128)(2,1)}, u32[]{:S(2)}) copy-start(bf16[16,384,256]{2,1,0:T(8,128)(2,1)} %get-tuple-element.17.x_ref) | copy-start | bytes 9437188
  118.9 57.3 %copy-start.6 = (f32[80,128]{1,0:T(8,128)S(1)}, f32[80,128]{1,0:T(8,128)}, u32[]{:S(2)}) copy-start(f32[80,128]{1,0:T(8,128)} %get-tuple-element.20.side_ref) | copy-start | bytes 122884
  176.1 59.9 %copy-start.5 = (f32[64,128]{1,0:T(8,128)S(1)}, f32[64,128]{1,0:T(8,128)}, u32[]{:S(2)}) copy-start(f32[64,128]{1,0:T(8,128)} %get-tuple-element.19.side_ref) | copy-start | bytes 98308
  176.2 59.9 %copy-start.8 = (s32[280]{0:T(512)S(1)}, s32[280]{0:T(512)}, u32[]{:S(2)}) copy-start(s32[280]{0:T(512)} %get-tuple-element.16.item_ref) | copy-start | bytes 3364
  176.2 59.9 %copy-start.9 = (f32[3,128]{1,0:T(4,128)S(1)}, f32[3,128]{1,0:T(4,128)}, u32[]{:S(2)}) copy-start(f32[3,128]{1,0:T(4,128)} %get-tuple-element.22.norm_ref) | copy-start | bytes 4612
  236.1 53.2 %copy-start.21 = (f32[8,128]{1,0:T(8,128)S(1)}, f32[8,128]{1,0:T(8,128)}, u32[]{:S(2)}) copy-start(f32[8,128]{1,0:T(8,128)} %get-tuple-element.24) | copy-start | bytes 12292
  (4 other events, 3.4 us)

commit v4 on v3

--- a/solution.py
+++ b/solution.py
@@ -20,7 +20,8 @@
 ROWS = ("y", "z")
 COLS = ("x", "core")
 N_ROWS = 16
-N_PIECES = 15
+N_PIECES = 8
+N_COPIES = 12
 N_COLS = 8
 RING = 4
 SRC = 384
@@ -29,8 +30,7 @@
 FEAT = 256
 TILES = N_COLS * TSUB
 SLOTS = N_ROWS * N_COLS * CAP
-ROW_UNROLL = 8
-COL_UNROLL = 16
+UNROLL = 16
 LAST_UNROLL = 4
 EXTRA = 16
 LISTED = 8 + SLOTS + 4 * LAST_UNROLL
@@ -92,7 +92,7 @@
     return jnp.concatenate([y_ref[r0], y_ref[r1]], axis=1)
 
 
-def sweep(n_items, work, many):
+def sweep(n_items, work):
     def steps(first, size):
         def step(w, _):
             for k in range(size):
@@ -101,11 +101,11 @@
 
         return step
 
-    whole = lax.div(n_items, many)
-    lax.fori_loop(0, whole, steps(0, many), 0)
-    left = n_items - many * whole
+    whole = lax.div(n_items, UNROLL)
+    lax.fori_loop(0, whole, steps(0, UNROLL), 0)
+    left = n_items - UNROLL * whole
     lax.fori_loop(
-        0, lax.div(left + LAST_UNROLL - 1, LAST_UNROLL), steps(many * whole, LAST_UNROLL), 0
+        0, lax.div(left + LAST_UNROLL - 1, LAST_UNROLL), steps(UNROLL * whole, LAST_UNROLL), 0
     )
 
 
@@ -189,9 +189,10 @@
 def piece_copies(x_refs, y_refs, xs, ys, x_rows, y_rows):
     pairs = []
     for half in range(2):
-        for later in range(RING):
-            place = pl.ds(RING * later + 2 * half, 2)
-            pairs.append((x_refs[RING * half + later].at[:, x_rows, :], xs.at[place]))
+        for k in range(RING):
+            later = k if half == 0 else (0, 2, 1, 3)[k]
+            piece = x_refs[2 * half + k // 2].at[pl.ds(2 * (k % 2), 2), x_rows, :]
+            pairs.append((piece, xs.at[pl.ds(RING * later + 2 * half, 2)]))
     start = 0
     for piece in y_refs:
         pairs.append((piece.at[:, y_rows, :], ys.at[pl.ds(start, piece.shape[0])]))
@@ -201,7 +202,7 @@
 
 def first_kernel(*refs):
     at_ref, pieces = refs[0], refs[1 : 1 + N_PIECES]
-    x_refs, y_refs = pieces[: 2 * RING], pieces[2 * RING :]
+    x_refs, y_refs = pieces[:RING], pieces[RING:]
     out_ref, item_ref, cols_ref, rows_ref, xs_out, ys_out = refs[1 + N_PIECES : 7 + N_PIECES]
     a_buf, u_buf, acc, top, xs, ys, sems = refs[7 + N_PIECES : 14 + N_PIECES]
     a_ref, table, numbers, x_extra, y_extra, small_sems, sem, out_sems = refs[14 + N_PIECES :]
@@ -315,12 +316,13 @@
             e = exps(x_ref[h], two_tiles(y_ref, r0, r1))
             acc[s] += e[:, :TILE] * u0 + e[:, TILE:] * u1
 
-        sweep(n_items, work, ROW_UNROLL)
+        sweep(n_items, work)
         for k in range(N_ROWS * SUBS):
             s, b = k // SUBS, k % SUBS
             col = jnp.sum(acc[s, b * TILE : (b + 1) * TILE, :], axis=1, keepdims=True)
-            done = mid + jnp.log(as_row(eye, col))
-            out_ref[:, k : k + 1, :] = jnp.broadcast_to(done[None], (N_ROWS, 1, TILE))
+            a_buf[k : k + 1, :] = as_row(eye, col)
+        done = mid + jnp.log(a_buf[0 : N_ROWS * SUBS])
+        out_ref[...] = jnp.broadcast_to(done[None], out_ref.shape)
 
     @pl.when(jnp.logical_not(fast))
     def _():
@@ -399,7 +401,7 @@
             acc[t0] += jnp.sum((e[:, :TILE] * v).reshape(SRC // 8, 8, TILE), axis=0)
             acc[t1] += jnp.sum((e[:, TILE:] * v).reshape(SRC // 8, 8, TILE), axis=0)
 
-        sweep(n_items, work, COL_UNROLL)
+        sweep(n_items, work)
         done = mid + jnp.log(jnp.sum(acc[0:TILES], axis=1))
         out_ref[...] = jnp.broadcast_to(done[None], out_ref.shape)
 
@@ -501,13 +503,13 @@
         + [
             pltpu.VMEM((N_ROWS, SRC, FEAT), jnp.bfloat16),
             pltpu.VMEM((TILES, FEAT, TILE), jnp.bfloat16),
-            pltpu.SemaphoreType.DMA((N_PIECES,)),
+            pltpu.SemaphoreType.DMA((N_COPIES,)),
             pltpu.VMEM((TILES, TILE), jnp.float32),
             pltpu.VMEM((N_ROWS, 8, TILE), jnp.int32),
             pltpu.SMEM((N_ROWS, 8, TILE), jnp.int32),
             pltpu.VMEM((N_ROWS, EXTRA, FEAT), jnp.bfloat16),
             pltpu.VMEM((TILES, EXTRA, TILE), jnp.bfloat16),
-            pltpu.SemaphoreType.DMA((N_PIECES,)),
+            pltpu.SemaphoreType.DMA((N_COPIES,)),
             pltpu.SemaphoreType.DMA,
             pltpu.SemaphoreType.DMA((2,)),
         ],
@@ -564,20 +566,22 @@
     return lax.ppermute(block, NAMES, pairs)
 
 
-def gather_ring(block, one, two):
-    first = exchange(block, one)
-    second = exchange(block, two)
-    return [block, first, second, exchange(second, one)]
+def doubled(block, partner):
+    return jnp.concatenate([block, exchange(block, partner)])
 
 
 def gather_sources(block):
-    pair = jnp.stack([block, exchange(block, source_partner(0, 1))])
+    pair = doubled(block[None], source_partner(0, 1))
     other = exchange(pair, source_partner(0, 3))
     one, two = source_partner(1, 1), source_partner(1, 3)
-    first, second = exchange(pair, one), exchange(pair, two)
-    pieces = [pair, first, second, exchange(second, one)]
-    first, second = exchange(other, one), exchange(other, two)
-    return pieces + [other, first, second, exchange(first, two)]
+    pair, other = doubled(pair, one), doubled(other, two)
+    return [pair, exchange(pair, two), other, exchange(other, one)]
+
+
+def gather_targets(block):
+    pair = doubled(block, target_partner(0))
+    pieces = [pair, exchange(pair, target_partner(1))]
+    return pieces + [exchange(piece, sibling) for piece in pieces]
 
 
 def source_partner(stage, flip):
@@ -607,13 +611,10 @@
         pair_tiles.T,
         pair_count.reshape(1, -1),
     )
-    xs = gather_sources(x_block)
-    near = gather_ring(y_block, target_partner(0), target_partner(1))
-    far = [exchange(jnp.concatenate(near[:2]), sibling)]
-    far += [exchange(block, sibling) for block in near[2:]]
+    pieces = gather_sources(x_block) + gather_targets(y_block)
 
     at = jnp.stack([lax.axis_index(name) for name in NAMES]).astype(jnp.int32)
-    row_parts, items, cols, rows, xs, ys = first_pass(at, xs + near + far)
+    row_parts, items, cols, rows, xs, ys = first_pass(at, pieces)
     for iteration in range(ITERS - 1):
         col_parts = col_pass(items, xs, ys, cols, swap(row_parts, ROWS))
         row_parts = row_pass(items, xs, ys, rows, swap(col_parts, COLS))

time: 295 us -> 297 us (level)
  waiting for transfers between devices: 18.3 us -> 24.9 us
  blocking collectives: 52.8 us -> 47.8 us
  Pallas kernels: 186 us -> 189 us
    ppermute x14 -> x10, waiting for transfers between devices: 18.3 us -> 24.9 us  [exchange(): return lax.ppermute(block, NAMES, pairs)]
    all_to_all x4, blocking collectives: 52.8 us -> 47.8 us  [swap(): return lax.all_to_all(blocks, axes, split_axis=0, concat_axis=0, tiled=True)]
    ppermute x14 -> x10, starting transfers between devices: 20.8 us -> 22.1 us  [exchange(): return lax.ppermute(block, NAMES, pairs)]
    unnamed x44 -> x32, local copies, waits for them, and re-layouts: 7.47 us -> 6.7 us
  transfers between devices with their start and end apart: 14 -> 10, of which waited for: 7 -> 5; matrix products, arithmetic and copies ran while one was open for 1% -> 1% of each run, Pallas kernels for 0% -> 0%
where the time goes in v4:
time: 297 us; the launch traced here: 293 us
  Pallas kernels  189 us (64%)
  blocking collectives  47.8 us (16%)
  waiting for transfers between devices  24.9 us (8%)
  starting transfers between devices  22.1 us (7%)
  local copies, waits for them, and re-layouts  6.8 us (2%)
    pallas_call x1, Pallas kernels, first_pass(): pl.pallas_call(first_kernel, out_shape=(ROW_PARTS, shape((LISTED,), jnp.i...  54.1 us
    all_to_all x4, blocking collectives, swap(): return lax.all_to_all(blocks, axes, split_axis=0, concat_axis=0, tiled=True)  47.8 us
    pallas_call x1, Pallas kernels, row_pass(): pl.pallas_call(row_kernel, out_shape=ROW_PARTS, in_specs=[SMEM] + [VMEM]...  47.7 us
    pallas_call x1, Pallas kernels, last_col_pass(): pl.pallas_call(last_col_kernel, out_shape=(shape((1, TILES, TILE)), shape...  42.9 us
    pallas_call x1, Pallas kernels, col_pass(): pl.pallas_call(col_kernel, out_shape=shape((N_COLS, TILES, TILE)), in_spe...  42.3 us
    ppermute x10, waiting for transfers between devices, exchange(): return lax.ppermute(block, NAMES, pairs)  24.9 us
    ppermute x10, starting transfers between devices, exchange(): return lax.ppermute(block, NAMES, pairs)  22.1 us
    unnamed x32, local copies, waits for them, and re-layouts  6.7 us
  transfers between devices with their start and end apart: 10, of which 5 were waited for; matrix products, arithmetic and copies ran while one was open for 1% of the time, Pallas kernels for 0%

profile of v4, /device:TPU:1, one launch (start us, length us, event | category | flops | bytes accessed | tf_op | source)
XLA Modules:
  0.0 293.2 jit_solution(14434809395651523069)
XLA Ops:
  0.6 2.5 prepare.1
  3.1 3.4 %collective-permute-start.6 = (bf16[8,272,128]{2,1,0:T(8,128)(2,1)}, bf16[8,272,128]{2,1,0:T(8,128)(2,1)S(1)}, u32[]{:S(2)}, u32[]{:S(2)}) collective-permute-start(bf16[8,272,128]{2,1,0:T(8,128)(2,1)} %get-tuple-element.15), channel_id=1, source_target_pairs={{0,32},{1,97},{2,34},{3,99},{4,36},{5,101},{6,38},{7,103},{8,40},{... | collective-permute-start | bytes 1671176 | tf_op jit(solution)/shard_map/ppermute | solution.py:566
  6.5 1.1 constant_dynamic-update-slice_fusion.3
  7.6 6.0 %collective-permute-done.6 = bf16[8,272,128]{2,1,0:T(8,128)(2,1)S(1)} collective-permute-done((bf16[8,272,128]{2,1,0:T(8,128)(2,1)}, bf16[8,272,128]{2,1,0:T(8,128)(2,1)S(1)}, u32[]{:S(2)}, u32[]{:S(2)}) %collective-permute-start.6) | collective-permute-done | bytes 557088 | tf_op jit(solution)/shard_map/ppermute | solution.py:566
  13.6 0.1 constant_dynamic-update-slice_fusion.2.refs_5_
  13.7 0.6 collective-permute-start.7
  14.3 1.6 collective-permute-start
  15.9 3.5 %collective-permute-done = bf16[1,400,256]{2,1,0:T(8,128)(2,1)S(1)} collective-permute-done((bf16[1,400,256]{2,1,0:T(8,128)(2,1)S(1)}, bf16[1,400,256]{2,1,0:T(8,128)(2,1)S(1)}, u32[]{:S(2)}, u32[]{:S(2)}) %collective-permute-start) | collective-permute-done | bytes 204832 | tf_op jit(solution)/shard_map/ppermute | solution.py:566
  19.5 3.7 %collective-permute-start.3 = (bf16[2,400,256]{2,1,0:T(8,128)(2,1)S(1)}, bf16[2,400,256]{2,1,0:T(8,128)(2,1)S(1)}, u32[]{:S(2)}, u32[]{:S(2)}) collective-permute-start(bf16[2,400,256]{2,1,0:T(8,128)(2,1)S(1)} %pad_maximum_fusion.1), channel_id=1, source_target_pairs={{0,24},{1,7},{2,26},{3,5},{4,28},{5,3},{6,30},{7,1},{8,16},{9,15},... | collective-permute-start | bytes 1228808 | tf_op jit(solution)/shard_map/ppermute | solution.py:566
  23.2 1.3 collective-permute-start.1
  24.5 4.4 %collective-permute-done.3 = bf16[2,400,256]{2,1,0:T(8,128)(2,1)S(1)} collective-permute-done((bf16[2,400,256]{2,1,0:T(8,128)(2,1)S(1)}, bf16[2,400,256]{2,1,0:T(8,128)(2,1)S(1)}, u32[]{:S(2)}, u32[]{:S(2)}) %collective-permute-start.3) | collective-permute-done | bytes 409632 | tf_op jit(solution)/shard_map/ppermute | solution.py:566
  28.9 2.7 collective-permute-start.4
  31.7 5.8 %collective-permute-start.8 = (bf16[16,272,128]{2,1,0:T(8,128)(2,1)S(1)}, bf16[16,272,128]{2,1,0:T(8,128)(2,1)}, u32[]{:S(2)}, u32[]{:S(2)}) collective-permute-start(bf16[16,272,128]{2,1,0:T(8,128)(2,1)S(1)} %constant_dynamic-update-slice_fusion.2.refs_5_), channel_id=1, source_target_pairs={{0,1},{1,0},{2,3},{3,2},{4,5},{5,4},{6,7},{7,6},{8,9},{9,8},{10,11... | collective-permute-start | bytes 3342344 | tf_op jit(solution)/shard_map/ppermute | solution.py:566
  37.5 0.1 pad_maximum_fusion.refs_1_
  37.6 2.9 collective-permute-start.2
  40.5 0.1 collective-permute-start.5
  40.6 0.7 pad_add_fusion.refs_0_
  41.3 9.3 %collective-permute-done.2.refs_2_ = bf16[4,400,256]{2,1,0:T(8,128)(2,1)} collective-permute-done((bf16[4,400,256]{2,1,0:T(8,128)(2,1)S(1)}, bf16[4,400,256]{2,1,0:T(8,128)(2,1)}, u32[]{:S(2)}, u32[]{:S(2)}) %collective-permute-start.2) | collective-permute-done | bytes 819232 | tf_op jit(solution)/shard_map/ppermute | solution.py:566
  50.6 1.6 collective-permute-done.5.refs_4_
  52.2 54.1 %first_row_pass.1 = (f32[16,48,128]{2,1,0:T(8,128)}, s32[280]{0:T(512)}, f32[64,128]{1,0:T(8,128)}, f32[80,128]{1,0:T(8,128)}, bf16[16,384,256]{2,1,0:T(8,128)(2,1)}, /*index=5*/bf16[64,256,128]{2,1,0:T(8,128)(2,1)}) custom-call(s32[4]{0:T(128)} %pad_add_fusion.refs_0_, bf16[4,400,256]{2,1,0:T(8,128)(2,1)} %copy-done.10, ...), custom_call_target="tpu_custom_call" | custom-call | tf_op jit(solution)/shard_map/first_row_pass/pallas_call | solution.py:490
  106.3 14.2 %all_to_all.20.parts_ref = f32[16,48,128]{2,1,0:T(8,128)S(1)} all-to-all(f32[16,48,128]{2,1,0:T(8,128)} %get-tuple-element.21), channel_id=1, replica_groups=mesh['x'=4,'y'=4,'z'=4,'core'=2] {'y','z'}, dimensions={0} | all-to-all | bytes 786432 | tf_op jit(solution)/shard_map/all_to_all | solution.py:558
  120.5 2.2 copy-done
  122.7 1.9 copy-done.2
  124.6 0.8 copy-done.4
  125.4 0.7 copy-done.7
  126.0 42.3 %col_pass.1 = f32[8,64,128]{2,1,0:T(8,128)S(1)} custom-call(s32[280]{0:T(512)S(1)} %copy-done.7, bf16[16,384,256]{2,1,0:T(8,128)(2,1)S(1)} %copy-done.2, bf16[64,256,128]{2,1,0:T(8,128)(2,1)S(1)} %copy-done, f32[64,128]{1,0:T(8,128)S(1)} %copy-done.4, f32[16,48,128]{2,1,0:T(8,128)S(1)} %all_to_all.20.parts_ref), custom_call_target="tpu_custom_call" | custom-call | tf_op jit(solution)/shard_map/col_pass/pallas_call | solution.py:534
  168.3 9.6 %all_to_all.21.parts_ref = f32[8,64,128]{2,1,0:T(8,128)S(1)} all-to-all(f32[8,64,128]{2,1,0:T(8,128)S(1)} %col_pass.1), channel_id=1, replica_groups=mesh['x'=4,'y'=4,'z'=4,'core'=2] {'x','core'}, dimensions={0} | all-to-all | bytes 524288 | tf_op jit(solution)/shard_map/all_to_all | solution.py:558
  177.9 47.7 %row_pass.1 = f32[16,48,128]{2,1,0:T(8,128)S(1)} custom-call(s32[280]{0:T(512)S(1)} %copy-done.7, bf16[16,384,256]{2,1,0:T(8,128)(2,1)S(1)} %copy-done.3, bf16[64,256,128]{2,1,0:T(8,128)(2,1)S(1)} %copy-done.1, f32[80,128]{1,0:T(8,128)S(1)} %copy-done.6, f32[8,64,128]{2,1,0:T(8,128)S(1)} %all_to_all.21.parts_ref), custom_call_target="tpu_custom_call" | custom-call | tf_op jit(solution)/shard_map/row_pass/pallas_call | solution.py:522
  225.7 15.7 %all_to_all.22.parts_ref = f32[16,48,128]{2,1,0:T(8,128)S(1)} all-to-all(f32[16,48,128]{2,1,0:T(8,128)S(1)} %row_pass.1), channel_id=1, replica_groups=mesh['x'=4,'y'=4,'z'=4,'core'=2] {'y','z'}, dimensions={0} | all-to-all | bytes 786432 | tf_op jit(solution)/shard_map/all_to_all | solution.py:558
  241.4 42.9 %last_col_pass.1 = (f32[1,64,128]{2,1,0:T(8,128)S(1)}, f32[3,128]{1,0:T(4,128)}) custom-call(s32[280]{0:T(512)S(1)} %copy-done.8, bf16[16,384,256]{2,1,0:T(8,128)(2,1)S(1)} %copy-done.3, bf16[64,256,128]{2,1,0:T(8,128)(2,1)S(1)} %copy-done.1, f32[64,128]{1,0:T(8,128)S(1)} %copy-done.5, f32[16,48,128]{2,1,0:T(8,128)S(1)} %all_to_all.22.parts_ref, ...), custom_call_target="tpu_custom_call" | custom-call | tf_op jit(solution)/shard_map/last_col_pass/pallas_call | solution.py:546
  284.2 8.4 %all_to_all.23 = f32[8,8,128]{2,1,0:T(8,128)S(1)} all-to-all(f32[8,8,128]{2,1,0:T(8,128)S(1)} %bitcast.14), channel_id=1, replica_groups=mesh['x'=4,'y'=4,'z'=4,'core'=2] {'x','core'}, dimensions={0} | all-to-all | bytes 65536 | tf_op jit(solution)/shard_map/all_to_all | solution.py:558
  292.6 0.6 subtract_bitcast_fusion
  (38 shorter events, 0.2 us)
Async XLA Ops:
  3.1 11.2 %copy-start.13 = (bf16[400,256]{1,0:T(8,128)(2,1)S(1)}, bf16[400,256]{1,0:T(8,128)(2,1)}, u32[]{:S(2)}) copy-start(bf16[400,256]{1,0:T(8,128)(2,1)} %get-tuple-element.14) | copy-start | bytes 614404
  3.1 10.5 %collective-permute-start.6 = (bf16[8,272,128]{2,1,0:T(8,128)(2,1)}, bf16[8,272,128]{2,1,0:T(8,128)(2,1)S(1)}, u32[]{:S(2)}, u32[]{:S(2)}) collective-permute-start(bf16[8,272,128]{2,1,0:T(8,128)(2,1)} %get-tuple-element.15), channel_id=1, source_target_pairs={{0,32},{1,97},{2,34},{3,99},{4,36},{5,101},{6,38},{7,103},{8,40},{... | collective-permute-start | bytes 1671176 | tf_op jit(solution)/shard_map/ppermute | solution.py:566
  13.7 23.9 %copy-start.11 = (bf16[16,272,128]{2,1,0:T(8,128)(2,1)}, bf16[16,272,128]{2,1,0:T(8,128)(2,1)S(1)}, u32[]{:S(2)}) copy-start(bf16[16,272,128]{2,1,0:T(8,128)(2,1)S(1)} %constant_dynamic-update-slice_fusion.2.refs_5_) | copy-start | bytes 3342340
  13.7 23.7 %collective-permute-start.7 = (bf16[16,272,128]{2,1,0:T(8,128)(2,1)S(1)}, bf16[16,272,128]{2,1,0:T(8,128)(2,1)}, u32[]{:S(2)}, u32[]{:S(2)}) collective-permute-start(bf16[16,272,128]{2,1,0:T(8,128)(2,1)S(1)} %constant_dynamic-update-slice_fusion.2.refs_5_), channel_id=1, source_target_pairs={{0,96},{1,33},{2,98},{3,35},{4,100},{5,37},{6,102},{7,39},{8,104},... | collective-permute-start | bytes 3342344 | tf_op jit(solution)/shard_map/ppermute | solution.py:566
  14.3 5.2 %collective-permute-start = (bf16[1,400,256]{2,1,0:T(8,128)(2,1)S(1)}, bf16[1,400,256]{2,1,0:T(8,128)(2,1)S(1)}, u32[]{:S(2)}, u32[]{:S(2)}) collective-permute-start(bf16[1,400,256]{2,1,0:T(8,128)(2,1)S(1)} %bitcast.15), channel_id=1, source_target_pairs={{0,8},{1,3},{2,10},{3,1},{4,12},{5,7},{6,14},{7,5},{8,0},{9,11},{1... | collective-permute-start | bytes 614408 | tf_op jit(solution)/shard_map/ppermute | solution.py:566
  19.5 9.4 %collective-permute-start.3 = (bf16[2,400,256]{2,1,0:T(8,128)(2,1)S(1)}, bf16[2,400,256]{2,1,0:T(8,128)(2,1)S(1)}, u32[]{:S(2)}, u32[]{:S(2)}) collective-permute-start(bf16[2,400,256]{2,1,0:T(8,128)(2,1)S(1)} %pad_maximum_fusion.1), channel_id=1, source_target_pairs={{0,24},{1,7},{2,26},{3,5},{4,28},{5,3},{6,30},{7,1},{8,16},{9,15},... | collective-permute-start | bytes 1228808 | tf_op jit(solution)/shard_map/ppermute | solution.py:566
  23.2 14.3 %collective-permute-start.1 = (bf16[2,400,256]{2,1,0:T(8,128)(2,1)S(1)}, bf16[2,400,256]{2,1,0:T(8,128)(2,1)S(1)}, u32[]{:S(2)}, u32[]{:S(2)}) collective-permute-start(bf16[2,400,256]{2,1,0:T(8,128)(2,1)S(1)} %pad_maximum_fusion.1), channel_id=1, source_target_pairs={{0,2},{1,9},{2,0},{3,11},{4,6},{5,13},{6,4},{7,15},{8,10},{9,1},{1... | collective-permute-start | bytes 1228808 | tf_op jit(solution)/shard_map/ppermute | solution.py:566
  28.9 11.6 %collective-permute-start.4 = (bf16[2,400,256]{2,1,0:T(8,128)(2,1)S(1)}, bf16[2,400,256]{2,1,0:T(8,128)(2,1)S(1)}, u32[]{:S(2)}, u32[]{:S(2)}) collective-permute-start(bf16[2,400,256]{2,1,0:T(8,128)(2,1)S(1)} %collective-permute-done.3), channel_id=1, source_target_pairs={{0,6},{1,25},{2,4},{3,27},{4,2},{5,29},{6,0},{7,31},{8,14},{9,17},... | collective-permute-start | bytes 1228808 | tf_op jit(solution)/shard_map/ppermute | solution.py:566
  31.7 18.9 %collective-permute-start.8 = (bf16[16,272,128]{2,1,0:T(8,128)(2,1)S(1)}, bf16[16,272,128]{2,1,0:T(8,128)(2,1)}, u32[]{:S(2)}, u32[]{:S(2)}) collective-permute-start(bf16[16,272,128]{2,1,0:T(8,128)(2,1)S(1)} %constant_dynamic-update-slice_fusion.2.refs_5_), channel_id=1, source_target_pairs={{0,1},{1,0},{2,3},{3,2},{4,5},{5,4},{6,7},{7,6},{8,9},{9,8},{10,11... | collective-permute-start | bytes 3342344 | tf_op jit(solution)/shard_map/ppermute | solution.py:566
  37.5 14.8 %collective-permute-start.9 = (bf16[16,272,128]{2,1,0:T(8,128)(2,1)}, bf16[16,272,128]{2,1,0:T(8,128)(2,1)}, u32[]{:S(2)}, u32[]{:S(2)}) collective-permute-start(bf16[16,272,128]{2,1,0:T(8,128)(2,1)} %collective-permute-done.7.refs_6_), channel_id=1, source_target_pairs={{0,1},{1,0},{2,3},{3,2},{4,5},{5,4},{6,7},{7,6},{8,9},{9,8},{10,11... | collective-permute-start | bytes 3342344 | tf_op jit(solution)/shard_map/ppermute | solution.py:566
  37.6 14.7 %copy-start.10 = (bf16[4,400,256]{2,1,0:T(8,128)(2,1)}, bf16[4,400,256]{2,1,0:T(8,128)(2,1)S(1)}, u32[]{:S(2)}) copy-start(bf16[4,400,256]{2,1,0:T(8,128)(2,1)S(1)} %pad_maximum_fusion.refs_1_) | copy-start | bytes 2457604
  37.6 13.0 %collective-permute-start.2 = (bf16[4,400,256]{2,1,0:T(8,128)(2,1)S(1)}, bf16[4,400,256]{2,1,0:T(8,128)(2,1)}, u32[]{:S(2)}, u32[]{:S(2)}) collective-permute-start(bf16[4,400,256]{2,1,0:T(8,128)(2,1)S(1)} %pad_maximum_fusion.refs_1_), channel_id=1, source_target_pairs={{0,6},{1,25},{2,4},{3,27},{4,2},{5,29},{6,0},{7,31},{8,14},{9,17},... | collective-permute-start | bytes 2457608 | tf_op jit(solution)/shard_map/ppermute | solution.py:566
  40.5 11.7 %copy-start.12 = (bf16[4,400,256]{2,1,0:T(8,128)(2,1)}, bf16[4,400,256]{2,1,0:T(8,128)(2,1)S(1)}, u32[]{:S(2)}) copy-start(bf16[4,400,256]{2,1,0:T(8,128)(2,1)S(1)} %constant_dynamic-update-slice_fusion.refs_3_) | copy-start | bytes 2457604
  40.5 11.7 %collective-permute-start.5 = (bf16[4,400,256]{2,1,0:T(8,128)(2,1)S(1)}, bf16[4,400,256]{2,1,0:T(8,128)(2,1)}, u32[]{:S(2)}, u32[]{:S(2)}) collective-permute-start(bf16[4,400,256]{2,1,0:T(8,128)(2,1)S(1)} %constant_dynamic-update-slice_fusion.refs_3_), channel_id=1, source_target_pairs={{0,2},{1,9},{2,0},{3,11},{4,6},{5,13},{6,4},{7,15},{8,10},{9,1},{1... | collective-permute-start | bytes 2457608 | tf_op jit(solution)/shard_map/ppermute | solution.py:566
  120.5 2.2 copy-start
  122.7 1.9 copy-start.2
  124.6 0.8 copy-start.4
  125.4 0.7 copy-start.7
  126.0 51.9 %copy-start.1 = (bf16[64,256,128]{2,1,0:T(8,128)(2,1)S(1)}, bf16[64,256,128]{2,1,0:T(8,128)(2,1)}, u32[]{:S(2)}) copy-start(bf16[64,256,128]{2,1,0:T(8,128)(2,1)} %get-tuple-element.18.y_ref) | copy-start | bytes 12582916
  126.0 51.9 %copy-start.3 = (bf16[16,384,256]{2,1,0:T(8,128)(2,1)S(1)}, bf16[16,384,256]{2,1,0:T(8,128)(2,1)}, u32[]{:S(2)}) copy-start(bf16[16,384,256]{2,1,0:T(8,128)(2,1)} %get-tuple-element.17.x_ref) | copy-start | bytes 9437188
  126.0 51.9 %copy-start.6 = (f32[80,128]{1,0:T(8,128)S(1)}, f32[80,128]{1,0:T(8,128)}, u32[]{:S(2)}) copy-start(f32[80,128]{1,0:T(8,128)} %get-tuple-element.20.side_ref) | copy-start | bytes 122884
  177.9 63.5 %copy-start.5 = (f32[64,128]{1,0:T(8,128)S(1)}, f32[64,128]{1,0:T(8,128)}, u32[]{:S(2)}) copy-start(f32[64,128]{1,0:T(8,128)} %get-tuple-element.19.side_ref) | copy-start | bytes 98308
  177.9 63.4 %copy-start.8 = (s32[280]{0:T(512)S(1)}, s32[280]{0:T(512)}, u32[]{:S(2)}) copy-start(s32[280]{0:T(512)} %get-tuple-element.16.item_ref) | copy-start | bytes 3364
  177.9 63.4 %copy-start.9 = (f32[3,128]{1,0:T(4,128)S(1)}, f32[3,128]{1,0:T(4,128)}, u32[]{:S(2)}) copy-start(f32[3,128]{1,0:T(4,128)} %get-tuple-element.22.norm_ref) | copy-start | bytes 4612
  241.3 51.3 %copy-start.14 = (f32[8,128]{1,0:T(8,128)S(1)}, f32[8,128]{1,0:T(8,128)}, u32[]{:S(2)}) copy-start(f32[8,128]{1,0:T(8,128)} %get-tuple-element.24) | copy-start | bytes 12292

commit v5 on v4

--- a/solution.py
+++ b/solution.py
@@ -20,8 +20,7 @@
 ROWS = ("y", "z")
 COLS = ("x", "core")
 N_ROWS = 16
-N_PIECES = 8
-N_COPIES = 12
+N_PIECES = 12
 N_COLS = 8
 RING = 4
 SRC = 384
@@ -189,10 +188,9 @@
 def piece_copies(x_refs, y_refs, xs, ys, x_rows, y_rows):
     pairs = []
     for half in range(2):
-        for k in range(RING):
-            later = k if half == 0 else (0, 2, 1, 3)[k]
-            piece = x_refs[2 * half + k // 2].at[pl.ds(2 * (k % 2), 2), x_rows, :]
-            pairs.append((piece, xs.at[pl.ds(RING * later + 2 * half, 2)]))
+        for later in range(RING):
+            place = pl.ds(RING * later + 2 * half, 2)
+            pairs.append((x_refs[RING * half + later].at[:, x_rows, :], xs.at[place]))
     start = 0
     for piece in y_refs:
         pairs.append((piece.at[:, y_rows, :], ys.at[pl.ds(start, piece.shape[0])]))
@@ -202,10 +200,10 @@
 
 def first_kernel(*refs):
     at_ref, pieces = refs[0], refs[1 : 1 + N_PIECES]
-    x_refs, y_refs = pieces[:RING], pieces[RING:]
-    out_ref, item_ref, cols_ref, rows_ref, xs_out, ys_out = refs[1 + N_PIECES : 7 + N_PIECES]
-    a_buf, u_buf, acc, top, xs, ys, sems = refs[7 + N_PIECES : 14 + N_PIECES]
-    a_ref, table, numbers, x_extra, y_extra, small_sems, sem, out_sems = refs[14 + N_PIECES :]
+    x_refs, y_refs = pieces[: 2 * RING], pieces[2 * RING :]
+    out_ref, item_ref, cols_ref, rows_ref, xs, ys = refs[1 + N_PIECES : 7 + N_PIECES]
+    a_buf, u_buf, acc, top, sems = refs[7 + N_PIECES : 12 + N_PIECES]
+    a_ref, table, numbers, x_extra, y_extra, small_sems, sem = refs[12 + N_PIECES :]
     la_ref, lb_ref = cols_ref.at[NORMS:], rows_ref.at[NORMS:]
     x, y, z, core = (at_ref[k] for k in range(4))
 
@@ -287,10 +285,7 @@
     item_ref[1] = RING * y + z
     for copy in large:
         copy.wait()
-    outward = start_all([(xs, xs_out), (ys, ys_out)], out_sems)
     row_core(a_ref[...], item_ref, xs, ys, cols_ref, out_ref, a_buf, u_buf, acc, top)
-    for copy in outward:
-        copy.wait()
 
 
 def row_kernel(item_ref, x_ref, y_ref, side_ref, parts_ref, out_ref, a_buf, u_buf, acc, top):
@@ -498,24 +493,21 @@
             shape((TILES, FEAT, TILE), jnp.bfloat16),
         ),
         in_specs=[SMEM] + [ANY] * N_PIECES,
-        out_specs=(VMEM, SMEM, VMEM, VMEM, ANY, ANY),
+        out_specs=(VMEM, SMEM, VMEM, VMEM, VMEM, VMEM),
         scratch_shapes=ROW_SCRATCH
         + [
-            pltpu.VMEM((N_ROWS, SRC, FEAT), jnp.bfloat16),
-            pltpu.VMEM((TILES, FEAT, TILE), jnp.bfloat16),
-            pltpu.SemaphoreType.DMA((N_COPIES,)),
+            pltpu.SemaphoreType.DMA((N_PIECES,)),
             pltpu.VMEM((TILES, TILE), jnp.float32),
             pltpu.VMEM((N_ROWS, 8, TILE), jnp.int32),
             pltpu.SMEM((N_ROWS, 8, TILE), jnp.int32),
             pltpu.VMEM((N_ROWS, EXTRA, FEAT), jnp.bfloat16),
             pltpu.VMEM((TILES, EXTRA, TILE), jnp.bfloat16),
-            pltpu.SemaphoreType.DMA((N_COPIES,)),
+            pltpu.SemaphoreType.DMA((N_PIECES,)),
             pltpu.SemaphoreType.DMA,
-            pltpu.SemaphoreType.DMA((2,)),
         ],
-        compiler_params=limit(60),
+        compiler_params=limit(24),
         name="first_row_pass",
-    )(at, *pieces)
+    )(at, *[pltpu.with_memory_space_constraint(piece, pltpu.HBM) for piece in pieces])
 
 
 def row_pass(items, *operands):
@@ -570,18 +562,27 @@
     return jnp.concatenate([block, exchange(block, partner)])
 
 
-def gather_sources(block):
-    pair = doubled(block[None], source_partner(0, 1))
-    other = exchange(pair, source_partner(0, 3))
-    one, two = source_partner(1, 1), source_partner(1, 3)
-    pair, other = doubled(pair, one), doubled(other, two)
-    return [pair, exchange(pair, two), other, exchange(other, one)]
-
-
-def gather_targets(block):
-    pair = doubled(block, target_partner(0))
-    pieces = [pair, exchange(pair, target_partner(1))]
-    return pieces + [exchange(piece, sibling) for piece in pieces]
+def after(value, events):
+    return lax.optimization_barrier((value, events))[0]
+
+
+def gather_all(sources, targets):
+    along = [source_partner(0, flip) for flip in (1, 3)]
+    across = [source_partner(1, flip) for flip in (1, 3)]
+    beside = [target_partner(order) for order in (0, 1)]
+
+    pair = jnp.stack([sources, exchange(sources, along[0])])
+    tiles = jnp.concatenate([targets, exchange(targets, beside[0])])
+    other = exchange(pair, along[1])
+    first, second = exchange(pair, across[0]), exchange(pair, across[1])
+    further = exchange(after(tiles, pair), beside[1])
+    relayed = exchange(first, across[1])
+    pieces = [pair, first, second, relayed]
+    near = exchange(after(tiles, (first, second)), sibling)
+    first, second = exchange(other, across[0]), exchange(other, across[1])
+    pieces += [other, first, second, exchange(second, across[0])]
+    far = exchange(after(further, (first, second)), sibling)
+    return pieces + [tiles, further, near, far]
 
 
 def source_partner(stage, flip):
@@ -611,7 +612,7 @@
         pair_tiles.T,
         pair_count.reshape(1, -1),
     )
-    pieces = gather_sources(x_block) + gather_targets(y_block)
+    pieces = gather_all(x_block, y_block)
 
     at = jnp.stack([lax.axis_index(name) for name in NAMES]).astype(jnp.int32)
     row_parts, items, cols, rows, xs, ys = first_pass(at, pieces)

time: 297 us -> 290 us (0.976); the launches traced: 293 us -> 293 us
  blocking collectives: 47.8 us -> 57.8 us
  waiting for transfers between devices: 24.9 us -> 19.3 us
  local copies, waits for them, and re-layouts: 6.8 us -> 1.96 us
  starting transfers between devices: 22.1 us -> 26.1 us
  Pallas kernels: 189 us -> 186 us
    all_to_all x4, blocking collectives: 47.8 us -> 57.8 us  [swap(): return lax.all_to_all(blocks, axes, split_axis=0, concat_axis=0, tiled=True)]
    ppermute x10 -> x12, waiting for transfers between devices: 24.9 us -> 19.3 us  [exchange(): return lax.ppermute(block, NAMES, pairs)]
    unnamed x32 -> x19, local copies, waits for them, and re-layouts: 6.7 us -> 1.88 us
    ppermute x10 -> x12, starting transfers between devices: 22.1 us -> 26.1 us  [exchange(): return lax.ppermute(block, NAMES, pairs)]
  transfers between devices with their start and end apart: 10 -> 12, of which waited for: 5 -> 7; matrix products, arithmetic and copies ran while one was open for 1% -> 0% of each run, Pallas kernels for 0% -> 0%
where the time goes in v5:
time: 290 us; the launch traced here: 293 us
  Pallas kernels  186 us (64%)
  blocking collectives  57.8 us (20%)
  starting transfers between devices  26.1 us (9%)
  waiting for transfers between devices  19.3 us (7%)
    all_to_all x4, blocking collectives, swap(): return lax.all_to_all(blocks, axes, split_axis=0, concat_axis=0, tiled=True)  57.8 us
    pallas_call x1, Pallas kernels, first_pass(): pl.pallas_call(first_kernel, out_shape=(ROW_PARTS, shape((LISTED,), jnp.i...  53.2 us
    pallas_call x1, Pallas kernels, row_pass(): pl.pallas_call(row_kernel, out_shape=ROW_PARTS, in_specs=[SMEM] + [VMEM]...  47 us
    pallas_call x1, Pallas kernels, last_col_pass(): pl.pallas_call(last_col_kernel, out_shape=(shape((1, TILES, TILE)), shape...  42 us
    pallas_call x1, Pallas kernels, col_pass(): pl.pallas_call(col_kernel, out_shape=shape((N_COLS, TILES, TILE)), in_spe...  41.4 us
    ppermute x12, starting transfers between devices, exchange(): return lax.ppermute(block, NAMES, pairs)  26.1 us
    ppermute x12, waiting for transfers between devices, exchange(): return lax.ppermute(block, NAMES, pairs)  19.3 us
  transfers between devices with their start and end apart: 12, of which 7 were waited for; matrix products, arithmetic and copies ran while one was open for 0% of the time, Pallas kernels for 0%

profile of v5, /device:TPU:1, one launch (start us, length us, event | category | flops | bytes accessed | tf_op | source)
XLA Modules:
  0.0 292.8 jit_solution(12505731441993871695)
XLA Ops:
  0.6 2.5 prepare.1
  3.1 3.4 %collective-permute-start.8 = (bf16[8,272,128]{2,1,0:T(8,128)(2,1)}, bf16[8,272,128]{2,1,0:T(8,128)(2,1)S(1)}, u32[]{:S(2)}, u32[]{:S(2)}) collective-permute-start(bf16[8,272,128]{2,1,0:T(8,128)(2,1)} %get-tuple-element.18), channel_id=1, source_target_pairs={{0,32},{1,97},{2,34},{3,99},{4,36},{5,101},{6,38},{7,103},{8,40},{... | collective-permute-start | bytes 1671176 | tf_op jit(solution)/shard_map/ppermute | solution.py:558
  6.5 1.6 collective-permute-start
  8.2 1.1 constant_dynamic-update-slice_fusion.1
  9.3 2.6 collective-permute-done
  11.9 1.8 collective-permute-done.8
  13.7 0.1 constant_dynamic-update-slice_fusion.refs_9_
  13.7 0.6 collective-permute-start.9
  14.3 3.8 %collective-permute-start.4 = (bf16[2,400,256]{2,1,0:T(8,128)(2,1)S(1)}, bf16[2,400,256]{2,1,0:T(8,128)(2,1)S(1)}, u32[]{:S(2)}, u32[]{:S(2)}) collective-permute-start(bf16[2,400,256]{2,1,0:T(8,128)(2,1)S(1)} %pad_maximum_fusion.refs_1_), channel_id=1, source_target_pairs={{0,24},{1,7},{2,26},{3,5},{4,28},{5,3},{6,30},{7,1},{8,16},{9,15},... | collective-permute-start | bytes 1228808 | tf_op jit(solution)/shard_map/ppermute | solution.py:558
  18.1 2.7 collective-permute-start.2
  20.8 2.9 collective-permute-done.4.refs_5_
  23.7 3.6 %collective-permute-start.6 = (bf16[2,400,256]{2,1,0:T(8,128)(2,1)S(1)}, bf16[2,400,256]{2,1,0:T(8,128)(2,1)}, u32[]{:S(2)}, u32[]{:S(2)}) collective-permute-start(bf16[2,400,256]{2,1,0:T(8,128)(2,1)S(1)} %collective-permute-done.4.refs_5_), channel_id=1, source_target_pairs={{0,6},{1,25},{2,4},{3,27},{4,2},{5,29},{6,0},{7,31},{8,14},{9,17},... | collective-permute-start | bytes 1228808 | tf_op jit(solution)/shard_map/ppermute | solution.py:558
  27.3 0.0 collective-permute-start.5
  27.3 3.3 %collective-permute-done.2.refs_3_ = bf16[2,400,256]{2,1,0:T(8,128)(2,1)S(1)} collective-permute-done((bf16[2,400,256]{2,1,0:T(8,128)(2,1)S(1)}, bf16[2,400,256]{2,1,0:T(8,128)(2,1)S(1)}, u32[]{:S(2)}, u32[]{:S(2)}) %collective-permute-start.2) | collective-permute-done | bytes 409632 | tf_op jit(solution)/shard_map/ppermute | solution.py:558
  30.5 0.0 collective-permute-done.1.refs_2_
  30.6 2.5 collective-permute-start.10
  33.0 1.7 collective-permute-done.6.refs_7_
  34.8 0.8 copy-done.6
  35.5 5.2 %collective-permute-start.11 = (bf16[16,272,128]{2,1,0:T(8,128)(2,1)S(1)}, bf16[16,272,128]{2,1,0:T(8,128)(2,1)}, u32[]{:S(2)}, u32[]{:S(2)}) collective-permute-start(bf16[16,272,128]{2,1,0:T(8,128)(2,1)S(1)} %collective-permute-done.9.refs_10_), channel_id=1, source_target_pairs={{0,1},{1,0},{2,3},{3,2},{4,5},{5,4},{6,7},{7,6},{8,9},{9,8},{10,11... | collective-permute-start | bytes 3342344 | tf_op jit(solution)/shard_map/ppermute | solution.py:558
  40.7 2.8 collective-permute-start.3
  43.5 0.1 pad_add_fusion.refs_0_
  43.6 5.9 %collective-permute-done.3.refs_4_ = bf16[2,400,256]{2,1,0:T(8,128)(2,1)} collective-permute-done((bf16[2,400,256]{2,1,0:T(8,128)(2,1)}, bf16[2,400,256]{2,1,0:T(8,128)(2,1)}, u32[]{:S(2)}, u32[]{:S(2)}) %collective-permute-start.3) | collective-permute-done | bytes 409632 | tf_op jit(solution)/shard_map/ppermute | solution.py:558
  49.4 1.2 collective-permute-done.7.refs_8_
  50.7 53.2 %first_row_pass.1 = (f32[16,48,128]{2,1,0:T(8,128)S(1)}, s32[280]{0:T(512)S(1)}, f32[64,128]{1,0:T(8,128)S(1)}, f32[80,128]{1,0:T(8,128)S(1)}, bf16[16,384,256]{...) custom-call(s32[4]{0:T(128)S(1)} %pad_add_fusion.refs_0_, bf16[2,400,256]{2,1,0:T(8,128)(2,1)} %copy-done.2, ...), custom_call_target="tpu_custom_call" | custom-call | tf_op jit(solution)/shard_map/first_row_pass/pallas_call | solution.py:485
  103.8 12.7 %all_to_all.20.parts_ref = f32[16,48,128]{2,1,0:T(8,128)S(1)} all-to-all(f32[16,48,128]{2,1,0:T(8,128)S(1)} %get-tuple-element.27), channel_id=1, replica_groups=mesh['x'=4,'y'=4,'z'=4,'core'=2] {'y','z'}, dimensions={0} | all-to-all | bytes 786432 | tf_op jit(solution)/shard_map/all_to_all | solution.py:550
  116.5 41.4 %col_pass.1 = f32[8,64,128]{2,1,0:T(8,128)S(1)} custom-call(s32[280]{0:T(512)S(1)} %get-tuple-element.22.item_ref, bf16[16,384,256]{2,1,0:T(8,128)(2,1)S(1)} %get-tuple-element.23.x_ref, bf16[64,256,128]{2,1,0:T(8,128)(2,1)S(1)} %get-tuple-element.24.y_ref, f32[64,128]{1,0:T(8,128)S(1)} %get-tuple-element.25.side_ref, f32[16,48,128]{2,1,0:T(8,128)S(1)} %all_to_all.20.parts_ref), custom_call_target="tpu_custom_call" | custom-call | tf_op jit(solution)/shard_map/col_pass/pallas_call | solution.py:526
  158.0 17.2 %all_to_all.21.parts_ref = f32[8,64,128]{2,1,0:T(8,128)S(1)} all-to-all(f32[8,64,128]{2,1,0:T(8,128)S(1)} %col_pass.1), channel_id=1, replica_groups=mesh['x'=4,'y'=4,'z'=4,'core'=2] {'x','core'}, dimensions={0} | all-to-all | bytes 524288 | tf_op jit(solution)/shard_map/all_to_all | solution.py:550
  175.2 47.0 %row_pass.1 = f32[16,48,128]{2,1,0:T(8,128)S(1)} custom-call(s32[280]{0:T(512)S(1)} %get-tuple-element.22.item_ref, bf16[16,384,256]{2,1,0:T(8,128)(2,1)S(1)} %get-tuple-element.23.x_ref, bf16[64,256,128]{2,1,0:T(8,128)(2,1)S(1)} %get-tuple-element.24.y_ref, f32[80,128]{1,0:T(8,128)S(1)} %get-tuple-element.26.side_ref, f32[8,64,128]{2,1,0:T(8,128)S(1)} %all_to_all.21.parts_ref), custom_call_target="tpu_custom_call" | custom-call | tf_op jit(solution)/shard_map/row_pass/pallas_call | solution.py:514
  222.2 12.4 %all_to_all.22.parts_ref = f32[16,48,128]{2,1,0:T(8,128)S(1)} all-to-all(f32[16,48,128]{2,1,0:T(8,128)S(1)} %row_pass.1), channel_id=1, replica_groups=mesh['x'=4,'y'=4,'z'=4,'core'=2] {'y','z'}, dimensions={0} | all-to-all | bytes 786432 | tf_op jit(solution)/shard_map/all_to_all | solution.py:550
  234.6 42.0 %last_col_pass.1 = (f32[1,64,128]{2,1,0:T(8,128)S(1)}, f32[3,128]{1,0:T(4,128)}) custom-call(s32[280]{0:T(512)S(1)} %get-tuple-element.22.item_ref, bf16[16,384,256]{2,1,0:T(8,128)(2,1)S(1)} %get-tuple-element.23.x_ref, bf16[64,256,128]{2,1,0:T(8,128)(2,1)S(1)} %get-tuple-element.24.y_ref, f32[64,128]{1,0:T(8,128)S(1)} %get-tuple-element.25.side_ref, ...), custom_call_target="tpu_custom_call" | custom-call | tf_op jit(solution)/shard_map/last_col_pass/pallas_call | solution.py:538
  276.6 15.6 %all_to_all.23 = f32[8,8,128]{2,1,0:T(8,128)S(1)} all-to-all(f32[8,8,128]{2,1,0:T(8,128)S(1)} %bitcast.15), channel_id=1, replica_groups=mesh['x'=4,'y'=4,'z'=4,'core'=2] {'x','core'}, dimensions={0} | all-to-all | bytes 65536 | tf_op jit(solution)/shard_map/all_to_all | solution.py:550
  292.2 0.6 subtract_bitcast_fusion
  (27 shorter events, 0.1 us)
Async XLA Ops:
  3.1 8.7 %copy-start.7 = (bf16[400,256]{1,0:T(8,128)(2,1)S(1)}, bf16[400,256]{1,0:T(8,128)(2,1)}, u32[]{:S(2)}) copy-start(bf16[400,256]{1,0:T(8,128)(2,1)} %get-tuple-element.17) | copy-start | bytes 614404
  3.1 10.5 %collective-permute-start.8 = (bf16[8,272,128]{2,1,0:T(8,128)(2,1)}, bf16[8,272,128]{2,1,0:T(8,128)(2,1)S(1)}, u32[]{:S(2)}, u32[]{:S(2)}) collective-permute-start(bf16[8,272,128]{2,1,0:T(8,128)(2,1)} %get-tuple-element.18), channel_id=1, source_target_pairs={{0,32},{1,97},{2,34},{3,99},{4,36},{5,101},{6,38},{7,103},{8,40},{... | collective-permute-start | bytes 1671176 | tf_op jit(solution)/shard_map/ppermute | solution.py:558
  6.5 5.3 %collective-permute-start = (bf16[400,256]{1,0:T(8,128)(2,1)}, bf16[400,256]{1,0:T(8,128)(2,1)S(1)}, u32[]{:S(2)}, u32[]{:S(2)}) collective-permute-start(bf16[400,256]{1,0:T(8,128)(2,1)} %get-tuple-element.17), channel_id=1, source_target_pairs={{0,8},{1,3},{2,10},{3,1},{4,12},{5,7},{6,14},{7,5},{8,0},{9,11},{1... | collective-permute-start | bytes 614408 | tf_op jit(solution)/shard_map/ppermute | solution.py:558
  11.9 38.8 %copy-start.2 = (bf16[2,400,256]{2,1,0:T(8,128)(2,1)}, bf16[2,400,256]{2,1,0:T(8,128)(2,1)S(1)}, u32[]{:S(2)}) copy-start(bf16[2,400,256]{2,1,0:T(8,128)(2,1)S(1)} %pad_maximum_fusion.refs_1_) | copy-start | bytes 1228804
  13.7 36.9 %copy-start.1 = (bf16[16,272,128]{2,1,0:T(8,128)(2,1)}, bf16[16,272,128]{2,1,0:T(8,128)(2,1)S(1)}, u32[]{:S(2)}) copy-start(bf16[16,272,128]{2,1,0:T(8,128)(2,1)S(1)} %constant_dynamic-update-slice_fusion.refs_9_) | copy-start | bytes 3342340
  13.7 21.0 %collective-permute-start.9 = (bf16[16,272,128]{2,1,0:T(8,128)(2,1)S(1)}, bf16[16,272,128]{2,1,0:T(8,128)(2,1)S(1)}, u32[]{:S(2)}, u32[]{:S(2)}) collective-permute-start(bf16[16,272,128]{2,1,0:T(8,128)(2,1)S(1)} %constant_dynamic-update-slice_fusion.refs_9_), channel_id=1, source_target_pairs={{0,96},{1,33},{2,98},{3,35},{4,100},{5,37},{6,102},{7,39},{8,104},... | collective-permute-start | bytes 3342344 | tf_op jit(solution)/shard_map/ppermute | solution.py:558
  14.3 9.4 %collective-permute-start.4 = (bf16[2,400,256]{2,1,0:T(8,128)(2,1)S(1)}, bf16[2,400,256]{2,1,0:T(8,128)(2,1)S(1)}, u32[]{:S(2)}, u32[]{:S(2)}) collective-permute-start(bf16[2,400,256]{2,1,0:T(8,128)(2,1)S(1)} %pad_maximum_fusion.refs_1_), channel_id=1, source_target_pairs={{0,24},{1,7},{2,26},{3,5},{4,28},{5,3},{6,30},{7,1},{8,16},{9,15},... | collective-permute-start | bytes 1228808 | tf_op jit(solution)/shard_map/ppermute | solution.py:558
  18.1 12.5 %collective-permute-start.2 = (bf16[2,400,256]{2,1,0:T(8,128)(2,1)S(1)}, bf16[2,400,256]{2,1,0:T(8,128)(2,1)S(1)}, u32[]{:S(2)}, u32[]{:S(2)}) collective-permute-start(bf16[2,400,256]{2,1,0:T(8,128)(2,1)S(1)} %pad_maximum_fusion.refs_1_), channel_id=1, source_target_pairs={{0,6},{1,25},{2,4},{3,27},{4,2},{5,29},{6,0},{7,31},{8,14},{9,17},... | collective-permute-start | bytes 1228808 | tf_op jit(solution)/shard_map/ppermute | solution.py:558
  20.8 9.7 %collective-permute-start.1 = (bf16[2,400,256]{2,1,0:T(8,128)(2,1)S(1)}, bf16[2,400,256]{2,1,0:T(8,128)(2,1)}, u32[]{:S(2)}, u32[]{:S(2)}) collective-permute-start(bf16[2,400,256]{2,1,0:T(8,128)(2,1)S(1)} %pad_maximum_fusion.refs_1_), channel_id=1, source_target_pairs={{0,2},{1,9},{2,0},{3,11},{4,6},{5,13},{6,4},{7,15},{8,10},{9,1},{1... | collective-permute-start | bytes 1228808 | tf_op jit(solution)/shard_map/ppermute | solution.py:558
  23.7 26.9 %copy-start.4 = (bf16[2,400,256]{2,1,0:T(8,128)(2,1)}, bf16[2,400,256]{2,1,0:T(8,128)(2,1)S(1)}, u32[]{:S(2)}) copy-start(bf16[2,400,256]{2,1,0:T(8,128)(2,1)S(1)} %collective-permute-done.4.refs_5_) | copy-start | bytes 1228804
  23.7 11.0 %collective-permute-start.6 = (bf16[2,400,256]{2,1,0:T(8,128)(2,1)S(1)}, bf16[2,400,256]{2,1,0:T(8,128)(2,1)}, u32[]{:S(2)}, u32[]{:S(2)}) collective-permute-start(bf16[2,400,256]{2,1,0:T(8,128)(2,1)S(1)} %collective-permute-done.4.refs_5_), channel_id=1, source_target_pairs={{0,6},{1,25},{2,4},{3,27},{4,2},{5,29},{6,0},{7,31},{8,14},{9,17},... | collective-permute-start | bytes 1228808 | tf_op jit(solution)/shard_map/ppermute | solution.py:558
  27.3 7.5 %collective-permute-start.5 = (bf16[2,400,256]{2,1,0:T(8,128)(2,1)S(1)}, bf16[2,400,256]{2,1,0:T(8,128)(2,1)S(1)}, u32[]{:S(2)}, u32[]{:S(2)}) collective-permute-start(bf16[2,400,256]{2,1,0:T(8,128)(2,1)S(1)} %collective-permute-done.4.refs_5_), channel_id=1, source_target_pairs={{0,2},{1,9},{2,0},{3,11},{4,6},{5,13},{6,4},{7,15},{8,10},{9,1},{1... | collective-permute-start | bytes 1228808 | tf_op jit(solution)/shard_map/ppermute | solution.py:558
  30.5 20.1 %copy-start.5 = (bf16[2,400,256]{2,1,0:T(8,128)(2,1)}, bf16[2,400,256]{2,1,0:T(8,128)(2,1)S(1)}, u32[]{:S(2)}) copy-start(bf16[2,400,256]{2,1,0:T(8,128)(2,1)S(1)} %collective-permute-done.2.refs_3_) | copy-start | bytes 1228804
  30.6 20.1 %collective-permute-start.10 = (bf16[16,272,128]{2,1,0:T(8,128)(2,1)S(1)}, bf16[16,272,128]{2,1,0:T(8,128)(2,1)}, u32[]{:S(2)}, u32[]{:S(2)}) collective-permute-start(bf16[16,272,128]{2,1,0:T(8,128)(2,1)S(1)} %constant_dynamic-update-slice_fusion.refs_9_), channel_id=1, source_target_pairs={{0,1},{1,0},{2,3},{3,2},{4,5},{5,4},{6,7},{7,6},{8,9},{9,8},{10,11... | collective-permute-start | bytes 3342344 | tf_op jit(solution)/shard_map/ppermute | solution.py:558
  34.7 0.8 copy-start.6
  35.5 15.1 %copy-start.3 = (bf16[16,272,128]{2,1,0:T(8,128)(2,1)}, bf16[16,272,128]{2,1,0:T(8,128)(2,1)S(1)}, u32[]{:S(2)}) copy-start(bf16[16,272,128]{2,1,0:T(8,128)(2,1)S(1)} %collective-permute-done.9.refs_10_) | copy-start | bytes 3342340
  35.5 15.1 %collective-permute-start.11 = (bf16[16,272,128]{2,1,0:T(8,128)(2,1)S(1)}, bf16[16,272,128]{2,1,0:T(8,128)(2,1)}, u32[]{:S(2)}, u32[]{:S(2)}) collective-permute-start(bf16[16,272,128]{2,1,0:T(8,128)(2,1)S(1)} %collective-permute-done.9.refs_10_), channel_id=1, source_target_pairs={{0,1},{1,0},{2,3},{3,2},{4,5},{5,4},{6,7},{7,6},{8,9},{9,8},{10,11... | collective-permute-start | bytes 3342344 | tf_op jit(solution)/shard_map/ppermute | solution.py:558
  40.7 8.7 %collective-permute-start.3 = (bf16[2,400,256]{2,1,0:T(8,128)(2,1)}, bf16[2,400,256]{2,1,0:T(8,128)(2,1)}, u32[]{:S(2)}, u32[]{:S(2)}) collective-permute-start(bf16[2,400,256]{2,1,0:T(8,128)(2,1)} %collective-permute-done.1.refs_2_), channel_id=1, source_target_pairs={{0,6},{1,25},{2,4},{3,27},{4,2},{5,29},{6,0},{7,31},{8,14},{9,17},... | collective-permute-start | bytes 1228808 | tf_op jit(solution)/shard_map/ppermute | solution.py:558
  43.5 7.1 %collective-permute-start.7 = (bf16[2,400,256]{2,1,0:T(8,128)(2,1)}, bf16[2,400,256]{2,1,0:T(8,128)(2,1)}, u32[]{:S(2)}, u32[]{:S(2)}) collective-permute-start(bf16[2,400,256]{2,1,0:T(8,128)(2,1)} %collective-permute-done.6.refs_7_), channel_id=1, source_target_pairs={{0,2},{1,9},{2,0},{3,11},{4,6},{5,13},{6,4},{7,15},{8,10},{9,1},{1... | collective-permute-start | bytes 1228808 | tf_op jit(solution)/shard_map/ppermute | solution.py:558
  175.2 59.4 %copy-start = (f32[3,128]{1,0:T(4,128)S(1)}, f32[3,128]{1,0:T(4,128)}, u32[]{:S(2)}) copy-start(f32[3,128]{1,0:T(4,128)} %get-tuple-element.28.norm_ref) | copy-start | bytes 4612
  234.6 57.6 %copy-start.8 = (f32[8,128]{1,0:T(8,128)S(1)}, f32[8,128]{1,0:T(8,128)}, u32[]{:S(2)}) copy-start(f32[8,128]{1,0:T(8,128)} %get-tuple-element.30) | copy-start | bytes 12292
